TPU v7x, 512 devices: a whole 4x8x8 slice. The times are simulated.
512 devices in a mesh: seq: 32 (over x, y), exp: 16 (over z, core).
Axes of the slice: x: 4, y: 8, z: 8, core: 2. Of those that a mesh axis runs over, the one named last changes fastest.
Arguments:
- conv_out: bfloat16 [4096, 8192], P('seq', 'exp'), may hold values from -6 to 6
- gate_z: bfloat16 [4096, 8192], P('seq', 'exp'), may hold values from -6 to 6
- delta_raw: bfloat16 [4096, 8192], P('seq', 'exp'), may hold values from -4 to 4
- decay_rate: float32 [8192, 16], P('exp'), may hold values from 0.0001 to 0.08
- b_proj: float32 [4096, 16], P('seq'), may hold values from -6 to 6
- c_proj: float32 [4096, 16], P('seq'), may hold values from -1.5 to 1.5
- skip_gain: float32 [8192], P('exp'), may hold values from 0.1 to 1.9
- out_weight: bfloat16 [8192, 4096], P('exp', 'seq'), may hold values from -0.0625 to 0.0625
- stream: bfloat16 [4096, 4096], P(('seq', 'exp')), may hold values from -6 to 6
- norm_gain: float32 [4096], replicated, may hold values from 0.1 to 1.9
- expert_ids: int32 [4096, 2], P(('seq', 'exp')), may hold values from 0 to 15, all different within a row; in each aligned block of 8 rows (0 to 7, 8 to 15, ...) at most 2 rows name the same one
- gate_weights: bfloat16 [4096, 2], P(('seq', 'exp')), may hold values from 0.099609375 to 0.8984375
- w_gate: bfloat16 [16, 7168, 4096], P('exp', 'seq'), may hold values from -0.09375 to 0.09375
- w_up: bfloat16 [16, 7168, 4096], P('exp', 'seq'), may hold values from -0.09375 to 0.09375
Outputs:
- expert_hidden: bfloat16 [16, 7168, 1024], P('exp', 'seq')
Inputs may be any that keep to these rules, and one draw needn't show every extreme that they name: `expert_ids`: the two ids of a token differ; among the 8 tokens of one aligned block no expert is named more than 2 times, a bound that some block reaches.
All inputs are finite; a program needn't handle non-finite values.
Results may differ from a plain program's by a relative error of at most 0.0071.
Values may be sent and summed in bfloat16 or wider, within the bound.
No kernel may reach another device: no remote copies, remote signals or barrier semaphores. Data moves between devices by JAX's collectives and lax.ppermute only.
A program may use at most 64 MiB of HBM per device.

v0:
```python
import jax
import jax.numpy as jnp
from jax import lax
from jax.sharding import PartitionSpec as P


def entering_2(part, axis, combine, identity):
    place = lax.axis_index(axis)
    gathered = jax.tree.map(lambda a: lax.all_gather(a, axis), part)
    state = jax.tree.map(lambda a, e: jnp.zeros_like(a) + jnp.asarray(e, a.dtype), part, identity)

    def one(hop, state):
        return combine(
            state, jax.tree.map(lambda a: lax.dynamic_index_in_dim(a, hop, 0, False), gathered)
        )

    return lax.fori_loop(0, place, one, state)


def chain_combine(earlier, later):
    return (earlier[0] * later[0], later[0] * earlier[1] + later[1])


def sweep(start, inputs, steps, b_proj, c_proj, rate_t):
    span = 16
    blocks = inputs.shape[0] // span
    width = inputs.shape[1]
    xs_in = inputs.reshape(blocks, span, width)
    xs_dt = steps.reshape(blocks, span, width)
    xs_b = b_proj.reshape(blocks, span, b_proj.shape[1])
    xs_c = c_proj.reshape(blocks, span, c_proj.shape[1])

    def advance(state, item):
        block_in, block_dt, block_b, block_c = item
        outputs = []
        for place in range(span):
            step_dt = block_dt[place]
            state = (
                jnp.exp(rate_t * step_dt[None, :]) * state
                + block_b[place][:, None] * (step_dt * block_in[place])[None, :]
            )
            outputs.append(jnp.sum(state * block_c[place][:, None], axis=0))
        return (state, jnp.stack(outputs, axis=0))

    final, results = lax.scan(advance, start, (xs_in, xs_dt, xs_b, xs_c))
    return (final, results.reshape(inputs.shape[0], width))


def body(
    conv_out,
    gate_z,
    delta_raw,
    decay_rate,
    b_proj,
    c_proj,
    skip_gain,
    out_weight,
    stream,
    norm_gain,
    expert_ids,
    gate_weights,
    w_gate,
    w_up,
):
    inputs = conv_out.astype(jnp.float32)
    steps = jax.nn.softplus(delta_raw.astype(jnp.float32))
    rate_t = -decay_rate.T
    zeros = jnp.zeros_like(rate_t)
    last_state, _ = sweep(zeros, inputs, steps, b_proj, c_proj, rate_t)
    last_decay = jnp.exp(rate_t * jnp.sum(steps, axis=0)[None, :])
    ones = jnp.ones_like(last_decay)
    entering = entering_2((last_decay, last_state), "seq", chain_combine, (ones, zeros))
    incoming = entering[1]
    _, ssm = sweep(incoming, inputs, steps, b_proj, c_proj, rate_t)
    gated = ((ssm + skip_gain[None, :] * inputs) * jax.nn.silu(gate_z.astype(jnp.float32))).astype(
        jnp.bfloat16
    )
    partial_sum = jnp.dot(
        gated,
        lax.all_gather(out_weight, "seq", axis=1, tiled=True),
        preferred_element_type=jnp.float32,
    )
    tok_rows = stream.shape[0]
    mixed = lax.psum_scatter(
        lax.slice_in_dim(partial_sum, 0, tok_rows * lax.axis_size("exp"), axis=0),
        "exp",
        scatter_dimension=0,
        tiled=True,
    )
    resid = stream.astype(jnp.float32) + mixed
    scale = lax.rsqrt(jnp.mean(resid * resid, axis=1, keepdims=True) + 1e-05)
    normed = (resid * scale * norm_gain[None, :]).astype(jnp.bfloat16)
    n_experts = lax.axis_size("exp")
    most_slots = 4 * tok_rows // n_experts
    onehot = (
        expert_ids[:, :, None] == jnp.arange(n_experts, dtype=jnp.int32)[None, None, :]
    ).astype(jnp.int32)
    flat = onehot.reshape(tok_rows * 2, n_experts)
    before = jnp.cumsum(flat, axis=0) - flat
    position = jnp.sum(before * flat, axis=1).reshape(tok_rows, 2)
    matched = (
        position[:, :, None] == jnp.arange(most_slots, dtype=jnp.int32)[None, None, :]
    ).astype(jnp.float32)
    selector = jnp.einsum("tke,tkm->emt", onehot.astype(jnp.float32), matched).astype(jnp.bfloat16)
    send_rows = jnp.einsum(
        "emt,td->emd", selector, normed, preferred_element_type=jnp.float32
    ).astype(jnp.bfloat16)
    send_gate = jnp.einsum(
        "tke,tkm,tk->em", onehot.astype(jnp.float32), matched, gate_weights.astype(jnp.float32)
    ).astype(jnp.bfloat16)
    got_rows, got_gate = (
        lax.all_to_all(send_rows, "exp", split_axis=0, concat_axis=0, tiled=True),
        lax.all_to_all(send_gate, "exp", split_axis=0, concat_axis=0, tiled=True),
    )
    all_rows, all_gate = (
        lax.all_gather(got_rows[None], "seq", axis=0, tiled=True),
        lax.all_gather(got_gate[None], "seq", axis=0, tiled=True),
    )
    slot_total = all_rows.shape[0] * all_rows.shape[1] * all_rows.shape[2]
    slot_rows = all_rows.reshape(slot_total, all_rows.shape[3])
    slot_gate = all_gate.reshape(slot_total).astype(jnp.float32)
    dims = (((1,), (1,)), ((), ()))
    hidden = lax.dot_general(w_gate[0], slot_rows, dims, preferred_element_type=jnp.float32)
    upward = lax.dot_general(w_up[0], slot_rows, dims, preferred_element_type=jnp.float32)
    result = (jax.nn.silu(hidden) * upward * slot_gate[None, :]).astype(jnp.bfloat16)
    return result[None]


def solution(mesh):
    in_specs = (
        P("seq", "exp"),
        P("seq", "exp"),
        P("seq", "exp"),
        P("exp", None),
        P("seq", None),
        P("seq", None),
        P("exp"),
        P("exp", "seq"),
        P(("seq", "exp"), None),
        P(),
        P(("seq", "exp"), None),
        P(("seq", "exp"), None),
        P("exp", "seq", None),
        P("exp", "seq", None),
    )
    out_specs = P("exp", "seq", None)
    return jax.shard_map(body, mesh=mesh, in_specs=in_specs, out_specs=out_specs, check_vma=False)
```

profile of v0, /device:TPU:6, one launch (start us, length us, event | category | flops | bytes accessed | tf_op | source)
XLA Modules:
  0.0 488.7 jit_solution(1163473454406905714)
XLA Ops:
  6.6 1.2 compare_select_fusion
  7.8 0.9 convert.6
  8.7 0.8 copy.38
  9.5 0.8 negate_bitcast_fusion
  10.3 5.7 %while.37 = (s32[]{:T(128)}, f32[16,512]{1,0:T(8,128)S(1)}, f32[8,16,512]{2,1,0:T(8,128)S(1)}, f32[16,512]{1,0:T(8,128)S(1)}, f32[8,16,16]{2,1,0:T(8,128)S(1)}, ...) while((s32[]{:T(128)}, f32[16,512]{1,0:T(8,128)S(1)}, ...), condition=%wide.region_4.5_spmd.clone, body=%wide.region_3.4_spmd.clone.sunk | while | flops 540690 | bytes 396811 | solution.py:45
  10.6 0.2 multiply_add_fusion.22
  12.8 0.2 multiply_add_fusion.22
  13.6 0.2 multiply_add_fusion.22
  14.3 0.2 multiply_add_fusion.22
  15.0 0.2 multiply_add_fusion.22
  15.7 0.2 multiply_add_fusion.22
  16.0 0.6 copy-done.6
  16.7 0.6 multiply_exponential_fusion
  17.4 0.7 all-gather.9.cloned.1.call-update
  18.3 83.3 %all-gather.13.cloned.1.call-done = f32[512,512]{1,0:T(8,128)} async-done(((f32[16,512]{1,0:T(8,128)}), f32[512,512]{1,0:T(8,128)}) %all-gather.13.cloned.1.call-update) | async-done | bytes 1048592 | tf_op jit(solution)/shard_map/all_gather | solution.py:9
  101.6 82.6 %all-gather.11.cloned.1.call-done = f32[512,512]{1,0:T(8,128)} async-done(((f32[16,512]{1,0:T(8,128)}), f32[512,512]{1,0:T(8,128)}) %all-gather.11.cloned.1.call-update) | async-done | bytes 1048592 | tf_op jit(solution)/shard_map/all_gather | solution.py:9
  184.2 19.6 %while.35 = (s32[]{:T(128)}, f32[16,512]{1,0:T(8,128)S(1)}, s32[]{:T(128)}, f32[32,16,512]{2,1,0:T(8,128)}, f32[32,16,512]{2,1,0:T(8,128)}, /*index=5*/s32[]{:T(128)}, s32[]{:T(128)}, s32[]{:T(128)}) while((s32[]{:T(128)}, f32[16,512]{1,0:T(8,128)S(1)}, s32[]{:T(128)}, f32[32,16,512]{2,1,0:T(8,128)}, f32[32,16,512]{2,1,0:T(8,128)}, ...), condition=%wide.region_6.7_spmd, body=%wide.region_5.6_spmd.sunk | while | flops 16389 | bytes 131195 | solution.py:17
  184.2 0.8 bitcast_add_fusion.3
  185.0 0.8 bitcast_add_fusion.3
  185.9 0.8 bitcast_add_fusion.3
  186.7 0.8 bitcast_add_fusion.3
  187.5 0.8 bitcast_add_fusion.3
  188.3 0.8 bitcast_add_fusion.3
  189.1 0.8 bitcast_add_fusion.3
  189.9 0.8 bitcast_add_fusion.3
  190.8 0.8 bitcast_add_fusion.3
  191.6 0.8 bitcast_add_fusion.3
  192.4 0.8 bitcast_add_fusion.3
  193.2 0.8 bitcast_add_fusion.3
  194.0 0.8 bitcast_add_fusion.3
  194.8 0.8 bitcast_add_fusion.3
  195.7 0.8 bitcast_add_fusion.3
  196.5 0.8 bitcast_add_fusion.3
  197.3 0.8 bitcast_add_fusion.3
  198.1 0.8 bitcast_add_fusion.3
  198.9 0.8 bitcast_add_fusion.3
  199.7 0.8 bitcast_add_fusion.3
  200.6 0.8 bitcast_add_fusion.3
  201.4 0.8 bitcast_add_fusion.3
  202.2 0.8 bitcast_add_fusion.3
  203.0 0.8 bitcast_add_fusion.3
  203.8 11.1 %while.36 = (s32[]{:T(128)}, f32[16,512]{1,0:T(8,128)S(1)}, f32[8,16,512]{2,1,0:T(8,128)S(1)}, f32[8,16,512]{2,1,0:T(8,128)S(1)}, f32[16,512]{1,0:T(8,128)S(1)},...) while((s32[]{:T(128)}, f32[16,512]{1,0:T(8,128)S(1)}, ...), condition=%wide.region_24.25_spmd, body=%wide.region_7.24_spmd.sunk | while | flops 1179665 | bytes 974101 | solution.py:45
  204.5 0.2 multiply_reduce_fusion.22
  205.9 0.2 multiply_reduce_fusion.22
  207.3 0.2 multiply_reduce_fusion.22
  208.7 0.2 multiply_reduce_fusion.22
  210.0 0.2 multiply_reduce_fusion.22
  211.4 0.2 multiply_reduce_fusion.22
  212.8 0.2 multiply_reduce_fusion.22
  214.2 0.2 multiply_reduce_fusion.22
  215.1 60.5 %all-gather.9.cloned.1.call-done = bf16[512,4096]{1,0:T(8,128)(2,1)} async-done(((bf16[512,128]{1,0:T(8,128)(2,1)}), bf16[512,4096]{1,0:T(8,128)(2,1)}) %all-gather.9.cloned.1.call-update) | async-done | bytes 4194320 | tf_op jit(solution)/shard_map/all_gather | solution.py:80
  275.6 4.2 fusion.118
  280.9 61.6 %reduce-scatter.2.cloned.1.call-done = f32[8,4096]{1,0:T(8,128)} async-done(((f32[128,4096]{1,0:T(8,128)}), f32[8,4096]{1,0:T(8,128)}) %reduce-scatter.2.cloned.1.call-update) | async-done | bytes 131088 | tf_op jit(solution)/shard_map/reduce_scatter | solution.py:84
  342.5 1.1 multiply_reduce_fusion.16
  343.6 1.2 convolution_convert_fusion
  344.8 0.3 copy.41
  345.0 14.9 %all_to_all.14 = bf16[16,2,4096]{2,1,0:T(2,128)(2,1)} all-to-all(bf16[16,2,4096]{2,1,0:T(2,128)(2,1)S(1)} %copy.41), channel_id=1, replica_groups=mesh['seq'=32,'exp'=16] {'exp'}, dimensions={0} | all-to-all | bytes 524288 | tf_op jit(solution)/shard_map/all_to_all | solution.py:112
  360.2 10.8 %all_to_all.15 = bf16[16,1,2]{2,1,0:T(2,128)(2,1)S(1)} all-to-all(bf16[16,1,2]{2,1,0:T(2,128)(2,1)S(1)} %copy.42), channel_id=1, replica_groups=mesh['seq'=32,'exp'=16] {'exp'}, dimensions={0} | all-to-all | bytes 128 | tf_op jit(solution)/shard_map/all_to_all | solution.py:113
  371.0 49.1 %all-gather.3 = bf16[512,1,2]{2,1,0:T(2,128)(2,1)S(1)} all-gather(bf16[16,1,2]{2,1,0:T(2,128)(2,1)S(1)} %all_to_all.15), channel_id=5, replica_groups=mesh['seq'=32,'exp'=16] {'seq'}, dimensions={0}, use_global_device_ids=true | all-gather | bytes 2112 | tf_op jit(solution)/shard_map/all_gather | solution.py:117
  420.1 0.8 convert_reduce_fusion
  421.0 38.2 %all-gather.15.cloned.1.call-done = bf16[512,2,4096]{2,1,0:T(2,128)(2,1)} async-done(((bf16[16,2,4096]{2,1,0:T(2,128)(2,1)}), bf16[512,2,4096]{2,1,0:T(2,128)(2,1)}) %all-gather.15.cloned.1.call-update) | async-done | bytes 8388624 | tf_op jit(solution)/shard_map/all_gather | solution.py:116
  459.2 13.1 %reshape.645 = bf16[1024,4096]{1,0:T(8,128)(2,1)} reshape(bf16[512,2,4096]{2,1,0:T(2,128)(2,1)} %all-gather.15.cloned.1.call-done) | data formatting | bytes 16777216 | tf_op jit(solution)/shard_map/reshape | solution.py:120
  472.3 6.1 %fusion.76 = f32[224,1024]{1,0:T(8,128)S(1)} fusion(bf16[1024,4096]{1,0:T(8,128)(2,1)} %reshape.645, bf16[1,224,4096]{2,1,0:T(8,128)(2,1)S(1)} %copy-done), kind=kOutput, calls=%fused_computation.226 | convolution fusion | flops 1879048192 | bytes 11141120 | tf_op jit(solution)/shard_map/dot_general | solution.py:123
  478.6 3.5 fusion.91
  (392 shorter events, 13.1 us)
Async XLA Ops:
  6.5 465.8 %copy-start = (bf16[1,224,4096]{2,1,0:T(8,128)(2,1)S(1)}, bf16[1,224,4096]{2,1,0:T(8,128)(2,1)}, u32[]{:S(2)}) copy-start(bf16[1,224,4096]{2,1,0:T(8,128)(2,1)} %param.32) | copy-start | bytes 5505028
  6.5 10.1 %copy-start.5 = (f32[512,16]{0,1:T(8,128)S(1)}, f32[512,16]{0,1:T(8,128)}, u32[]{:S(2)}) copy-start(f32[512,16]{0,1:T(8,128)} %param.23) | copy-start | bytes 98308
  6.5 11.7 %copy-start.8 = (f32[128,16]{0,1:T(8,128)S(1)}, f32[128,16]{0,1:T(8,128)}, u32[]{:S(2)}) copy-start(f32[128,16]{0,1:T(8,128)} %param.25) | copy-start | bytes 24580
  6.5 95.1 %all-gather.13.cloned.1.call-start = ((), (), s32[]{:S(2)}) async-start(), calls=%async_computation.6 | async-start | bytes 1081344 | tf_op jit(solution)/shard_map/all_gather | solution.py:9
  16.0 0.6 copy-start.6
  16.6 167.6 %all-gather.11.cloned.1.call-start = ((), (), s32[]{:S(2)}) async-start(), calls=%async_computation.5 | async-start | bytes 1081344 | tf_op jit(solution)/shard_map/all_gather | solution.py:9
  17.4 197.5 %copy-start.2 = (bf16[128,512]{1,0:T(8,128)(2,1)S(1)}, bf16[128,512]{1,0:T(8,128)(2,1)}, u32[]{:S(2)}) copy-start(bf16[128,512]{1,0:T(8,128)(2,1)} %param.20) | copy-start | bytes 393220
  17.4 197.5 %copy-start.4 = (bf16[128,512]{1,0:T(8,128)(2,1)S(1)}, bf16[128,512]{1,0:T(8,128)(2,1)}, u32[]{:S(2)}) copy-start(bf16[128,512]{1,0:T(8,128)(2,1)} %param.21) | copy-start | bytes 393220
  17.4 197.5 %copy-start.10 = (f32[512]{0:T(512)S(1)}, f32[512]{0:T(512)}, u32[]{:S(2)}) copy-start(f32[512]{0:T(512)} %param.26) | copy-start | bytes 6148
  17.4 258.2 %all-gather.9.cloned.1.call-start = ((), (), s32[]{:S(2)}) async-start(), calls=%async_computation.3 | async-start | bytes 4325376 | tf_op jit(solution)/shard_map/all_gather | solution.py:80
  18.1 324.4 %reduce-scatter.2.cloned.1.call-start = ((), (), s32[]{:S(2)}) async-start(), calls=%async_computation.4 | async-start | bytes 2228224 | tf_op jit(solution)/shard_map/reduce_scatter | solution.py:84
  215.0 64.9 %copy-start.9 = (s32[8,2]{0,1:T(2,128)S(1)}, s32[8,2]{0,1:T(2,128)}, u32[]{:S(2)}) copy-start(s32[8,2]{0,1:T(2,128)} %param.30) | copy-start | bytes 196
  215.0 127.5 %copy-start.3 = (bf16[8,4096]{1,0:T(8,128)(2,1)S(1)}, bf16[8,4096]{1,0:T(8,128)(2,1)}, u32[]{:S(2)}) copy-start(bf16[8,4096]{1,0:T(8,128)(2,1)} %param.28) | copy-start | bytes 196612
  215.1 128.5 %copy-start.7 = (f32[4096]{0:T(1024)S(1)}, f32[4096]{0:T(1024)}, u32[]{:S(2)}) copy-start(f32[4096]{0:T(1024)} %param.29) | copy-start | bytes 49156
  215.1 144.9 %copy-start.12 = (bf16[8,2]{0,1:T(2,128)(2,1)S(1)}, bf16[8,2]{0,1:T(2,128)(2,1)}, u32[]{:S(2)}) copy-start(bf16[8,2]{0,1:T(2,128)(2,1)} %param.31) | copy-start | bytes 100
  279.8 179.4 %all-gather.15.cloned.1.call-start = ((), (), s32[]{:S(2)}) async-start(), calls=%async_computation.7 | async-start | bytes 8650752 | tf_op jit(solution)/shard_map/all_gather | solution.py:116
  472.3 6.2 %copy-start.1 = (bf16[1024,4096]{1,0:T(8,128)(2,1)S(1)}, bf16[1024,4096]{1,0:T(8,128)(2,1)}, u32[]{:S(2)}) copy-start(bf16[1024,4096]{1,0:T(8,128)(2,1)} %reshape.645) | copy-start | bytes 25165828
  472.3 6.3 %copy-start.11 = (bf16[1,224,4096]{2,1,0:T(8,128)(2,1)S(1)}, bf16[1,224,4096]{2,1,0:T(8,128)(2,1)}, u32[]{:S(2)}) copy-start(bf16[1,224,4096]{2,1,0:T(8,128)(2,1)} %param.33) | copy-start | bytes 5505028
Sparse Core Ops, SparseCore 0:
  16.7 84.8 all-gather.12
  104.8 79.3 all-gather.10
  187.3 88.2 all-gather.8
  280.0 62.5 reduce-scatter.1
  360.1 99.1 all-gather.14
where the time goes:
time: 494 us; the launch traced here: 489 us
  waiting for transfers between devices  327 us (66%)
  blocking collectives  74.7 us (15%)
  other arithmetic  33.4 us (7%)
  local copies, waits for them, and re-layouts  21.4 us (4%)
  matrix products  15.4 us (3%)
  between operations  13.4 us (3%)
    all_gather x2, waiting for transfers between devices, entering_2(): gathered = jax.tree.map(lambda a: lax.all_gather(a, axis), part)  166 us
    reduce_scatter x1, waiting for transfers between devices, body(): lax.psum_scatter(lax.slice_in_dim(partial_sum, 0, tok_rows * lax.axis_siz...  61.6 us
    all_gather x1, waiting for transfers between devices, body(): lax.all_gather(out_weight, 'seq', axis=1, tiled=True)  60.5 us
    all_gather x1, blocking collectives, body(): lax.all_gather(got_gate[None], 'seq', axis=0, tiled=True)  49.1 us
    all_gather x1, waiting for transfers between devices, body(): lax.all_gather(got_rows[None], 'seq', axis=0, tiled=True)  38.2 us
    add x24, other arithmetic, chain_combine(): return (earlier[0] * later[0], later[0] * earlier[1] + later[1])  19 us
    all_to_all x1, blocking collectives, body(): lax.all_to_all(send_rows, 'exp', split_axis=0, concat_axis=0, tiled=True)  14.9 us
    reshape x1, local copies, waits for them, and re-layouts, body(): slot_rows = all_rows.reshape(slot_total, all_rows.shape[3])  13.1 us
  transfers between devices with their start and end apart: 5, of which 5 were waited for; matrix products, arithmetic and copies ran while one was open for 7% of the time, Pallas kernels for 0%

commit v1 on v0

v1 whole, which is shorter than its diff:
```python
import jax
import jax.numpy as jnp
import numpy as np
from jax import lax
from jax.experimental import pallas as pl
from jax.experimental.pallas import tpu as pltpu
from jax.sharding import Mesh
from jax.sharding import PartitionSpec as P

NX, NY = 4, 8
SEQ = ("x", "y")
EXP = ("z", "c")
LOG2E = 1.4426950408889634
SPAN = 16
PAD = 128
TURN = 256
MIB = 1024 * 1024


def softplus(v):
    return jnp.maximum(v, 0.0) + jnp.log1p(jnp.exp(-jnp.abs(v)))


def last_kernel(x_ref, d_ref, rate_ref, b_ref, part_ref):
    rate = rate_ref[...]
    states, width = rate.shape

    def some(i, carry):
        state, total = carry
        rows = pl.ds(pl.multiple_of(i * SPAN, SPAN), SPAN)
        dt = softplus(d_ref[rows, :].astype(jnp.float32))
        u = dt * x_ref[rows, :].astype(jnp.float32)
        b = b_ref[i]
        for t in range(SPAN):
            step = dt[t : t + 1, :]
            state = jnp.exp2(rate * step) * state + b[:, t : t + 1] * u[t : t + 1, :]
            total = total + step
        return state, total

    start = (jnp.zeros((states, width), jnp.float32), jnp.zeros((1, width), jnp.float32))
    state, total = lax.fori_loop(0, x_ref.shape[0] // SPAN, some, start)
    part_ref[:states, :] = state
    part_ref[states:, :] = jnp.broadcast_to(total, (8, width))


def row_kernel(y_ref, parts_ref, rate_ref, near_ref, row_ref):
    rate = rate_ref[...]
    states, width = rate.shape
    y = y_ref[0]
    state, total = jnp.zeros((states, width), jnp.float32), jnp.zeros((8, width), jnp.float32)
    near, near_total = state, total
    for k in range(parts_ref.shape[0]):
        sums = parts_ref[k, states:, :]
        decay = jnp.exp2(rate * sums[0:1])
        state = decay * state + parts_ref[k, :states, :]
        total = total + sums
        near = jnp.where(k + 1 == y, state, near)
        near_total = jnp.where(k + 1 == y, total, near_total)
    near_ref[:states, :] = near
    near_ref[states:, :] = near_total
    row_ref[:states, :] = state
    row_ref[states:, :] = total


def gated_kernel(place_ref, x_ref, d_ref, z_ref, rate_ref, b_ref, c_ref, skip_ref, near_ref, rows_ref, out_ref):
    rate = rate_ref[...]
    states, width = rate.shape
    place = lax.broadcasted_iota(jnp.int32, (SPAN, width), 0)
    start = jnp.zeros((states, width), jnp.float32)
    for k in range(rows_ref.shape[0] - 1):
        later = jnp.exp2(rate * rows_ref[k, states : states + 1, :]) * start + rows_ref[k, :states, :]
        start = jnp.where(k < place_ref[0], later, start)
    start = jnp.exp2(rate * near_ref[states : states + 1, :]) * start + near_ref[:states, :]

    def some(i, state):
        rows = pl.ds(pl.multiple_of(i * SPAN, SPAN), SPAN)
        dt = softplus(d_ref[rows, :].astype(jnp.float32))
        x = x_ref[rows, :].astype(jnp.float32)
        u = dt * x
        b, c = b_ref[i], c_ref[i]
        ssm = jnp.zeros((SPAN, width), jnp.float32)
        for t in range(SPAN):
            step = dt[t : t + 1, :]
            state = jnp.exp2(rate * step) * state + b[:, t : t + 1] * u[t : t + 1, :]
            row = jnp.sum(state * c[:, t : t + 1], axis=0, keepdims=True)
            ssm = jnp.where(place == t, row, ssm)
        z = z_ref[rows, :].astype(jnp.float32)
        gate = z / (1.0 + jnp.exp(-z))
        out_ref[rows, :] = ((ssm + skip_ref[...] * x) * gate).astype(jnp.bfloat16)
        return state

    lax.fori_loop(0, x_ref.shape[0] // SPAN, some, start)


def project_kernel(core_ref, g_ref, w_ref, own_ref, other_ref):
    n_x, zs, tok, _ = own_ref.shape
    n_y, _, wide = w_ref.shape
    g = g_ref[...].reshape(n_x * zs * 2 * tok, g_ref.shape[2])
    first = core_ref[0] == 0
    for y in range(0, n_y, 2):
        w = jnp.concatenate([w_ref[y], w_ref[y + 1]], axis=1)
        p = jnp.dot(g, w, preferred_element_type=jnp.float32)
        p = p.reshape(n_x, zs, 2, tok, 2 * wide)
        a, b = p[:, :, 0], p[:, :, 1]
        at = y * wide
        own_ref[:, :, :, at : at + 2 * wide] = jnp.where(first, a, b)
        other_ref[:, :, :, at : at + 2 * wide] = jnp.where(first, b, a).astype(jnp.bfloat16)


def slots_kernel(got_ref, stream_ref, gain_ref, sel_ref, gate_ref, out_ref):
    zs = got_ref.shape[0] // NX
    blocks = []
    for x in range(NX):
        block = got_ref[x * zs].astype(jnp.float32)
        for z in range(1, zs):
            block = block + got_ref[x * zs + z].astype(jnp.float32)
        blocks.append(block)
    resid = stream_ref[...].astype(jnp.float32) + jnp.concatenate(blocks, axis=1)
    mean = jnp.mean(resid * resid, axis=1, keepdims=True)
    normed = (resid * lax.rsqrt(mean + 1e-05) * gain_ref[...]).astype(jnp.bfloat16).astype(jnp.float32)
    sel = sel_ref[...]
    rows = sel[:, 0:1] * normed[0:1, :]
    for t in range(1, normed.shape[0]):
        rows = rows + sel[:, t : t + 1] * normed[t : t + 1, :]
    width = normed.shape[1]
    out_ref[:, :width] = rows.astype(jnp.bfloat16)
    out_ref[:, width:] = gate_ref[...]


def turn_kernel(wg_ref, wu_ref, out_ref):
    units = wg_ref.shape[0]
    block = out_ref.shape[1] // 2

    def some(i, _):
        at = pl.ds(pl.multiple_of(i * TURN, TURN), TURN)
        for k, ref in enumerate((wg_ref, wu_ref)):
            w = ref[:, at].astype(jnp.float32)
            if block > units:
                w = jnp.concatenate([w, jnp.zeros((block - units, TURN), jnp.float32)], axis=0)
            out_ref[at, k * block : (k + 1) * block] = w.T.astype(jnp.bfloat16)
        return 0

    lax.fori_loop(0, wg_ref.shape[1] // TURN, some, 0)


def experts_kernel(place_ref, a0, a1, a20, a21, a3, b0, b1, b2, b3, b40, b41, b5, b6, b7, w_ref, out_ref, b):
    my_x, my_y = place_ref[0], place_ref[1]
    units = out_ref.shape[0]
    block = w_ref.shape[1] // 2
    slots = b0.shape[1]
    wide = a0.shape[1]
    rest = w_ref.shape[0] - wide
    group = NY * slots
    for dx in range(NX):
        x = lax.rem(my_x - dx + NX, NX)
        for dy, ref in enumerate((b0, b1, b2, b3, None, b5, b6, b7)):
            y = lax.rem(my_y - dy + NY, NY)
            at = pl.ds(pl.multiple_of(y * slots, slots), slots)
            if ref is None:

                @pl.when(x < NX // 2)
                def _():
                    b[at, :] = b40[x]

                @pl.when(x >= NX // 2)
                def _():
                    b[at, :] = b41[x - NX // 2]

            else:
                b[at, :] = ref[x]
        if dx == 2:
            first = jnp.concatenate([a20[...], a21[...]], axis=0)
        else:
            first = (a0, a1, None, a3)[dx][...]
        p = jnp.dot(first, w_ref[:wide, :], preferred_element_type=jnp.float32)
        p = p + jnp.dot(b[:, :rest], w_ref[wide:, :], preferred_element_type=jnp.float32)
        gate = b[:, rest:].astype(jnp.float32)[:, 0:1]
        hidden, upward = p[:, :block], p[:, block:]
        value = hidden / (1.0 + jnp.exp(-hidden)) * upward * gate
        to = pl.ds(pl.multiple_of(x * group, group), group)
        out_ref[:, to] = value.T[:units].astype(jnp.bfloat16)


def spread(a, axis, size):
    copies = jnp.broadcast_to(a[None], (size,) + a.shape)
    return lax.all_to_all(copies, axis, split_axis=0, concat_axis=0, tiled=True)


def ring(a, axis, size, hop):
    return lax.ppermute(a, axis, [(i, (i + hop) % size) for i in range(size)])


def everywhere(rows):
    slots, width = rows.shape
    wide = (width - PAD) // 2
    a, b = rows[:, :wide], rows[:, wide:]
    a0 = lax.all_gather(a, "y").reshape(NY * slots, wide)
    b0 = spread(b, "x", NX)
    s1, t1 = ring(b0, "y", NY, 1), ring(b0, "y", NY, -1)
    a0, s1, t1 = lax.optimization_barrier((a0, s1, t1))
    ap, am = ring(a0, "x", NX, 1), ring(a0, "x", NX, -1)
    s2, t2 = ring(s1, "y", NY, 1), ring(t1, "y", NY, -1)
    s3, t3 = ring(s2, "y", NY, 1), ring(t2, "y", NY, -1)
    s4, t4 = ring(s3[: NX // 2], "y", NY, 1), ring(t3[NX // 2 :], "y", NY, -1)
    half = NY * slots // 2
    ao0, ao1 = ring(ap[:half], "x", NX, 1), ring(am[half:], "x", NX, -1)
    return [a0, ap, ao0, ao1, am], [b0, s1, s2, s3, s4, t4, t3, t2, t1]


VMEM = pl.BlockSpec(memory_space=pltpu.VMEM)
SMEM = pl.BlockSpec(memory_space=pltpu.SMEM)


def body(
    conv_out,
    gate_z,
    delta_raw,
    decay_rate,
    b_proj,
    c_proj,
    skip_gain,
    out_weight,
    stream,
    norm_gain,
    expert_ids,
    gate_weights,
    w_gate,
    w_up,
):
    tokens, width = conv_out.shape
    states = decay_rate.shape[1]
    tok_rows, features = stream.shape
    n_z = lax.axis_size("z")
    n_experts = n_z * 2
    small = pltpu.CompilerParams(vmem_limit_bytes=12 * MIB)

    columns = lax.all_gather(out_weight, "y")
    place = jnp.stack([lax.axis_index("x"), lax.axis_index("y")]).astype(jnp.int32)

    rate = decay_rate.T * -LOG2E
    spans = tokens // SPAN
    b3 = b_proj.reshape(spans, SPAN, states).transpose(0, 2, 1)
    c3 = c_proj.reshape(spans, SPAN, states).transpose(0, 2, 1)
    work = tokens * width * states
    part = pl.pallas_call(
        last_kernel,
        out_shape=jax.ShapeDtypeStruct((states + 8, width), jnp.float32),
        in_specs=[VMEM] * 4,
        out_specs=VMEM,
        compiler_params=small,
        cost_estimate=pl.CostEstimate(flops=4 * work, bytes_accessed=1 << 18, transcendentals=work),
    )(conv_out, delta_raw, rate, b3)
    part_shape = jax.ShapeDtypeStruct(part.shape, jnp.float32)
    near, row = pl.pallas_call(
        row_kernel,
        out_shape=[part_shape, part_shape],
        in_specs=[SMEM, VMEM, VMEM],
        out_specs=[VMEM, VMEM],
        compiler_params=small,
        cost_estimate=pl.CostEstimate(flops=1 << 18, bytes_accessed=1 << 19, transcendentals=1 << 16),
    )(place[1:], spread(part, "y", NY), rate)
    rows_before = spread(row, "x", NX)
    gated = pl.pallas_call(
        gated_kernel,
        out_shape=jax.ShapeDtypeStruct((tokens, width), jnp.bfloat16),
        in_specs=[SMEM] + [VMEM] * 9,
        out_specs=VMEM,
        compiler_params=small,
        cost_estimate=pl.CostEstimate(flops=6 * work, bytes_accessed=1 << 19, transcendentals=work),
    )(place[:1], conv_out, delta_raw, gate_z, rate, b3, c3, skip_gain[None, :], near, rows_before)

    core = lax.axis_index("c").astype(jnp.int32).reshape(1)
    shape = (NX, n_z, tok_rows, features // NX)
    own, other = pl.pallas_call(
        project_kernel,
        out_shape=[jax.ShapeDtypeStruct(shape, jnp.float32), jax.ShapeDtypeStruct(shape, jnp.bfloat16)],
        in_specs=[SMEM, VMEM, VMEM],
        out_specs=[VMEM, VMEM],
        compiler_params=small,
        cost_estimate=pl.CostEstimate(
            flops=2 * tokens * width * features, bytes_accessed=width * features * 2, transcendentals=0
        ),
    )(core, spread(gated, "x", NX), columns)
    theirs = ring(other, "c", 2, 1)
    both = (own + theirs.astype(jnp.float32)).astype(jnp.bfloat16)
    both = both.reshape(NX * n_z, tok_rows, features // NX)
    both, wg, wu = lax.optimization_barrier((both, w_gate[0], w_up[0]))
    hidden_units = w_gate.shape[1]
    block = -(-hidden_units // TURN) * TURN
    turned = pl.pallas_call(
        turn_kernel,
        out_shape=jax.ShapeDtypeStruct((features, 2 * block), jnp.bfloat16),
        in_specs=[VMEM] * 2,
        out_specs=VMEM,
        compiler_params=small,
        cost_estimate=pl.CostEstimate(flops=1 << 24, bytes_accessed=16 * MIB, transcendentals=0),
    )(wg, wu)
    got = lax.all_to_all(both, ("x", "z"), split_axis=0, concat_axis=0, tiled=True)

    most_slots = 4 * tok_rows // n_experts
    onehot = (
        expert_ids[:, :, None] == jnp.arange(n_experts, dtype=jnp.int32)[None, None, :]
    ).astype(jnp.int32)
    flat = onehot.reshape(tok_rows * 2, n_experts)
    before = jnp.cumsum(flat, axis=0) - flat
    position = jnp.sum(before * flat, axis=1).reshape(tok_rows, 2)
    matched = (
        position[:, :, None] == jnp.arange(most_slots, dtype=jnp.int32)[None, None, :]
    ).astype(jnp.float32)
    pairs = onehot.astype(jnp.float32)[:, :, :, None] * matched[:, :, None, :]
    slots = n_experts * most_slots
    sel = jnp.sum(pairs, axis=1).reshape(tok_rows, slots).T
    gate = jnp.sum(pairs * gate_weights.astype(jnp.float32)[:, :, None, None], axis=(0, 1)).reshape(slots, 1)
    gate = jnp.pad(gate, ((0, 0), (0, PAD - 1))).astype(jnp.bfloat16)

    rows = pl.pallas_call(
        slots_kernel,
        out_shape=jax.ShapeDtypeStruct((slots, features + PAD), jnp.bfloat16),
        in_specs=[VMEM] * 5,
        out_specs=VMEM,
        compiler_params=small,
        cost_estimate=pl.CostEstimate(flops=1 << 21, bytes_accessed=1 << 20, transcendentals=0),
    )(got, stream, norm_gain[None, :], sel, gate)
    rows = rows.reshape(n_experts, most_slots, features + PAD)
    rows = lax.all_to_all(rows, EXP, split_axis=0, concat_axis=0, tiled=True)
    a_parts, b_parts = everywhere(rows.reshape(slots, features + PAD))

    total = NX * NY * slots
    result = pl.pallas_call(
        experts_kernel,
        out_shape=jax.ShapeDtypeStruct((hidden_units, total), jnp.bfloat16),
        in_specs=[SMEM] + [VMEM] * 15,
        out_specs=VMEM,
        scratch_shapes=[pltpu.VMEM((NY * slots, features // 2 + PAD), jnp.bfloat16)],
        compiler_params=pltpu.CompilerParams(vmem_limit_bytes=28 * MIB),
        cost_estimate=pl.CostEstimate(
            flops=4 * hidden_units * total * features,
            bytes_accessed=total * features * 2,
            transcendentals=hidden_units * total,
        ),
    )(place, *a_parts, *b_parts, turned)
    return result[None]


def solution(mesh):
    n_z = mesh.shape["exp"] // 2
    fine = Mesh(np.asarray(mesh.devices).reshape(NX, NY, n_z, 2), ("x", "y", "z", "c"))
    in_specs = (
        P(SEQ, EXP),
        P(SEQ, EXP),
        P(SEQ, EXP),
        P(EXP, None),
        P(SEQ, None),
        P(SEQ, None),
        P(EXP),
        P(EXP, SEQ),
        P(SEQ + EXP, None),
        P(),
        P(SEQ + EXP, None),
        P(SEQ + EXP, None),
        P(EXP, SEQ, None),
        P(EXP, SEQ, None),
    )
    out_specs = P(EXP, SEQ, None)
    return jax.shard_map(body, mesh=fine, in_specs=in_specs, out_specs=out_specs, check_vma=False)
```

time: 494 us -> 218 us (0.44)
  waiting for transfers between devices: 327 us -> 71.9 us
  starting transfers between devices: 0.17 us -> 76.5 us
  blocking collectives: 74.7 us -> 29 us
  other arithmetic: 33.4 us -> 2.25 us
  matrix products: 15.4 us -> 0 us
  Pallas kernels: 0 us -> 14.1 us
  local copies, waits for them, and re-layouts: 21.4 us -> 9.43 us
    all_gather x4 -> x2, waiting for transfers between devices: 265 us -> 0.01 us  [the longest x1 0.01 us: body(): columns = lax.all_gather(out_weight, 'y')]
    reduce_scatter x1 -> x0, waiting for transfers between devices: 61.6 us -> none  [body(): lax.psum_scatter(lax.slice_in_dim(partial_sum, 0, tok_rows * lax.axis_siz...]
    all_gather x1 -> x0, blocking collectives: 49.1 us -> none  [body(): lax.all_gather(got_gate[None], 'seq', axis=0, tiled=True)]
    ppermute x0 -> x13, starting transfers between devices: none -> 43.3 us  [ring(): return lax.ppermute(a, axis, [(i, (i + hop) % size) for i in range(size)])]
    all_to_all x0 -> x4, waiting for transfers between devices: none -> 39.5 us  [the longest x3 25.2 us: spread(): return lax.all_to_all(copies, axis, split_axis=0, concat_axis=0, tiled=True)]
    all_to_all x0 -> x4, starting transfers between devices: none -> 33.2 us  [the longest x3 17.4 us: spread(): return lax.all_to_all(copies, axis, split_axis=0, concat_axis=0, tiled=True)]
    ppermute x0 -> x13, waiting for transfers between devices: none -> 31.6 us  [ring(): return lax.ppermute(a, axis, [(i, (i + hop) % size) for i in range(size)])]
    add x32 -> x0, other arithmetic: 20.7 us -> none  [the longest x24 19 us: chain_combine(): return (earlier[0] * later[0], later[0] * earlier[1] + later[1])]
  transfers between devices with their start and end apart: 5 -> 19, of which waited for: 5 -> 10; matrix products, arithmetic and copies ran while one was open for 7% -> 2% of each run, Pallas kernels for 0% -> 3%
where the time goes in v1:
time: 218 us; the launch traced here: 217 us
  starting transfers between devices  76.5 us (35%)
  waiting for transfers between devices  71.9 us (33%)
  blocking collectives  29 us (13%)
  Pallas kernels  14.1 us (6%)
  between operations  13.8 us (6%)
  local copies, waits for them, and re-layouts  9.43 us (4%)
  other arithmetic  2.25 us (1%)
    ppermute x13, starting transfers between devices, ring(): return lax.ppermute(a, axis, [(i, (i + hop) % size) for i in range(size)])  43.3 us
    ppermute x13, waiting for transfers between devices, ring(): return lax.ppermute(a, axis, [(i, (i + hop) % size) for i in range(size)])  31.6 us
    all_to_all x3, waiting for transfers between devices, spread(): return lax.all_to_all(copies, axis, split_axis=0, concat_axis=0, tiled=True)  25.2 us
    all_to_all x3, starting transfers between devices, spread(): return lax.all_to_all(copies, axis, split_axis=0, concat_axis=0, tiled=True)  17.4 us
    all_to_all x1, starting transfers between devices, body(): lax.all_to_all(both, ('x', 'z'), split_axis=0, concat_axis=0, tiled=True)  15.8 us
    all_to_all x1, blocking collectives, body(): rows = lax.all_to_all(rows, EXP, split_axis=0, concat_axis=0, tiled=True)  15.4 us
    all_to_all x1, waiting for transfers between devices, body(): lax.all_to_all(both, ('x', 'z'), split_axis=0, concat_axis=0, tiled=True)  14.3 us
    all_to_all x1, blocking collectives, spread(): return lax.all_to_all(copies, axis, split_axis=0, concat_axis=0, tiled=True)  13.6 us
  transfers between devices with their start and end apart: 19, of which 10 were waited for; matrix products, arithmetic and copies ran while one was open for 2% of the time, Pallas kernels for 3%

profile of v1, /device:TPU:6, one launch (start us, length us, event | category | flops | bytes accessed | tf_op | source)
XLA Modules:
  0.0 216.9 jit_solution(13597050976136572971)
XLA Ops:
  6.5 0.7 all-gather.5.cloned.1.call-update
  7.3 0.8 reshape.47
  8.1 0.8 multiply_bitcast_fusion.rate_ref
  8.8 0.9 copy-done.6
  9.7 0.9 copy-done.8
  10.7 1.3 shard_map.136
  12.0 0.8 broadcast_in_dim.15
  12.8 7.1 %all-to-all-start = ((f32[8,24,512]{2,1,0:T(8,128)}), f32[8,24,512]{2,1,0:T(8,128)S(1)}, u32[]{:S(2)}, u32[]{:S(2)}) async-start(f32[8,24,512]{2,1,0:T(8,128)} %broadcast_in_dim.15), calls=%async_computation | async-start | bytes 786432 | tf_op jit(solution)/shard_map/all_to_all | solution.py:186
  19.9 15.0 %all-to-all-done.parts_ref = f32[8,24,512]{2,1,0:T(8,128)S(1)} async-done(((f32[8,24,512]{2,1,0:T(8,128)}), f32[8,24,512]{2,1,0:T(8,128)S(1)}, u32[]{:S(2)}, u32[]{:S(2)}) %all-to-all-start) | async-done | bytes 393248 | tf_op jit(solution)/shard_map/all_to_all | solution.py:186
  34.9 0.1 shard_map.137
  34.9 0.7 broadcast_in_dim.16
  35.6 4.8 %all-to-all-start.1 = ((f32[4,24,512]{2,1,0:T(8,128)}), f32[4,24,512]{2,1,0:T(8,128)S(1)}, u32[]{:S(2)}, u32[]{:S(2)}) async-start(f32[4,24,512]{2,1,0:T(8,128)} %broadcast_in_dim.16), calls=%async_computation.1 | async-start | bytes 393216 | tf_op jit(solution)/shard_map/all_to_all | solution.py:186
  40.4 0.1 reshape.48
  40.5 4.2 %all-to-all-done.1.rows_ref = f32[4,24,512]{2,1,0:T(8,128)S(1)} async-done(((f32[4,24,512]{2,1,0:T(8,128)}), f32[4,24,512]{2,1,0:T(8,128)S(1)}, u32[]{:S(2)}, u32[]{:S(2)}) %all-to-all-start.1) | async-done | bytes 196640 | tf_op jit(solution)/shard_map/all_to_all | solution.py:186
  44.7 2.2 %shard_map.138 = bf16[128,512]{1,0:T(8,128)(2,1)S(1)} custom-call(s32[1]{0:T(128)} %bitcast.place_ref, bf16[128,512]{1,0:T(8,128)(2,1)S(1)} %copy-done.7, bf16[128,512]{1,0:T(8,128)(2,1)S(1)} %copy-done.9, bf16[128,512]{1,0:T(8,128)(2,1)S(1)} %copy-done.10, f32[16,512]{1,0:T(8,128)S(1)} %multiply_bitcast_fusion.rate_ref, f32[8,16,16]{2,1,0:T(8,128)S(1)} %bitcast.29, ...), custom_call_target="tpu_custom_call" | custom-call | flops 6291456 | bytes 524288 | tf_op jit(solution)/shard_map/pallas_call | solution.py:263
  46.9 0.8 broadcast_in_dim.17
  47.7 5.5 %all-to-all-start.2 = ((bf16[4,128,512]{2,1,0:T(8,128)(2,1)}), bf16[4,128,512]{2,1,0:T(8,128)(2,1)S(1)}, u32[]{:S(2)}, u32[]{:S(2)}) async-start(bf16[4,128,512]{2,1,0:T(8,128)(2,1)} %broadcast_in_dim.17), calls=%async_computation.2 | async-start | bytes 1048576 | tf_op jit(solution)/shard_map/all_to_all | solution.py:186
  53.3 6.0 %all-to-all-done.2.g_ref = bf16[4,128,512]{2,1,0:T(8,128)(2,1)S(1)} async-done(((bf16[4,128,512]{2,1,0:T(8,128)(2,1)}), bf16[4,128,512]{2,1,0:T(8,128)(2,1)S(1)}, u32[]{:S(2)}, u32[]{:S(2)}) %all-to-all-start.2) | async-done | bytes 524320 | tf_op jit(solution)/shard_map/all_to_all | solution.py:186
  59.3 1.2 copy-done.5
  60.5 0.7 shard_map.139
  61.3 2.1 collective-permute-start
  63.3 1.9 collective-permute-done
  65.2 0.9 add_convert_fusion
  66.1 15.8 %all-to-all-start.3 = ((bf16[32,8,1024]{2,1,0:T(8,128)(2,1)}), bf16[32,8,1024]{2,1,0:T(8,128)(2,1)S(1)}, u32[]{:S(2)}, u32[]{:S(2)}) async-start(bf16[32,8,1024]{2,1,0:T(8,128)(2,1)} %bitcast.8), calls=%async_computation.3 | async-start | bytes 1048576 | tf_op jit(solution)/shard_map/all_to_all | solution.py:298
  81.9 0.0 all-gather.7.cloned.1.call-start
  82.0 0.1 copy.27
  82.1 0.1 eq.48
  82.2 0.1 fusion.1
  82.3 0.2 select_reduce_fusion
  82.5 0.1 eq.52
  82.6 0.1 copy.28
  82.7 0.1 convert_convert_fusion
  82.7 0.1 fusion
  82.8 0.1 copy.30
  82.9 0.1 reshape.58
  83.0 0.1 copy.29
  83.1 14.3 %all-to-all-done.3.got_ref = bf16[32,8,1024]{2,1,0:T(8,128)(2,1)S(1)} async-done(((bf16[32,8,1024]{2,1,0:T(8,128)(2,1)}), bf16[32,8,1024]{2,1,0:T(8,128)(2,1)S(1)}, u32[]{:S(2)}, u32[]{:S(2)}) %all-to-all-start.3) | async-done | bytes 524320 | tf_op jit(solution)/shard_map/all_to_all | solution.py:298
  97.4 0.7 shard_map.140
  98.2 0.1 reshape.52
  98.3 15.4 %all_to_all.30 = bf16[16,2,4224]{2,1,0:T(2,128)(2,1)S(1)} all-to-all(bf16[16,2,4224]{2,1,0:T(2,128)(2,1)S(1)} %reshape.52), channel_id=1, replica_groups=mesh['x'=4,'y'=8,'z'=8,'c'=2] {'z','c'}, dimensions={0} | all-to-all | bytes 540672 | tf_op jit(solution)/shard_map/all_to_all | solution.py:325
  113.7 0.1 reshape.53
  113.8 0.7 slice.24
  114.5 13.6 %all_to_all.31.b0 = bf16[4,32,2176]{2,1,0:T(8,128)(2,1)S(1)} all-to-all(bf16[4,32,2176]{2,1,0:T(8,128)(2,1)S(1)} %broadcast_in_dim.19), channel_id=1, replica_groups=mesh['x'=4,'y'=8,'z'=8,'c'=2] {'x'}, dimensions={0} | all-to-all | bytes 1114112 | tf_op jit(solution)/shard_map/all_to_all | solution.py:186
  128.2 2.0 collective-permute-start.2
  130.2 3.9 %collective-permute-start.1 = (bf16[4,32,2176]{2,1,0:T(8,128)(2,1)S(1)}, bf16[4,32,2176]{2,1,0:T(8,128)(2,1)S(1)}, u32[]{:S(2)}, u32[]{:S(2)}) collective-permute-start(bf16[4,32,2176]{2,1,0:T(8,128)(2,1)S(1)} %all_to_all.31.b0), channel_id=1, source_target_pairs={{0,16},{16,32},{32,48},{48,64},{64,80},{80,96},{96,112},{112,0},{1... | collective-permute-start | bytes 1671176 | tf_op jit(solution)/shard_map/ppermute | solution.py:190
  134.2 15.9 %collective-permute-done.2.b7 = bf16[4,32,2176]{2,1,0:T(8,128)(2,1)S(1)} collective-permute-done((bf16[4,32,2176]{2,1,0:T(8,128)(2,1)S(1)}, bf16[4,32,2176]{2,1,0:T(8,128)(2,1)S(1)}, u32[]{:S(2)}, u32[]{:S(2)}) %collective-permute-start.2) | collective-permute-done | bytes 557088 | tf_op jit(solution)/shard_map/ppermute | solution.py:190
  150.0 2.2 %collective-permute-done.1.b1 = bf16[4,32,2176]{2,1,0:T(8,128)(2,1)S(1)} collective-permute-done((bf16[4,32,2176]{2,1,0:T(8,128)(2,1)S(1)}, bf16[4,32,2176]{2,1,0:T(8,128)(2,1)S(1)}, u32[]{:S(2)}, u32[]{:S(2)}) %collective-permute-start.1) | collective-permute-done | bytes 557088 | tf_op jit(solution)/shard_map/ppermute | solution.py:190
  152.3 2.6 %collective-permute-start.5 = (bf16[256,2048]{1,0:T(8,128)(2,1)}, bf16[256,2048]{1,0:T(8,128)(2,1)S(1)}, u32[]{:S(2)}, u32[]{:S(2)}) collective-permute-start(bf16[256,2048]{1,0:T(8,128)(2,1)} %all-gather.7.cloned.1.call-done.a0), channel_id=1, source_target_pairs={{0,384},{128,0},{256,128},{384,256},{1,385},{129,1},{257,129},{385... | collective-permute-start | bytes 3145736 | tf_op jit(solution)/shard_map/ppermute | solution.py:190
  154.8 4.5 %collective-permute-start.3 = (bf16[256,2048]{1,0:T(8,128)(2,1)}, bf16[256,2048]{1,0:T(8,128)(2,1)S(1)}, u32[]{:S(2)}, u32[]{:S(2)}) collective-permute-start(bf16[256,2048]{1,0:T(8,128)(2,1)} %all-gather.7.cloned.1.call-done.a0), channel_id=1, source_target_pairs={{0,128},{128,256},{256,384},{384,0},{1,129},{129,257},{257,385},{3... | collective-permute-start | bytes 3145736 | tf_op jit(solution)/shard_map/ppermute | solution.py:190
  159.3 2.6 %collective-permute-start.7 = (bf16[4,32,2176]{2,1,0:T(8,128)(2,1)S(1)}, bf16[4,32,2176]{2,1,0:T(8,128)(2,1)S(1)}, u32[]{:S(2)}, u32[]{:S(2)}) collective-permute-start(bf16[4,32,2176]{2,1,0:T(8,128)(2,1)S(1)} %collective-permute-done.1.b1), channel_id=1, source_target_pairs={{0,16},{16,32},{32,48},{48,64},{64,80},{80,96},{96,112},{112,0},{1... | collective-permute-start | bytes 1671176 | tf_op jit(solution)/shard_map/ppermute | solution.py:190
  161.9 4.5 %collective-permute-start.10 = (bf16[4,32,2176]{2,1,0:T(8,128)(2,1)S(1)}, bf16[4,32,2176]{2,1,0:T(8,128)(2,1)S(1)}, u32[]{:S(2)}, u32[]{:S(2)}) collective-permute-start(bf16[4,32,2176]{2,1,0:T(8,128)(2,1)S(1)} %collective-permute-done.2.b7), channel_id=1, source_target_pairs={{0,112},{16,0},{32,16},{48,32},{64,48},{80,64},{96,80},{112,96},{1... | collective-permute-start | bytes 1671176 | tf_op jit(solution)/shard_map/ppermute | solution.py:190
  166.4 9.8 %collective-permute-done.7.b2 = bf16[4,32,2176]{2,1,0:T(8,128)(2,1)S(1)} collective-permute-done((bf16[4,32,2176]{2,1,0:T(8,128)(2,1)S(1)}, bf16[4,32,2176]{2,1,0:T(8,128)(2,1)S(1)}, u32[]{:S(2)}, u32[]{:S(2)}) %collective-permute-start.7) | collective-permute-done | bytes 557088 | tf_op jit(solution)/shard_map/ppermute | solution.py:190
  176.2 1.9 collective-permute-start.8
  178.1 5.1 %collective-permute-start.11 = (bf16[4,32,2176]{2,1,0:T(8,128)(2,1)S(1)}, bf16[4,32,2176]{2,1,0:T(8,128)(2,1)S(1)}, u32[]{:S(2)}, u32[]{:S(2)}) collective-permute-start(bf16[4,32,2176]{2,1,0:T(8,128)(2,1)S(1)} %collective-permute-done.10.b6), channel_id=1, source_target_pairs={{0,112},{16,0},{32,16},{48,32},{64,48},{80,64},{96,80},{112,96},{1... | collective-permute-start | bytes 1671176 | tf_op jit(solution)/shard_map/ppermute | solution.py:190
  183.3 1.9 collective-permute-start.6
  185.3 5.1 %collective-permute-start.4 = (bf16[128,2048]{1,0:T(8,128)(2,1)S(1)}, bf16[128,2048]{1,0:T(8,128)(2,1)S(1)}, u32[]{:S(2)}, u32[]{:S(2)}) collective-permute-start(bf16[128,2048]{1,0:T(8,128)(2,1)S(1)} %slice.26), channel_id=1, source_target_pairs={{0,128},{128,256},{256,384},{384,0},{1,129},{129,257},{257,385},{3... | collective-permute-start | bytes 1572872 | tf_op jit(solution)/shard_map/ppermute | solution.py:190
  190.4 1.6 collective-permute-done.8.b3
  192.1 1.9 collective-permute-start.9
  194.1 5.1 %collective-permute-start.12 = (bf16[2,32,2176]{2,1,0:T(8,128)(2,1)S(1)}, bf16[2,32,2176]{2,1,0:T(8,128)(2,1)S(1)}, u32[]{:S(2)}, u32[]{:S(2)}) collective-permute-start(bf16[2,32,2176]{2,1,0:T(8,128)(2,1)S(1)} %slice.29), channel_id=1, source_target_pairs={{0,112},{16,0},{32,16},{48,32},{64,48},{80,64},{96,80},{112,96},{1... | collective-permute-start | bytes 835592 | tf_op jit(solution)/shard_map/ppermute | solution.py:190
  199.2 0.1 pad_add_fusion.place_ref
  199.3 1.5 copy-done.1
  200.8 2.2 %shard_map.141.w_ref = bf16[4096,512]{1,0:T(8,128)(2,1)S(1)} custom-call(bf16[224,4096]{1,0:T(8,128)(2,1)S(1)} %bitcast.25, bf16[224,4096]{1,0:T(8,128)(2,1)S(1)} %bitcast.26), custom_call_target="tpu_custom_call" | custom-call | flops 16777216 | bytes 16777216 | tf_op jit(solution)/shard_map/pallas_call | solution.py:290
  203.0 0.2 collective-permute-done.12.b41
  203.3 6.8 %shard_map.142 = bf16[224,1024]{1,0:T(8,128)(2,1)} custom-call(s32[2]{0:T(128)S(1)} %pad_add_fusion.place_ref, bf16[256,2048]{1,0:T(8,128)(2,1)S(1)} %copy-done.4, bf16[256,2048]{1,0:T(8,128)(2,1)S(1)} %collective-permute-done.3.a1, bf16[128,2048]{1,0:T(8,128)(2,1)S(1)} %collective-permute-done.4.a20, bf16[128,2048]{1,0:T(8,128)(2,1)S(1)} %collective-permute-done.6.a21, ...), custom_call_target="tpu_custom_call" | custom-call | flops 3758096384 | bytes 8388608 | tf_op jit(solution)/shard_map/pallas_call | solution.py:329
  (49 shorter events, 0.4 us)
Async XLA Ops:
  6.5 52.7 %all-gather.5.cloned.1.call-start = ((), (), s32[]{:S(2)}) async-start(), calls=%async_computation.6 | async-start | bytes 1179648 | tf_op jit(solution)/shard_map/all_gather | solution.py:237
  8.8 0.9 copy-start.6
  9.7 0.9 copy-start.8
  10.6 29.8 %copy-start.12 = (f32[128,16]{0,1:T(8,128)S(1)}, f32[128,16]{0,1:T(8,128)}, u32[]{:S(2)}) copy-start(f32[128,16]{0,1:T(8,128)} %param.19) | copy-start | bytes 24580
  10.6 34.1 %copy-start.7 = (bf16[128,512]{1,0:T(8,128)(2,1)S(1)}, bf16[128,512]{1,0:T(8,128)(2,1)}, u32[]{:S(2)}) copy-start(bf16[128,512]{1,0:T(8,128)(2,1)} %x_ref.3) | copy-start | bytes 393220
  10.6 34.1 %copy-start.9 = (bf16[128,512]{1,0:T(8,128)(2,1)S(1)}, bf16[128,512]{1,0:T(8,128)(2,1)}, u32[]{:S(2)}) copy-start(bf16[128,512]{1,0:T(8,128)(2,1)} %d_ref.3) | copy-start | bytes 393220
  10.6 34.1 %copy-start.10 = (bf16[128,512]{1,0:T(8,128)(2,1)S(1)}, bf16[128,512]{1,0:T(8,128)(2,1)}, u32[]{:S(2)}) copy-start(bf16[128,512]{1,0:T(8,128)(2,1)} %z_ref.1) | copy-start | bytes 393220
  10.6 34.1 %copy-start.11 = (f32[512]{0:T(512)S(1)}, f32[512]{0:T(512)}, u32[]{:S(2)}) copy-start(f32[512]{0:T(512)} %param.20) | copy-start | bytes 6148
  12.8 22.1 %all-to-all-start = ((f32[8,24,512]{2,1,0:T(8,128)}), f32[8,24,512]{2,1,0:T(8,128)S(1)}, u32[]{:S(2)}, u32[]{:S(2)}) async-start(f32[8,24,512]{2,1,0:T(8,128)} %broadcast_in_dim.15), calls=%async_computation | async-start | bytes 786432 | tf_op jit(solution)/shard_map/all_to_all | solution.py:186
  35.6 9.1 %all-to-all-start.1 = ((f32[4,24,512]{2,1,0:T(8,128)}), f32[4,24,512]{2,1,0:T(8,128)S(1)}, u32[]{:S(2)}, u32[]{:S(2)}) async-start(f32[4,24,512]{2,1,0:T(8,128)} %broadcast_in_dim.16), calls=%async_computation.1 | async-start | bytes 393216 | tf_op jit(solution)/shard_map/all_to_all | solution.py:186
  47.7 11.5 %all-to-all-start.2 = ((bf16[4,128,512]{2,1,0:T(8,128)(2,1)}), bf16[4,128,512]{2,1,0:T(8,128)(2,1)S(1)}, u32[]{:S(2)}, u32[]{:S(2)}) async-start(bf16[4,128,512]{2,1,0:T(8,128)(2,1)} %broadcast_in_dim.17), calls=%async_computation.2 | async-start | bytes 1048576 | tf_op jit(solution)/shard_map/all_to_all | solution.py:186
  59.3 1.2 copy-start.5
  61.2 20.8 %copy-start.14 = (bf16[8,2]{0,1:T(2,128)(2,1)S(1)}, bf16[8,2]{0,1:T(2,128)(2,1)}, u32[]{:S(2)}) copy-start(bf16[8,2]{0,1:T(2,128)(2,1)} %param.25) | copy-start | bytes 100
  61.2 20.8 %copy-start.13 = (s32[8,2]{0,1:T(2,128)S(1)}, s32[8,2]{0,1:T(2,128)}, u32[]{:S(2)}) copy-start(s32[8,2]{0,1:T(2,128)} %param.24) | copy-start | bytes 196
  61.2 36.2 %copy-start.2 = (bf16[8,4096]{1,0:T(8,128)(2,1)S(1)}, bf16[8,4096]{1,0:T(8,128)(2,1)}, u32[]{:S(2)}) copy-start(bf16[8,4096]{1,0:T(8,128)(2,1)} %stream_ref.1) | copy-start | bytes 196612
  61.3 36.2 %copy-start.3 = (f32[4096]{0:T(1024)S(1)}, f32[4096]{0:T(1024)}, u32[]{:S(2)}) copy-start(f32[4096]{0:T(1024)} %param.23) | copy-start | bytes 49156
  61.3 3.9 %collective-permute-start = (bf16[4,8,8,1024]{3,2,1,0:T(8,128)(2,1)S(1)}, bf16[4,8,8,1024]{3,2,1,0:T(8,128)(2,1)S(1)}, u32[]{:S(2)}, u32[]{:S(2)}) collective-permute-start(bf16[4,8,8,1024]{3,2,1,0:T(8,128)(2,1)S(1)} %get-tuple-element.18), channel_id=1, source_target_pairs={{0,1},{1,0},{2,3},{3,2},{4,5},{5,4},{6,7},{7,6},{8,9},{9,8},{10,11... | collective-permute-start | bytes 1572872 | tf_op jit(solution)/shard_map/ppermute | solution.py:190
  66.1 31.3 %all-to-all-start.3 = ((bf16[32,8,1024]{2,1,0:T(8,128)(2,1)}), bf16[32,8,1024]{2,1,0:T(8,128)(2,1)S(1)}, u32[]{:S(2)}, u32[]{:S(2)}) async-start(bf16[32,8,1024]{2,1,0:T(8,128)(2,1)} %bitcast.8), calls=%async_computation.3 | async-start | bytes 1048576 | tf_op jit(solution)/shard_map/all_to_all | solution.py:298
  81.9 70.3 %all-gather.7.cloned.1.call-start = ((), (), s32[]{:S(2)}) async-start(), calls=%async_computation.7 | async-start | bytes 1179648 | tf_op jit(solution)/shard_map/all_gather | solution.py:197
  128.2 71.1 %copy-start = (bf16[1,224,4096]{2,1,0:T(8,128)(2,1)S(1)}, bf16[1,224,4096]{2,1,0:T(8,128)(2,1)}, u32[]{:S(2)}) copy-start(bf16[1,224,4096]{2,1,0:T(8,128)(2,1)} %param.26) | copy-start | bytes 5505028
  128.2 21.8 %collective-permute-start.2 = (bf16[4,32,2176]{2,1,0:T(8,128)(2,1)S(1)}, bf16[4,32,2176]{2,1,0:T(8,128)(2,1)S(1)}, u32[]{:S(2)}, u32[]{:S(2)}) collective-permute-start(bf16[4,32,2176]{2,1,0:T(8,128)(2,1)S(1)} %all_to_all.31.b0), channel_id=1, source_target_pairs={{0,112},{16,0},{32,16},{48,32},{64,48},{80,64},{96,80},{112,96},{1... | collective-permute-start | bytes 1671176 | tf_op jit(solution)/shard_map/ppermute | solution.py:190
  130.2 22.0 %collective-permute-start.1 = (bf16[4,32,2176]{2,1,0:T(8,128)(2,1)S(1)}, bf16[4,32,2176]{2,1,0:T(8,128)(2,1)S(1)}, u32[]{:S(2)}, u32[]{:S(2)}) collective-permute-start(bf16[4,32,2176]{2,1,0:T(8,128)(2,1)S(1)} %all_to_all.31.b0), channel_id=1, source_target_pairs={{0,16},{16,32},{32,48},{48,64},{64,80},{80,96},{96,112},{112,0},{1... | collective-permute-start | bytes 1671176 | tf_op jit(solution)/shard_map/ppermute | solution.py:190
  152.3 31.0 %collective-permute-start.5 = (bf16[256,2048]{1,0:T(8,128)(2,1)}, bf16[256,2048]{1,0:T(8,128)(2,1)S(1)}, u32[]{:S(2)}, u32[]{:S(2)}) collective-permute-start(bf16[256,2048]{1,0:T(8,128)(2,1)} %all-gather.7.cloned.1.call-done.a0), channel_id=1, source_target_pairs={{0,384},{128,0},{256,128},{384,256},{1,385},{129,1},{257,129},{385... | collective-permute-start | bytes 3145736 | tf_op jit(solution)/shard_map/ppermute | solution.py:190
  154.8 30.4 %collective-permute-start.3 = (bf16[256,2048]{1,0:T(8,128)(2,1)}, bf16[256,2048]{1,0:T(8,128)(2,1)S(1)}, u32[]{:S(2)}, u32[]{:S(2)}) collective-permute-start(bf16[256,2048]{1,0:T(8,128)(2,1)} %all-gather.7.cloned.1.call-done.a0), channel_id=1, source_target_pairs={{0,128},{128,256},{256,384},{384,0},{1,129},{129,257},{257,385},{3... | collective-permute-start | bytes 3145736 | tf_op jit(solution)/shard_map/ppermute | solution.py:190
  159.3 16.8 %collective-permute-start.7 = (bf16[4,32,2176]{2,1,0:T(8,128)(2,1)S(1)}, bf16[4,32,2176]{2,1,0:T(8,128)(2,1)S(1)}, u32[]{:S(2)}, u32[]{:S(2)}) collective-permute-start(bf16[4,32,2176]{2,1,0:T(8,128)(2,1)S(1)} %collective-permute-done.1.b1), channel_id=1, source_target_pairs={{0,16},{16,32},{32,48},{48,64},{64,80},{80,96},{96,112},{112,0},{1... | collective-permute-start | bytes 1671176 | tf_op jit(solution)/shard_map/ppermute | solution.py:190
  161.9 16.2 %collective-permute-start.10 = (bf16[4,32,2176]{2,1,0:T(8,128)(2,1)S(1)}, bf16[4,32,2176]{2,1,0:T(8,128)(2,1)S(1)}, u32[]{:S(2)}, u32[]{:S(2)}) collective-permute-start(bf16[4,32,2176]{2,1,0:T(8,128)(2,1)S(1)} %collective-permute-done.2.b7), channel_id=1, source_target_pairs={{0,112},{16,0},{32,16},{48,32},{64,48},{80,64},{96,80},{112,96},{1... | collective-permute-start | bytes 1671176 | tf_op jit(solution)/shard_map/ppermute | solution.py:190
  176.2 15.9 %collective-permute-start.8 = (bf16[4,32,2176]{2,1,0:T(8,128)(2,1)S(1)}, bf16[4,32,2176]{2,1,0:T(8,128)(2,1)S(1)}, u32[]{:S(2)}, u32[]{:S(2)}) collective-permute-start(bf16[4,32,2176]{2,1,0:T(8,128)(2,1)S(1)} %collective-permute-done.7.b2), channel_id=1, source_target_pairs={{0,16},{16,32},{32,48},{48,64},{64,80},{80,96},{96,112},{112,0},{1... | collective-permute-start | bytes 1671176 | tf_op jit(solution)/shard_map/ppermute | solution.py:190
  178.1 15.9 %collective-permute-start.11 = (bf16[4,32,2176]{2,1,0:T(8,128)(2,1)S(1)}, bf16[4,32,2176]{2,1,0:T(8,128)(2,1)S(1)}, u32[]{:S(2)}, u32[]{:S(2)}) collective-permute-start(bf16[4,32,2176]{2,1,0:T(8,128)(2,1)S(1)} %collective-permute-done.10.b6), channel_id=1, source_target_pairs={{0,112},{16,0},{32,16},{48,32},{64,48},{80,64},{96,80},{112,96},{1... | collective-permute-start | bytes 1671176 | tf_op jit(solution)/shard_map/ppermute | solution.py:190
  183.3 20.0 %collective-permute-start.6 = (bf16[128,2048]{1,0:T(8,128)(2,1)S(1)}, bf16[128,2048]{1,0:T(8,128)(2,1)S(1)}, u32[]{:S(2)}, u32[]{:S(2)}) collective-permute-start(bf16[128,2048]{1,0:T(8,128)(2,1)S(1)} %slice.27), channel_id=1, source_target_pairs={{0,384},{128,0},{256,128},{384,256},{1,385},{129,1},{257,129},{385... | collective-permute-start | bytes 1572872 | tf_op jit(solution)/shard_map/ppermute | solution.py:190
  185.3 18.0 %collective-permute-start.4 = (bf16[128,2048]{1,0:T(8,128)(2,1)S(1)}, bf16[128,2048]{1,0:T(8,128)(2,1)S(1)}, u32[]{:S(2)}, u32[]{:S(2)}) collective-permute-start(bf16[128,2048]{1,0:T(8,128)(2,1)S(1)} %slice.26), channel_id=1, source_target_pairs={{0,128},{128,256},{256,384},{384,0},{1,129},{129,257},{257,385},{3... | collective-permute-start | bytes 1572872 | tf_op jit(solution)/shard_map/ppermute | solution.py:190
  192.1 10.9 %collective-permute-start.9 = (bf16[2,32,2176]{2,1,0:T(8,128)(2,1)S(1)}, bf16[2,32,2176]{2,1,0:T(8,128)(2,1)S(1)}, u32[]{:S(2)}, u32[]{:S(2)}) collective-permute-start(bf16[2,32,2176]{2,1,0:T(8,128)(2,1)S(1)} %slice.28), channel_id=1, source_target_pairs={{0,16},{16,32},{32,48},{48,64},{64,80},{80,96},{96,112},{112,0},{1... | collective-permute-start | bytes 835592 | tf_op jit(solution)/shard_map/ppermute | solution.py:190
  194.1 9.2 %collective-permute-start.12 = (bf16[2,32,2176]{2,1,0:T(8,128)(2,1)S(1)}, bf16[2,32,2176]{2,1,0:T(8,128)(2,1)S(1)}, u32[]{:S(2)}, u32[]{:S(2)}) collective-permute-start(bf16[2,32,2176]{2,1,0:T(8,128)(2,1)S(1)} %slice.29), channel_id=1, source_target_pairs={{0,112},{16,0},{32,16},{48,32},{64,48},{80,64},{96,80},{112,96},{1... | collective-permute-start | bytes 835592 | tf_op jit(solution)/shard_map/ppermute | solution.py:190
  199.3 1.5 copy-start.1
  200.8 2.5 %copy-start.4 = (bf16[256,2048]{1,0:T(8,128)(2,1)S(1)}, bf16[256,2048]{1,0:T(8,128)(2,1)}, u32[]{:S(2)}) copy-start(bf16[256,2048]{1,0:T(8,128)(2,1)} %all-gather.7.cloned.1.call-done.a0) | copy-start | bytes 3145732
Sparse Core Ops, SparseCore 0:
  9.4 46.8 all-gather.4
  114.6 35.4 all-gather.6

commit v2 on v1

--- a/solution.py
+++ b/solution.py
@@ -39,8 +39,9 @@
 
     start = (jnp.zeros((states, width), jnp.float32), jnp.zeros((1, width), jnp.float32))
     state, total = lax.fori_loop(0, x_ref.shape[0] // SPAN, some, start)
-    part_ref[:states, :] = state
-    part_ref[states:, :] = jnp.broadcast_to(total, (8, width))
+    for k in range(part_ref.shape[0]):
+        part_ref[k, :states, :] = state
+        part_ref[k, states:, :] = jnp.broadcast_to(total, (8, width))
 
 
 def row_kernel(y_ref, parts_ref, rate_ref, near_ref, row_ref):
@@ -58,8 +59,9 @@
         near_total = jnp.where(k + 1 == y, total, near_total)
     near_ref[:states, :] = near
     near_ref[states:, :] = near_total
-    row_ref[:states, :] = state
-    row_ref[states:, :] = total
+    for k in range(row_ref.shape[0]):
+        row_ref[k, :states, :] = state
+        row_ref[k, states:, :] = total
 
 
 def gated_kernel(place_ref, x_ref, d_ref, z_ref, rate_ref, b_ref, c_ref, skip_ref, near_ref, rows_ref, out_ref):
@@ -86,7 +88,9 @@
             ssm = jnp.where(place == t, row, ssm)
         z = z_ref[rows, :].astype(jnp.float32)
         gate = z / (1.0 + jnp.exp(-z))
-        out_ref[rows, :] = ((ssm + skip_ref[...] * x) * gate).astype(jnp.bfloat16)
+        gated = ((ssm + skip_ref[...] * x) * gate).astype(jnp.bfloat16)
+        for k in range(out_ref.shape[0]):
+            out_ref[k, rows, :] = gated
         return state
 
     lax.fori_loop(0, x_ref.shape[0] // SPAN, some, start)
@@ -107,7 +111,7 @@
         other_ref[:, :, :, at : at + 2 * wide] = jnp.where(first, b, a).astype(jnp.bfloat16)
 
 
-def slots_kernel(got_ref, stream_ref, gain_ref, sel_ref, gate_ref, out_ref):
+def slots_kernel(got_ref, stream_ref, gain_ref, sel_ref, gate_ref, a_ref, b_ref):
     zs = got_ref.shape[0] // NX
     blocks = []
     for x in range(NX):
@@ -122,9 +126,10 @@
     rows = sel[:, 0:1] * normed[0:1, :]
     for t in range(1, normed.shape[0]):
         rows = rows + sel[:, t : t + 1] * normed[t : t + 1, :]
-    width = normed.shape[1]
-    out_ref[:, :width] = rows.astype(jnp.bfloat16)
-    out_ref[:, width:] = gate_ref[...]
+    wide = b_ref.shape[1]
+    a_ref[:, :wide] = rows[:, :wide].astype(jnp.bfloat16)
+    a_ref[:, wide:] = gate_ref[...]
+    b_ref[...] = rows[:, wide:].astype(jnp.bfloat16)
 
 
 def turn_kernel(wg_ref, wu_ref, out_ref):
@@ -148,8 +153,7 @@
     units = out_ref.shape[0]
     block = w_ref.shape[1] // 2
     slots = b0.shape[1]
-    wide = a0.shape[1]
-    rest = w_ref.shape[0] - wide
+    wide = a0.shape[1] - PAD
     group = NY * slots
     for dx in range(NX):
         x = lax.rem(my_x - dx + NX, NX)
@@ -172,17 +176,16 @@
             first = jnp.concatenate([a20[...], a21[...]], axis=0)
         else:
             first = (a0, a1, None, a3)[dx][...]
-        p = jnp.dot(first, w_ref[:wide, :], preferred_element_type=jnp.float32)
-        p = p + jnp.dot(b[:, :rest], w_ref[wide:, :], preferred_element_type=jnp.float32)
-        gate = b[:, rest:].astype(jnp.float32)[:, 0:1]
+        p = jnp.dot(first[:, :wide], w_ref[:wide, :], preferred_element_type=jnp.float32)
+        p = p + jnp.dot(b[...], w_ref[wide:, :], preferred_element_type=jnp.float32)
+        gate = first[:, wide:].astype(jnp.float32)[:, 0:1]
         hidden, upward = p[:, :block], p[:, block:]
         value = hidden / (1.0 + jnp.exp(-hidden)) * upward * gate
         to = pl.ds(pl.multiple_of(x * group, group), group)
         out_ref[:, to] = value.T[:units].astype(jnp.bfloat16)
 
 
-def spread(a, axis, size):
-    copies = jnp.broadcast_to(a[None], (size,) + a.shape)
+def spread(copies, axis):
     return lax.all_to_all(copies, axis, split_axis=0, concat_axis=0, tiled=True)
 
 
@@ -190,21 +193,27 @@
     return lax.ppermute(a, axis, [(i, (i + hop) % size) for i in range(size)])
 
 
-def everywhere(rows):
+def dispatched(rows, n_experts):
     slots, width = rows.shape
-    wide = (width - PAD) // 2
-    a, b = rows[:, :wide], rows[:, wide:]
+    rows = rows.reshape(n_experts, slots // n_experts, width)
+    return lax.all_to_all(rows, EXP, split_axis=0, concat_axis=0, tiled=True).reshape(slots, width)
+
+
+def everywhere(a, b, n_experts, turned):
+    slots, wide = a.shape
+    a = dispatched(a, n_experts)
     a0 = lax.all_gather(a, "y").reshape(NY * slots, wide)
-    b0 = spread(b, "x", NX)
+    b = dispatched(b, n_experts)
+    b0 = spread(jnp.broadcast_to(b[None], (NX,) + b.shape), "x")
     s1, t1 = ring(b0, "y", NY, 1), ring(b0, "y", NY, -1)
-    a0, s1, t1 = lax.optimization_barrier((a0, s1, t1))
+    a0, turned = lax.optimization_barrier((a0, turned))
     ap, am = ring(a0, "x", NX, 1), ring(a0, "x", NX, -1)
     s2, t2 = ring(s1, "y", NY, 1), ring(t1, "y", NY, -1)
     s3, t3 = ring(s2, "y", NY, 1), ring(t2, "y", NY, -1)
     s4, t4 = ring(s3[: NX // 2], "y", NY, 1), ring(t3[NX // 2 :], "y", NY, -1)
     half = NY * slots // 2
     ao0, ao1 = ring(ap[:half], "x", NX, 1), ring(am[half:], "x", NX, -1)
-    return [a0, ap, ao0, ao1, am], [b0, s1, s2, s3, s4, t4, t3, t2, t1]
+    return [a0, ap, ao0, ao1, am], [b0, s1, s2, s3, s4, t4, t3, t2, t1], turned
 
 
 VMEM = pl.BlockSpec(memory_space=pltpu.VMEM)
@@ -244,25 +253,26 @@
     work = tokens * width * states
     part = pl.pallas_call(
         last_kernel,
-        out_shape=jax.ShapeDtypeStruct((states + 8, width), jnp.float32),
+        out_shape=jax.ShapeDtypeStruct((NY, states + 8, width), jnp.float32),
         in_specs=[VMEM] * 4,
         out_specs=VMEM,
         compiler_params=small,
         cost_estimate=pl.CostEstimate(flops=4 * work, bytes_accessed=1 << 18, transcendentals=work),
     )(conv_out, delta_raw, rate, b3)
-    part_shape = jax.ShapeDtypeStruct(part.shape, jnp.float32)
+    part_shape = jax.ShapeDtypeStruct(part.shape[1:], jnp.float32)
+    row_shape = jax.ShapeDtypeStruct((NX,) + part.shape[1:], jnp.float32)
     near, row = pl.pallas_call(
         row_kernel,
-        out_shape=[part_shape, part_shape],
+        out_shape=[part_shape, row_shape],
         in_specs=[SMEM, VMEM, VMEM],
         out_specs=[VMEM, VMEM],
         compiler_params=small,
         cost_estimate=pl.CostEstimate(flops=1 << 18, bytes_accessed=1 << 19, transcendentals=1 << 16),
-    )(place[1:], spread(part, "y", NY), rate)
-    rows_before = spread(row, "x", NX)
+    )(place[1:], spread(part, "y"), rate)
+    rows_before = spread(row, "x")
     gated = pl.pallas_call(
         gated_kernel,
-        out_shape=jax.ShapeDtypeStruct((tokens, width), jnp.bfloat16),
+        out_shape=jax.ShapeDtypeStruct((NX, tokens, width), jnp.bfloat16),
         in_specs=[SMEM] + [VMEM] * 9,
         out_specs=VMEM,
         compiler_params=small,
@@ -280,7 +290,7 @@
         cost_estimate=pl.CostEstimate(
             flops=2 * tokens * width * features, bytes_accessed=width * features * 2, transcendentals=0
         ),
-    )(core, spread(gated, "x", NX), columns)
+    )(core, spread(gated, "x"), columns)
     theirs = ring(other, "c", 2, 1)
     both = (own + theirs.astype(jnp.float32)).astype(jnp.bfloat16)
     both = both.reshape(NX * n_z, tok_rows, features // NX)
@@ -313,17 +323,19 @@
     gate = jnp.sum(pairs * gate_weights.astype(jnp.float32)[:, :, None, None], axis=(0, 1)).reshape(slots, 1)
     gate = jnp.pad(gate, ((0, 0), (0, PAD - 1))).astype(jnp.bfloat16)
 
-    rows = pl.pallas_call(
+    wide = features // 2
+    a_rows, b_rows = pl.pallas_call(
         slots_kernel,
-        out_shape=jax.ShapeDtypeStruct((slots, features + PAD), jnp.bfloat16),
+        out_shape=[
+            jax.ShapeDtypeStruct((slots, wide + PAD), jnp.bfloat16),
+            jax.ShapeDtypeStruct((slots, features - wide), jnp.bfloat16),
+        ],
         in_specs=[VMEM] * 5,
-        out_specs=VMEM,
+        out_specs=[VMEM, VMEM],
         compiler_params=small,
         cost_estimate=pl.CostEstimate(flops=1 << 21, bytes_accessed=1 << 20, transcendentals=0),
     )(got, stream, norm_gain[None, :], sel, gate)
-    rows = rows.reshape(n_experts, most_slots, features + PAD)
-    rows = lax.all_to_all(rows, EXP, split_axis=0, concat_axis=0, tiled=True)
-    a_parts, b_parts = everywhere(rows.reshape(slots, features + PAD))
+    a_parts, b_parts, turned = everywhere(a_rows, b_rows, n_experts, turned)
 
     total = NX * NY * slots
     result = pl.pallas_call(
@@ -331,7 +343,7 @@
         out_shape=jax.ShapeDtypeStruct((hidden_units, total), jnp.bfloat16),
         in_specs=[SMEM] + [VMEM] * 15,
         out_specs=VMEM,
-        scratch_shapes=[pltpu.VMEM((NY * slots, features // 2 + PAD), jnp.bfloat16)],
+        scratch_shapes=[pltpu.VMEM((NY * slots, features - wide), jnp.bfloat16)],
         compiler_params=pltpu.CompilerParams(vmem_limit_bytes=28 * MIB),
         cost_estimate=pl.CostEstimate(
             flops=4 * hidden_units * total * features,

time: 218 us -> 217 us (level)
  waiting for transfers between devices: 71.9 us -> 59.3 us
  blocking collectives: 29 us -> 37.9 us
  starting transfers between devices: 76.5 us -> 74.3 us
  Pallas kernels: 14.1 us -> 16.3 us
    ppermute x13, waiting for transfers between devices: 31.6 us -> 19 us  [ring(): return lax.ppermute(a, axis, [(i, (i + hop) % size) for i in range(size)])]
    all_to_all x1 -> x2, blocking collectives: 15.4 us -> 24.7 us  [dispatched(): lax.all_to_all(rows, EXP, split_axis=0, concat_axis=0, tiled=True)]
    unnamed x31 -> x35, local copies, waits for them, and re-layouts: 4.67 us -> 8.8 us
    ppermute x13, starting transfers between devices: 43.3 us -> 40.8 us  [ring(): return lax.ppermute(a, axis, [(i, (i + hop) % size) for i in range(size)])]
    broadcast_in_dim x4 -> x2, local copies, waits for them, and re-layouts: 2.37 us -> 0.09 us  [everywhere(): b0 = spread(jnp.broadcast_to(b[None], (NX,) + b.shape), 'x')]
    pallas_call x4, Pallas kernels: 4.28 us -> 6.51 us  [the longest x1 2.97 us: body(): pl.pallas_call(gated_kernel, out_shape=jax.ShapeDtypeStruct((NX, tokens,...]
  transfers between devices with their start and end apart: 19 -> 19, of which waited for: 10 -> 9; matrix products, arithmetic and copies ran while one was open for 2% -> 1% of each run, Pallas kernels for 3% -> 4%
where the time goes in v2:
time: 217 us; the launch traced here: 215 us
  starting transfers between devices  74.3 us (34%)
  waiting for transfers between devices  59.3 us (27%)
  blocking collectives  37.9 us (17%)
  Pallas kernels  16.3 us (8%)
  between operations  13.8 us (6%)
  local copies, waits for them, and re-layouts  11.3 us (5%)
  other arithmetic  2.26 us (1%)
    ppermute x13, starting transfers between devices, ring(): return lax.ppermute(a, axis, [(i, (i + hop) % size) for i in range(size)])  40.8 us
    all_to_all x3, waiting for transfers between devices, spread(): return lax.all_to_all(copies, axis, split_axis=0, concat_axis=0, tiled=True)  25.2 us
    all_to_all x2, blocking collectives, dispatched(): lax.all_to_all(rows, EXP, split_axis=0, concat_axis=0, tiled=True)  24.7 us
    ppermute x13, waiting for transfers between devices, ring(): return lax.ppermute(a, axis, [(i, (i + hop) % size) for i in range(size)])  19 us
    all_to_all x3, starting transfers between devices, spread(): return lax.all_to_all(copies, axis, split_axis=0, concat_axis=0, tiled=True)  17.4 us
    all_to_all x1, starting transfers between devices, body(): lax.all_to_all(both, ('x', 'z'), split_axis=0, concat_axis=0, tiled=True)  16 us
    all_to_all x1, waiting for transfers between devices, body(): lax.all_to_all(both, ('x', 'z'), split_axis=0, concat_axis=0, tiled=True)  14.4 us
    all_to_all x1, blocking collectives, spread(): return lax.all_to_all(copies, axis, split_axis=0, concat_axis=0, tiled=True)  13.2 us
  transfers between devices with their start and end apart: 19, of which 9 were waited for; matrix products, arithmetic and copies ran while one was open for 1% of the time, Pallas kernels for 4%

profile of v2, /device:TPU:6, one launch (start us, length us, event | category | flops | bytes accessed | tf_op | source)
XLA Modules:
  0.0 215.1 jit_solution(13769693578563547657)
XLA Ops:
  6.5 0.7 all-gather.6.cloned.1.call-update
  7.3 0.8 reshape.44
  8.1 0.8 multiply_bitcast_fusion.rate_ref
  8.8 0.9 copy-done.8
  9.7 0.9 copy-done.10
  10.7 2.1 shard_map.136
  12.7 7.1 %all-to-all-start = ((f32[8,24,512]{2,1,0:T(8,128)}), f32[8,24,512]{2,1,0:T(8,128)S(1)}, u32[]{:S(2)}, u32[]{:S(2)}) async-start(f32[8,24,512]{2,1,0:T(8,128)} %shard_map.136), calls=%async_computation | async-start | bytes 786432 | tf_op jit(solution)/shard_map/all_to_all | solution.py:189
  19.8 15.1 %all-to-all-done.parts_ref = f32[8,24,512]{2,1,0:T(8,128)S(1)} async-done(((f32[8,24,512]{2,1,0:T(8,128)}), f32[8,24,512]{2,1,0:T(8,128)S(1)}, u32[]{:S(2)}, u32[]{:S(2)}) %all-to-all-start) | async-done | bytes 393248 | tf_op jit(solution)/shard_map/all_to_all | solution.py:189
  34.9 0.7 shard_map.137
  35.6 4.8 %all-to-all-start.1 = ((f32[4,24,512]{2,1,0:T(8,128)}), f32[4,24,512]{2,1,0:T(8,128)S(1)}, u32[]{:S(2)}, u32[]{:S(2)}) async-start(f32[4,24,512]{2,1,0:T(8,128)} %get-tuple-element.17), calls=%async_computation.1 | async-start | bytes 393216 | tf_op jit(solution)/shard_map/all_to_all | solution.py:189
  40.4 0.1 reshape.45
  40.5 4.2 %all-to-all-done.1.rows_ref = f32[4,24,512]{2,1,0:T(8,128)S(1)} async-done(((f32[4,24,512]{2,1,0:T(8,128)}), f32[4,24,512]{2,1,0:T(8,128)S(1)}, u32[]{:S(2)}, u32[]{:S(2)}) %all-to-all-start.1) | async-done | bytes 196640 | tf_op jit(solution)/shard_map/all_to_all | solution.py:189
  44.7 3.0 %shard_map.138 = bf16[4,128,512]{2,1,0:T(8,128)(2,1)} custom-call(s32[1]{0:T(128)} %bitcast.place_ref, bf16[128,512]{1,0:T(8,128)(2,1)S(1)} %copy-done.9, bf16[128,512]{1,0:T(8,128)(2,1)S(1)} %copy-done.11, bf16[128,512]{1,0:T(8,128)(2,1)S(1)} %copy-done.12, f32[16,512]{1,0:T(8,128)S(1)} %multiply_bitcast_fusion.rate_ref, f32[8,16,16]{2,1,0:T(8,128)S(1)} %bitcast.30, ...), custom_call_target="tpu_custom_call" | custom-call | flops 6291456 | bytes 524288 | tf_op jit(solution)/shard_map/pallas_call | solution.py:273
  47.7 5.5 %all-to-all-start.2 = ((bf16[4,128,512]{2,1,0:T(8,128)(2,1)}), bf16[4,128,512]{2,1,0:T(8,128)(2,1)S(1)}, u32[]{:S(2)}, u32[]{:S(2)}) async-start(bf16[4,128,512]{2,1,0:T(8,128)(2,1)} %shard_map.138), calls=%async_computation.2 | async-start | bytes 1048576 | tf_op jit(solution)/shard_map/all_to_all | solution.py:189
  53.2 6.0 %all-to-all-done.2.g_ref = bf16[4,128,512]{2,1,0:T(8,128)(2,1)S(1)} async-done(((bf16[4,128,512]{2,1,0:T(8,128)(2,1)}), bf16[4,128,512]{2,1,0:T(8,128)(2,1)S(1)}, u32[]{:S(2)}, u32[]{:S(2)}) %all-to-all-start.2) | async-done | bytes 524320 | tf_op jit(solution)/shard_map/all_to_all | solution.py:189
  59.2 1.2 copy-done.7
  60.4 0.7 shard_map.139
  61.2 2.1 collective-permute-start
  63.2 1.9 collective-permute-done
  65.1 0.9 add_convert_fusion
  66.1 16.0 %all-to-all-start.3 = ((bf16[32,8,1024]{2,1,0:T(8,128)(2,1)}), bf16[32,8,1024]{2,1,0:T(8,128)(2,1)S(1)}, u32[]{:S(2)}, u32[]{:S(2)}) async-start(bf16[32,8,1024]{2,1,0:T(8,128)(2,1)} %bitcast.8), calls=%async_computation.3 | async-start | bytes 1048576 | tf_op jit(solution)/shard_map/all_to_all | solution.py:308
  82.1 0.0 all-gather.4.cloned.1.call-start
  82.1 0.1 copy.33
  82.2 0.1 eq.48
  82.3 0.1 fusion.1
  82.4 0.2 select_reduce_fusion
  82.6 0.1 eq.52
  82.7 0.1 copy.34
  82.8 0.1 convert_convert_fusion
  82.9 0.1 fusion
  83.0 0.1 copy.36
  83.1 0.1 reshape.53
  83.1 0.1 copy.35
  83.2 14.4 %all-to-all-done.3.got_ref = bf16[32,8,1024]{2,1,0:T(8,128)(2,1)S(1)} async-done(((bf16[32,8,1024]{2,1,0:T(8,128)(2,1)}), bf16[32,8,1024]{2,1,0:T(8,128)(2,1)S(1)}, u32[]{:S(2)}, u32[]{:S(2)}) %all-to-all-start.3) | async-done | bytes 524320 | tf_op jit(solution)/shard_map/all_to_all | solution.py:308
  97.6 0.7 shard_map.140
  98.3 0.1 reshape.49
  98.4 13.1 %all_to_all.35 = bf16[16,2,2176]{2,1,0:T(2,128)(2,1)S(1)} all-to-all(bf16[16,2,2176]{2,1,0:T(2,128)(2,1)S(1)} %reshape.49), channel_id=1, replica_groups=mesh['x'=4,'y'=8,'z'=8,'c'=2] {'z','c'}, dimensions={0} | all-to-all | bytes 278528 | tf_op jit(solution)/shard_map/all_to_all | solution.py:199
  111.5 0.7 all_gather_reshape.3
  112.2 0.1 reshape.51
  112.3 11.6 %all_to_all.36 = bf16[16,2,2048]{2,1,0:T(2,128)(2,1)S(1)} all-to-all(bf16[16,2,2048]{2,1,0:T(2,128)(2,1)S(1)} %reshape.51), channel_id=1, replica_groups=mesh['x'=4,'y'=8,'z'=8,'c'=2] {'z','c'}, dimensions={0} | all-to-all | bytes 262144 | tf_op jit(solution)/shard_map/all_to_all | solution.py:199
  123.9 0.1 broadcast_in_dim.24
  124.0 13.2 %all_to_all.37.b0 = bf16[4,32,2048]{2,1,0:T(8,128)(2,1)S(1)} all-to-all(bf16[4,32,2048]{2,1,0:T(8,128)(2,1)S(1)} %broadcast_in_dim.25), channel_id=1, replica_groups=mesh['x'=4,'y'=8,'z'=8,'c'=2] {'x'}, dimensions={0} | all-to-all | bytes 1048576 | tf_op jit(solution)/shard_map/all_to_all | solution.py:189
  137.2 1.9 collective-permute-start.9
  139.2 3.9 %collective-permute-start.5 = (bf16[4,32,2048]{2,1,0:T(8,128)(2,1)S(1)}, bf16[4,32,2048]{2,1,0:T(8,128)(2,1)S(1)}, u32[]{:S(2)}, u32[]{:S(2)}) collective-permute-start(bf16[4,32,2048]{2,1,0:T(8,128)(2,1)S(1)} %all_to_all.37.b0), channel_id=1, source_target_pairs={{0,16},{16,32},{32,48},{48,64},{64,80},{80,96},{96,112},{112,0},{1... | collective-permute-start | bytes 1572872 | tf_op jit(solution)/shard_map/ppermute | solution.py:193
  143.1 1.5 copy-done.3
  144.6 2.2 %shard_map.141.w_ref = bf16[4096,512]{1,0:T(8,128)(2,1)S(1)} custom-call(bf16[224,4096]{1,0:T(8,128)(2,1)S(1)} %bitcast.26, bf16[224,4096]{1,0:T(8,128)(2,1)S(1)} %bitcast.27), custom_call_target="tpu_custom_call" | custom-call | flops 16777216 | bytes 16777216 | tf_op jit(solution)/shard_map/pallas_call | solution.py:300
  146.9 2.0 copy-done
  148.8 4.1 %collective-permute-start.1 = (bf16[256,2176]{1,0:T(8,128)(2,1)}, bf16[256,2176]{1,0:T(8,128)(2,1)S(1)}, u32[]{:S(2)}, u32[]{:S(2)}) collective-permute-start(bf16[256,2176]{1,0:T(8,128)(2,1)} %bitcast.33), channel_id=1, source_target_pairs={{0,128},{128,256},{256,384},{384,0},{1,129},{129,257},{257,385},{3... | collective-permute-start | bytes 3342344 | tf_op jit(solution)/shard_map/ppermute | solution.py:193
  152.9 1.9 collective-permute-start.3
  154.9 3.1 %collective-permute-start.10 = (bf16[4,32,2048]{2,1,0:T(8,128)(2,1)S(1)}, bf16[4,32,2048]{2,1,0:T(8,128)(2,1)S(1)}, u32[]{:S(2)}, u32[]{:S(2)}) collective-permute-start(bf16[4,32,2048]{2,1,0:T(8,128)(2,1)S(1)} %collective-permute-done.9.b7), channel_id=1, source_target_pairs={{0,112},{16,0},{32,16},{48,32},{64,48},{80,64},{96,80},{112,96},{1... | collective-permute-start | bytes 1572872 | tf_op jit(solution)/shard_map/ppermute | solution.py:193
  158.0 2.7 %collective-permute-start.6 = (bf16[4,32,2048]{2,1,0:T(8,128)(2,1)S(1)}, bf16[4,32,2048]{2,1,0:T(8,128)(2,1)S(1)}, u32[]{:S(2)}, u32[]{:S(2)}) collective-permute-start(bf16[4,32,2048]{2,1,0:T(8,128)(2,1)S(1)} %collective-permute-done.5.b1), channel_id=1, source_target_pairs={{0,16},{16,32},{32,48},{48,64},{64,80},{80,96},{96,112},{112,0},{1... | collective-permute-start | bytes 1572872 | tf_op jit(solution)/shard_map/ppermute | solution.py:193
  160.7 8.9 %collective-permute-done.10.b6 = bf16[4,32,2048]{2,1,0:T(8,128)(2,1)S(1)} collective-permute-done((bf16[4,32,2048]{2,1,0:T(8,128)(2,1)S(1)}, bf16[4,32,2048]{2,1,0:T(8,128)(2,1)S(1)}, u32[]{:S(2)}, u32[]{:S(2)}) %collective-permute-start.10) | collective-permute-done | bytes 524320 | tf_op jit(solution)/shard_map/ppermute | solution.py:193
  169.7 4.6 %collective-permute-start.11 = (bf16[4,32,2048]{2,1,0:T(8,128)(2,1)S(1)}, bf16[4,32,2048]{2,1,0:T(8,128)(2,1)S(1)}, u32[]{:S(2)}, u32[]{:S(2)}) collective-permute-start(bf16[4,32,2048]{2,1,0:T(8,128)(2,1)S(1)} %collective-permute-done.10.b6), channel_id=1, source_target_pairs={{0,112},{16,0},{32,16},{48,32},{64,48},{80,64},{96,80},{112,96},{1... | collective-permute-start | bytes 1572872 | tf_op jit(solution)/shard_map/ppermute | solution.py:193
  174.3 1.9 collective-permute-start.7
  176.2 0.6 collective-permute-done.1.a1
  176.9 5.2 %collective-permute-start.2 = (bf16[128,2176]{1,0:T(8,128)(2,1)S(1)}, bf16[128,2176]{1,0:T(8,128)(2,1)S(1)}, u32[]{:S(2)}, u32[]{:S(2)}) collective-permute-start(bf16[128,2176]{1,0:T(8,128)(2,1)S(1)} %slice.16), channel_id=1, source_target_pairs={{0,128},{128,256},{256,384},{384,0},{1,129},{129,257},{257,385},{3... | collective-permute-start | bytes 1671176 | tf_op jit(solution)/shard_map/ppermute | solution.py:193
  182.2 1.9 collective-permute-start.4
  184.1 5.5 %collective-permute-start.12 = (bf16[2,32,2048]{2,1,0:T(8,128)(2,1)S(1)}, bf16[2,32,2048]{2,1,0:T(8,128)(2,1)S(1)}, u32[]{:S(2)}, u32[]{:S(2)}) collective-permute-start(bf16[2,32,2048]{2,1,0:T(8,128)(2,1)S(1)} %slice.19), channel_id=1, source_target_pairs={{0,112},{16,0},{32,16},{48,32},{64,48},{80,64},{96,80},{112,96},{1... | collective-permute-start | bytes 786440 | tf_op jit(solution)/shard_map/ppermute | solution.py:193
  189.7 1.9 collective-permute-start.8
  191.6 0.1 pad_add_fusion.place_ref
  191.7 1.8 collective-permute-done.12.b41
  193.5 5.6 %collective-permute-done.8.b40 = bf16[2,32,2048]{2,1,0:T(8,128)(2,1)S(1)} collective-permute-done((bf16[2,32,2048]{2,1,0:T(8,128)(2,1)S(1)}, bf16[2,32,2048]{2,1,0:T(8,128)(2,1)S(1)}, u32[]{:S(2)}, u32[]{:S(2)}) %collective-permute-start.8) | collective-permute-done | bytes 262176 | tf_op jit(solution)/shard_map/ppermute | solution.py:193
  199.2 2.2 %copy-done.1 = bf16[4096,512]{1,0:T(8,128)(2,1)S(1)} copy-done((bf16[4096,512]{1,0:T(8,128)(2,1)S(1)}, bf16[4096,512]{1,0:T(8,128)(2,1)}, u32[]{:S(2)}) %copy-start.1) | copy-done | bytes 4194328
  201.4 6.9 %shard_map.142 = bf16[224,1024]{1,0:T(8,128)(2,1)} custom-call(s32[2]{0:T(128)S(1)} %pad_add_fusion.place_ref, bf16[256,2176]{1,0:T(8,128)(2,1)S(1)} %bitcast.35, bf16[256,2176]{1,0:T(8,128)(2,1)S(1)} %collective-permute-done.1.a1, bf16[128,2176]{1,0:T(8,128)(2,1)S(1)} %collective-permute-done.2.a20, bf16[128,2176]{1,0:T(8,128)(2,1)S(1)} %collective-permute-done.4.a21, ...), custom_call_target="tpu_custom_call" | custom-call | flops 3758096384 | bytes 8388608 | tf_op jit(solution)/shard_map/pallas_call | solution.py:341
  (51 shorter events, 0.4 us)
Async XLA Ops:
  6.5 52.6 %all-gather.6.cloned.1.call-start = ((), (), s32[]{:S(2)}) async-start(), calls=%async_computation.8 | async-start | bytes 1179648 | tf_op jit(solution)/shard_map/all_gather | solution.py:246
  8.1 32.3 %copy-start.14 = (f32[128,16]{0,1:T(8,128)S(1)}, f32[128,16]{0,1:T(8,128)}, u32[]{:S(2)}) copy-start(f32[128,16]{0,1:T(8,128)} %param.19) | copy-start | bytes 24580
  8.8 0.9 copy-start.8
  9.7 0.9 copy-start.10
  10.6 34.0 %copy-start.9 = (bf16[128,512]{1,0:T(8,128)(2,1)S(1)}, bf16[128,512]{1,0:T(8,128)(2,1)}, u32[]{:S(2)}) copy-start(bf16[128,512]{1,0:T(8,128)(2,1)} %x_ref.3) | copy-start | bytes 393220
  10.7 34.0 %copy-start.11 = (bf16[128,512]{1,0:T(8,128)(2,1)S(1)}, bf16[128,512]{1,0:T(8,128)(2,1)}, u32[]{:S(2)}) copy-start(bf16[128,512]{1,0:T(8,128)(2,1)} %d_ref.3) | copy-start | bytes 393220
  10.7 34.0 %copy-start.12 = (bf16[128,512]{1,0:T(8,128)(2,1)S(1)}, bf16[128,512]{1,0:T(8,128)(2,1)}, u32[]{:S(2)}) copy-start(bf16[128,512]{1,0:T(8,128)(2,1)} %z_ref.1) | copy-start | bytes 393220
  10.7 34.0 %copy-start.13 = (f32[512]{0:T(512)S(1)}, f32[512]{0:T(512)}, u32[]{:S(2)}) copy-start(f32[512]{0:T(512)} %param.20) | copy-start | bytes 6148
  12.7 22.2 %all-to-all-start = ((f32[8,24,512]{2,1,0:T(8,128)}), f32[8,24,512]{2,1,0:T(8,128)S(1)}, u32[]{:S(2)}, u32[]{:S(2)}) async-start(f32[8,24,512]{2,1,0:T(8,128)} %shard_map.136), calls=%async_computation | async-start | bytes 786432 | tf_op jit(solution)/shard_map/all_to_all | solution.py:189
  35.6 9.0 %all-to-all-start.1 = ((f32[4,24,512]{2,1,0:T(8,128)}), f32[4,24,512]{2,1,0:T(8,128)S(1)}, u32[]{:S(2)}, u32[]{:S(2)}) async-start(f32[4,24,512]{2,1,0:T(8,128)} %get-tuple-element.17), calls=%async_computation.1 | async-start | bytes 393216 | tf_op jit(solution)/shard_map/all_to_all | solution.py:189
  47.7 11.5 %all-to-all-start.2 = ((bf16[4,128,512]{2,1,0:T(8,128)(2,1)}), bf16[4,128,512]{2,1,0:T(8,128)(2,1)S(1)}, u32[]{:S(2)}, u32[]{:S(2)}) async-start(bf16[4,128,512]{2,1,0:T(8,128)(2,1)} %shard_map.138), calls=%async_computation.2 | async-start | bytes 1048576 | tf_op jit(solution)/shard_map/all_to_all | solution.py:189
  59.2 1.2 copy-start.7
  61.1 21.0 %copy-start.15 = (s32[8,2]{0,1:T(2,128)S(1)}, s32[8,2]{0,1:T(2,128)}, u32[]{:S(2)}) copy-start(s32[8,2]{0,1:T(2,128)} %param.24) | copy-start | bytes 196
  61.1 21.6 %copy-start.16 = (bf16[8,2]{0,1:T(2,128)(2,1)S(1)}, bf16[8,2]{0,1:T(2,128)(2,1)}, u32[]{:S(2)}) copy-start(bf16[8,2]{0,1:T(2,128)(2,1)} %param.25) | copy-start | bytes 100
  61.2 36.4 %copy-start.4 = (bf16[8,4096]{1,0:T(8,128)(2,1)S(1)}, bf16[8,4096]{1,0:T(8,128)(2,1)}, u32[]{:S(2)}) copy-start(bf16[8,4096]{1,0:T(8,128)(2,1)} %stream_ref.1) | copy-start | bytes 196612
  61.2 36.4 %copy-start.5 = (f32[4096]{0:T(1024)S(1)}, f32[4096]{0:T(1024)}, u32[]{:S(2)}) copy-start(f32[4096]{0:T(1024)} %param.23) | copy-start | bytes 49156
  61.2 3.9 %collective-permute-start = (bf16[4,8,8,1024]{3,2,1,0:T(8,128)(2,1)S(1)}, bf16[4,8,8,1024]{3,2,1,0:T(8,128)(2,1)S(1)}, u32[]{:S(2)}, u32[]{:S(2)}) collective-permute-start(bf16[4,8,8,1024]{3,2,1,0:T(8,128)(2,1)S(1)} %get-tuple-element.19), channel_id=1, source_target_pairs={{0,1},{1,0},{2,3},{3,2},{4,5},{5,4},{6,7},{7,6},{8,9},{9,8},{10,11... | collective-permute-start | bytes 1572872 | tf_op jit(solution)/shard_map/ppermute | solution.py:193
  66.1 31.5 %all-to-all-start.3 = ((bf16[32,8,1024]{2,1,0:T(8,128)(2,1)}), bf16[32,8,1024]{2,1,0:T(8,128)(2,1)S(1)}, u32[]{:S(2)}, u32[]{:S(2)}) async-start(bf16[32,8,1024]{2,1,0:T(8,128)(2,1)} %bitcast.8), calls=%async_computation.3 | async-start | bytes 1048576 | tf_op jit(solution)/shard_map/all_to_all | solution.py:308
  82.1 66.7 %all-gather.4.cloned.1.call-start = ((), (), s32[]{:S(2)}) async-start(), calls=%async_computation.7 | async-start | bytes 1253376 | tf_op jit(solution)/shard_map/all_gather | solution.py:205
  98.3 44.8 %copy-start.2 = (bf16[1,224,4096]{2,1,0:T(8,128)(2,1)S(1)}, bf16[1,224,4096]{2,1,0:T(8,128)(2,1)}, u32[]{:S(2)}) copy-start(bf16[1,224,4096]{2,1,0:T(8,128)(2,1)} %param.26) | copy-start | bytes 5505028
  137.2 17.6 %collective-permute-start.9 = (bf16[4,32,2048]{2,1,0:T(8,128)(2,1)S(1)}, bf16[4,32,2048]{2,1,0:T(8,128)(2,1)S(1)}, u32[]{:S(2)}, u32[]{:S(2)}) collective-permute-start(bf16[4,32,2048]{2,1,0:T(8,128)(2,1)S(1)} %all_to_all.37.b0), channel_id=1, source_target_pairs={{0,112},{16,0},{32,16},{48,32},{64,48},{80,64},{96,80},{112,96},{1... | collective-permute-start | bytes 1572872 | tf_op jit(solution)/shard_map/ppermute | solution.py:193
  139.2 18.8 %collective-permute-start.5 = (bf16[4,32,2048]{2,1,0:T(8,128)(2,1)S(1)}, bf16[4,32,2048]{2,1,0:T(8,128)(2,1)S(1)}, u32[]{:S(2)}, u32[]{:S(2)}) collective-permute-start(bf16[4,32,2048]{2,1,0:T(8,128)(2,1)S(1)} %all_to_all.37.b0), channel_id=1, source_target_pairs={{0,16},{16,32},{32,48},{48,64},{64,80},{80,96},{96,112},{112,0},{1... | collective-permute-start | bytes 1572872 | tf_op jit(solution)/shard_map/ppermute | solution.py:193
  143.1 1.5 copy-start.3
  146.8 2.0 copy-start
  148.8 50.4 %copy-start.6 = (bf16[8,32,2176]{2,1,0:T(8,128)(2,1)S(1)}, bf16[8,32,2176]{2,1,0:T(8,128)(2,1)}, u32[]{:S(2)}) copy-start(bf16[8,32,2176]{2,1,0:T(8,128)(2,1)} %all-gather.4.cloned.1.call-done) | copy-start | bytes 3342340
  148.8 28.1 %collective-permute-start.1 = (bf16[256,2176]{1,0:T(8,128)(2,1)}, bf16[256,2176]{1,0:T(8,128)(2,1)S(1)}, u32[]{:S(2)}, u32[]{:S(2)}) collective-permute-start(bf16[256,2176]{1,0:T(8,128)(2,1)} %bitcast.33), channel_id=1, source_target_pairs={{0,128},{128,256},{256,384},{384,0},{1,129},{129,257},{257,385},{3... | collective-permute-start | bytes 3342344 | tf_op jit(solution)/shard_map/ppermute | solution.py:193
  152.9 29.2 %collective-permute-start.3 = (bf16[256,2176]{1,0:T(8,128)(2,1)}, bf16[256,2176]{1,0:T(8,128)(2,1)S(1)}, u32[]{:S(2)}, u32[]{:S(2)}) collective-permute-start(bf16[256,2176]{1,0:T(8,128)(2,1)} %bitcast.34), channel_id=1, source_target_pairs={{0,384},{128,0},{256,128},{384,256},{1,385},{129,1},{257,129},{385... | collective-permute-start | bytes 3342344 | tf_op jit(solution)/shard_map/ppermute | solution.py:193
  154.9 14.8 %collective-permute-start.10 = (bf16[4,32,2048]{2,1,0:T(8,128)(2,1)S(1)}, bf16[4,32,2048]{2,1,0:T(8,128)(2,1)S(1)}, u32[]{:S(2)}, u32[]{:S(2)}) collective-permute-start(bf16[4,32,2048]{2,1,0:T(8,128)(2,1)S(1)} %collective-permute-done.9.b7), channel_id=1, source_target_pairs={{0,112},{16,0},{32,16},{48,32},{64,48},{80,64},{96,80},{112,96},{1... | collective-permute-start | bytes 1572872 | tf_op jit(solution)/shard_map/ppermute | solution.py:193
  158.0 16.3 %collective-permute-start.6 = (bf16[4,32,2048]{2,1,0:T(8,128)(2,1)S(1)}, bf16[4,32,2048]{2,1,0:T(8,128)(2,1)S(1)}, u32[]{:S(2)}, u32[]{:S(2)}) collective-permute-start(bf16[4,32,2048]{2,1,0:T(8,128)(2,1)S(1)} %collective-permute-done.5.b1), channel_id=1, source_target_pairs={{0,16},{16,32},{32,48},{48,64},{64,80},{80,96},{96,112},{112,0},{1... | collective-permute-start | bytes 1572872 | tf_op jit(solution)/shard_map/ppermute | solution.py:193
  169.7 14.4 %collective-permute-start.11 = (bf16[4,32,2048]{2,1,0:T(8,128)(2,1)S(1)}, bf16[4,32,2048]{2,1,0:T(8,128)(2,1)S(1)}, u32[]{:S(2)}, u32[]{:S(2)}) collective-permute-start(bf16[4,32,2048]{2,1,0:T(8,128)(2,1)S(1)} %collective-permute-done.10.b6), channel_id=1, source_target_pairs={{0,112},{16,0},{32,16},{48,32},{64,48},{80,64},{96,80},{112,96},{1... | collective-permute-start | bytes 1572872 | tf_op jit(solution)/shard_map/ppermute | solution.py:193
  174.3 15.4 %collective-permute-start.7 = (bf16[4,32,2048]{2,1,0:T(8,128)(2,1)S(1)}, bf16[4,32,2048]{2,1,0:T(8,128)(2,1)S(1)}, u32[]{:S(2)}, u32[]{:S(2)}) collective-permute-start(bf16[4,32,2048]{2,1,0:T(8,128)(2,1)S(1)} %collective-permute-done.6.b2), channel_id=1, source_target_pairs={{0,16},{16,32},{32,48},{48,64},{64,80},{80,96},{96,112},{112,0},{1... | collective-permute-start | bytes 1572872 | tf_op jit(solution)/shard_map/ppermute | solution.py:193
  176.9 22.3 %collective-permute-start.2 = (bf16[128,2176]{1,0:T(8,128)(2,1)S(1)}, bf16[128,2176]{1,0:T(8,128)(2,1)S(1)}, u32[]{:S(2)}, u32[]{:S(2)}) collective-permute-start(bf16[128,2176]{1,0:T(8,128)(2,1)S(1)} %slice.16), channel_id=1, source_target_pairs={{0,128},{128,256},{256,384},{384,0},{1,129},{129,257},{257,385},{3... | collective-permute-start | bytes 1671176 | tf_op jit(solution)/shard_map/ppermute | solution.py:193
  182.2 17.0 %collective-permute-start.4 = (bf16[128,2176]{1,0:T(8,128)(2,1)S(1)}, bf16[128,2176]{1,0:T(8,128)(2,1)S(1)}, u32[]{:S(2)}, u32[]{:S(2)}) collective-permute-start(bf16[128,2176]{1,0:T(8,128)(2,1)S(1)} %slice.17), channel_id=1, source_target_pairs={{0,384},{128,0},{256,128},{384,256},{1,385},{129,1},{257,129},{385... | collective-permute-start | bytes 1671176 | tf_op jit(solution)/shard_map/ppermute | solution.py:193
  184.1 9.4 %collective-permute-start.12 = (bf16[2,32,2048]{2,1,0:T(8,128)(2,1)S(1)}, bf16[2,32,2048]{2,1,0:T(8,128)(2,1)S(1)}, u32[]{:S(2)}, u32[]{:S(2)}) collective-permute-start(bf16[2,32,2048]{2,1,0:T(8,128)(2,1)S(1)} %slice.19), channel_id=1, source_target_pairs={{0,112},{16,0},{32,16},{48,32},{64,48},{80,64},{96,80},{112,96},{1... | collective-permute-start | bytes 786440 | tf_op jit(solution)/shard_map/ppermute | solution.py:193
  189.7 9.5 %collective-permute-start.8 = (bf16[2,32,2048]{2,1,0:T(8,128)(2,1)S(1)}, bf16[2,32,2048]{2,1,0:T(8,128)(2,1)S(1)}, u32[]{:S(2)}, u32[]{:S(2)}) collective-permute-start(bf16[2,32,2048]{2,1,0:T(8,128)(2,1)S(1)} %slice.18), channel_id=1, source_target_pairs={{0,16},{16,32},{32,48},{48,64},{64,80},{80,96},{96,112},{112,0},{1... | collective-permute-start | bytes 786440 | tf_op jit(solution)/shard_map/ppermute | solution.py:193
  199.2 2.2 %copy-start.1 = (bf16[4096,512]{1,0:T(8,128)(2,1)S(1)}, bf16[4096,512]{1,0:T(8,128)(2,1)}, u32[]{:S(2)}) copy-start(bf16[4096,512]{1,0:T(8,128)(2,1)} %copy-done) | copy-start | bytes 12582916
Sparse Core Ops, SparseCore 0:
  9.4 46.7 all-gather.5
  112.3 33.2 all-gather.3

commit v3 on v2

--- a/solution.py
+++ b/solution.py
@@ -19,6 +19,21 @@
 
 def softplus(v):
     return jnp.maximum(v, 0.0) + jnp.log1p(jnp.exp(-jnp.abs(v)))
+
+
+def pack(ref, state, total):
+    width = state.shape[1]
+    lanes = ref.shape[1] - width
+    ref[:, :width] = state
+    rows = [total[:, k * lanes : (k + 1) * lanes] for k in range(width // lanes)]
+    rows.append(jnp.zeros((state.shape[0] - len(rows), lanes), jnp.float32))
+    ref[:, width:] = jnp.concatenate(rows, axis=0)
+
+
+def unpack(part, width):
+    lanes = part.shape[1] - width
+    sums = [part[k : k + 1, width:] for k in range(width // lanes)]
+    return part[:, :width], jnp.concatenate(sums, axis=1)
 
 
 def last_kernel(x_ref, d_ref, rate_ref, b_ref, part_ref):
@@ -40,28 +55,24 @@
     start = (jnp.zeros((states, width), jnp.float32), jnp.zeros((1, width), jnp.float32))
     state, total = lax.fori_loop(0, x_ref.shape[0] // SPAN, some, start)
     for k in range(part_ref.shape[0]):
-        part_ref[k, :states, :] = state
-        part_ref[k, states:, :] = jnp.broadcast_to(total, (8, width))
+        pack(part_ref.at[k], state, total)
 
 
 def row_kernel(y_ref, parts_ref, rate_ref, near_ref, row_ref):
     rate = rate_ref[...]
     states, width = rate.shape
     y = y_ref[0]
-    state, total = jnp.zeros((states, width), jnp.float32), jnp.zeros((8, width), jnp.float32)
+    state, total = jnp.zeros((states, width), jnp.float32), jnp.zeros((1, width), jnp.float32)
     near, near_total = state, total
     for k in range(parts_ref.shape[0]):
-        sums = parts_ref[k, states:, :]
-        decay = jnp.exp2(rate * sums[0:1])
-        state = decay * state + parts_ref[k, :states, :]
+        own, sums = unpack(parts_ref[k], width)
+        state = jnp.exp2(rate * sums) * state + own
         total = total + sums
         near = jnp.where(k + 1 == y, state, near)
         near_total = jnp.where(k + 1 == y, total, near_total)
-    near_ref[:states, :] = near
-    near_ref[states:, :] = near_total
+    pack(near_ref, near, near_total)
     for k in range(row_ref.shape[0]):
-        row_ref[k, :states, :] = state
-        row_ref[k, states:, :] = total
+        pack(row_ref.at[k], state, total)
 
 
 def gated_kernel(place_ref, x_ref, d_ref, z_ref, rate_ref, b_ref, c_ref, skip_ref, near_ref, rows_ref, out_ref):
@@ -70,9 +81,10 @@
     place = lax.broadcasted_iota(jnp.int32, (SPAN, width), 0)
     start = jnp.zeros((states, width), jnp.float32)
     for k in range(rows_ref.shape[0] - 1):
-        later = jnp.exp2(rate * rows_ref[k, states : states + 1, :]) * start + rows_ref[k, :states, :]
-        start = jnp.where(k < place_ref[0], later, start)
-    start = jnp.exp2(rate * near_ref[states : states + 1, :]) * start + near_ref[:states, :]
+        own, sums = unpack(rows_ref[k], width)
+        start = jnp.where(k < place_ref[0], jnp.exp2(rate * sums) * start + own, start)
+    own, sums = unpack(near_ref[...], width)
+    start = jnp.exp2(rate * sums) * start + own
 
     def some(i, state):
         rows = pl.ds(pl.multiple_of(i * SPAN, SPAN), SPAN)
@@ -126,7 +138,7 @@
     rows = sel[:, 0:1] * normed[0:1, :]
     for t in range(1, normed.shape[0]):
         rows = rows + sel[:, t : t + 1] * normed[t : t + 1, :]
-    wide = b_ref.shape[1]
+    wide = a_ref.shape[1] - PAD
     a_ref[:, :wide] = rows[:, :wide].astype(jnp.bfloat16)
     a_ref[:, wide:] = gate_ref[...]
     b_ref[...] = rows[:, wide:].astype(jnp.bfloat16)
@@ -148,7 +160,7 @@
     lax.fori_loop(0, wg_ref.shape[1] // TURN, some, 0)
 
 
-def experts_kernel(place_ref, a0, a1, a20, a21, a3, b0, b1, b2, b3, b40, b41, b5, b6, b7, w_ref, out_ref, b):
+def experts_kernel(place_ref, a0, a1, a20, a21, a3, b0, b1, b2, b3, b4, b5, b6, b7, w_ref, out_ref, b):
     my_x, my_y = place_ref[0], place_ref[1]
     units = out_ref.shape[0]
     block = w_ref.shape[1] // 2
@@ -157,21 +169,9 @@
     group = NY * slots
     for dx in range(NX):
         x = lax.rem(my_x - dx + NX, NX)
-        for dy, ref in enumerate((b0, b1, b2, b3, None, b5, b6, b7)):
+        for dy, ref in enumerate((b0, b1, b2, b3, b4, b5, b6, b7)):
             y = lax.rem(my_y - dy + NY, NY)
-            at = pl.ds(pl.multiple_of(y * slots, slots), slots)
-            if ref is None:
-
-                @pl.when(x < NX // 2)
-                def _():
-                    b[at, :] = b40[x]
-
-                @pl.when(x >= NX // 2)
-                def _():
-                    b[at, :] = b41[x - NX // 2]
-
-            else:
-                b[at, :] = ref[x]
+            b[pl.ds(pl.multiple_of(y * slots, slots), slots), :] = ref[x]
         if dx == 2:
             first = jnp.concatenate([a20[...], a21[...]], axis=0)
         else:
@@ -199,21 +199,20 @@
     return lax.all_to_all(rows, EXP, split_axis=0, concat_axis=0, tiled=True).reshape(slots, width)
 
 
-def everywhere(a, b, n_experts, turned):
+def everywhere(a, b, n_experts):
     slots, wide = a.shape
     a = dispatched(a, n_experts)
     a0 = lax.all_gather(a, "y").reshape(NY * slots, wide)
     b = dispatched(b, n_experts)
     b0 = spread(jnp.broadcast_to(b[None], (NX,) + b.shape), "x")
     s1, t1 = ring(b0, "y", NY, 1), ring(b0, "y", NY, -1)
-    a0, turned = lax.optimization_barrier((a0, turned))
     ap, am = ring(a0, "x", NX, 1), ring(a0, "x", NX, -1)
     s2, t2 = ring(s1, "y", NY, 1), ring(t1, "y", NY, -1)
     s3, t3 = ring(s2, "y", NY, 1), ring(t2, "y", NY, -1)
-    s4, t4 = ring(s3[: NX // 2], "y", NY, 1), ring(t3[NX // 2 :], "y", NY, -1)
+    s4 = ring(s3, "y", NY, 1)
     half = NY * slots // 2
     ao0, ao1 = ring(ap[:half], "x", NX, 1), ring(am[half:], "x", NX, -1)
-    return [a0, ap, ao0, ao1, am], [b0, s1, s2, s3, s4, t4, t3, t2, t1], turned
+    return [a0, ap, ao0, ao1, am], [b0, s1, s2, s3, s4, t3, t2, t1]
 
 
 VMEM = pl.BlockSpec(memory_space=pltpu.VMEM)
@@ -251,12 +250,13 @@
     b3 = b_proj.reshape(spans, SPAN, states).transpose(0, 2, 1)
     c3 = c_proj.reshape(spans, SPAN, states).transpose(0, 2, 1)
     work = tokens * width * states
+    lanes = min(PAD, width)
     part = pl.pallas_call(
         last_kernel,
-        out_shape=jax.ShapeDtypeStruct((NY, states + 8, width), jnp.float32),
+        out_shape=jax.ShapeDtypeStruct((NY, states, width + lanes), jnp.float32),
         in_specs=[VMEM] * 4,
         out_specs=VMEM,
-        compiler_params=small,
+        compiler_params=pltpu.CompilerParams(vmem_limit_bytes=56 * MIB),
         cost_estimate=pl.CostEstimate(flops=4 * work, bytes_accessed=1 << 18, transcendentals=work),
     )(conv_out, delta_raw, rate, b3)
     part_shape = jax.ShapeDtypeStruct(part.shape[1:], jnp.float32)
@@ -306,6 +306,7 @@
         cost_estimate=pl.CostEstimate(flops=1 << 24, bytes_accessed=16 * MIB, transcendentals=0),
     )(wg, wu)
     got = lax.all_to_all(both, ("x", "z"), split_axis=0, concat_axis=0, tiled=True)
+    got, turned = lax.optimization_barrier((got, turned))
 
     most_slots = 4 * tok_rows // n_experts
     onehot = (
@@ -323,7 +324,7 @@
     gate = jnp.sum(pairs * gate_weights.astype(jnp.float32)[:, :, None, None], axis=(0, 1)).reshape(slots, 1)
     gate = jnp.pad(gate, ((0, 0), (0, PAD - 1))).astype(jnp.bfloat16)
 
-    wide = features // 2
+    wide = features * 17 // 32
     a_rows, b_rows = pl.pallas_call(
         slots_kernel,
         out_shape=[
@@ -335,13 +336,13 @@
         compiler_params=small,
         cost_estimate=pl.CostEstimate(flops=1 << 21, bytes_accessed=1 << 20, transcendentals=0),
     )(got, stream, norm_gain[None, :], sel, gate)
-    a_parts, b_parts, turned = everywhere(a_rows, b_rows, n_experts, turned)
+    a_parts, b_parts = everywhere(a_rows, b_rows, n_experts)
 
     total = NX * NY * slots
     result = pl.pallas_call(
         experts_kernel,
         out_shape=jax.ShapeDtypeStruct((hidden_units, total), jnp.bfloat16),
-        in_specs=[SMEM] + [VMEM] * 15,
+        in_specs=[SMEM] + [VMEM] * 14,
         out_specs=VMEM,
         scratch_shapes=[pltpu.VMEM((NY * slots, features - wide), jnp.bfloat16)],
         compiler_params=pltpu.CompilerParams(vmem_limit_bytes=28 * MIB),

time: 217 us -> 210 us (0.968)
  starting transfers between devices: 74.3 us -> 66.2 us
    ppermute x13 -> x12, starting transfers between devices: 40.8 us -> 33 us  [ring(): return lax.ppermute(a, axis, [(i, (i + hop) % size) for i in range(size)])]
    all_gather x1, waiting for transfers between devices: 0.01 us -> 7.45 us  [everywhere(): a0 = lax.all_gather(a, 'y').reshape(NY * slots, wide)]
    all_to_all x1, waiting for transfers between devices: 14.4 us -> 8.63 us  [body(): lax.all_to_all(both, ('x', 'z'), split_axis=0, concat_axis=0, tiled=True)]
    ppermute x13 -> x12, waiting for transfers between devices: 19 us -> 20.8 us  [ring(): return lax.ppermute(a, axis, [(i, (i + hop) % size) for i in range(size)])]
  transfers between devices with their start and end apart: 19 -> 18, of which waited for: 9 -> 11; matrix products, arithmetic and copies ran while one was open for 1% -> 2% of each run, Pallas kernels for 4% -> 4%
where the time goes in v3:
time: 210 us; the launch traced here: 208 us
  starting transfers between devices  66.2 us (32%)
  waiting for transfers between devices  60.9 us (29%)
  blocking collectives  37.4 us (18%)
  Pallas kernels  16.9 us (8%)
  between operations  13.8 us (7%)
  local copies, waits for them, and re-layouts  10 us (5%)
  other arithmetic  2.93 us (1%)
    ppermute x12, starting transfers between devices, ring(): return lax.ppermute(a, axis, [(i, (i + hop) % size) for i in range(size)])  33 us
    all_to_all x2, blocking collectives, dispatched(): lax.all_to_all(rows, EXP, split_axis=0, concat_axis=0, tiled=True)  24.6 us
    all_to_all x3, waiting for transfers between devices, spread(): return lax.all_to_all(copies, axis, split_axis=0, concat_axis=0, tiled=True)  23.3 us
    ppermute x12, waiting for transfers between devices, ring(): return lax.ppermute(a, axis, [(i, (i + hop) % size) for i in range(size)])  20.8 us
    all_to_all x3, starting transfers between devices, spread(): return lax.all_to_all(copies, axis, split_axis=0, concat_axis=0, tiled=True)  17.4 us
    all_to_all x1, starting transfers between devices, body(): lax.all_to_all(both, ('x', 'z'), split_axis=0, concat_axis=0, tiled=True)  15.7 us
    all_to_all x1, blocking collectives, spread(): return lax.all_to_all(copies, axis, split_axis=0, concat_axis=0, tiled=True)  12.8 us
    all_to_all x1, waiting for transfers between devices, body(): lax.all_to_all(both, ('x', 'z'), split_axis=0, concat_axis=0, tiled=True)  8.63 us
  transfers between devices with their start and end apart: 18, of which 11 were waited for; matrix products, arithmetic and copies ran while one was open for 2% of the time, Pallas kernels for 4%

profile of v3, /device:TPU:6, one launch (start us, length us, event | category | flops | bytes accessed | tf_op | source)
XLA Modules:
  0.0 208.0 jit_solution(16996199111630301420)
XLA Ops:
  6.5 0.7 all-gather.6.cloned.1.call-update
  7.3 0.8 reshape.44
  8.1 0.6 copy.41
  8.7 1.4 multiply_bitcast_fusion.rate_ref
  10.1 3.0 %shard_map.136 = f32[8,16,640]{2,1,0:T(8,128)} custom-call(bf16[128,512]{1,0:T(8,128)(2,1)} %x_ref.3, bf16[128,512]{1,0:T(8,128)(2,1)} %d_ref.3, f32[16,512]{1,0:T(8,128)} %multiply_bitcast_fusion.rate_ref, f32[8,16,16]{2,1,0:T(8,128)} %bitcast.29), custom_call_target="tpu_custom_call" | custom-call | flops 4194304 | bytes 262144 | tf_op jit(solution)/shard_map/pallas_call | solution.py:254
  13.2 7.1 %all-to-all-start = ((f32[8,16,640]{2,1,0:T(8,128)}), f32[8,16,640]{2,1,0:T(8,128)S(1)}, u32[]{:S(2)}, u32[]{:S(2)}) async-start(f32[8,16,640]{2,1,0:T(8,128)} %shard_map.136), calls=%async_computation | async-start | bytes 655360 | tf_op jit(solution)/shard_map/all_to_all | solution.py:189
  20.3 13.3 %all-to-all-done.parts_ref = f32[8,16,640]{2,1,0:T(8,128)S(1)} async-done(((f32[8,16,640]{2,1,0:T(8,128)}), f32[8,16,640]{2,1,0:T(8,128)S(1)}, u32[]{:S(2)}, u32[]{:S(2)}) %all-to-all-start) | async-done | bytes 327712 | tf_op jit(solution)/shard_map/all_to_all | solution.py:189
  33.6 0.7 shard_map.137
  34.3 4.8 %all-to-all-start.1 = ((f32[4,16,640]{2,1,0:T(8,128)}), f32[4,16,640]{2,1,0:T(8,128)S(1)}, u32[]{:S(2)}, u32[]{:S(2)}) async-start(f32[4,16,640]{2,1,0:T(8,128)} %get-tuple-element.17), calls=%async_computation.1 | async-start | bytes 327680 | tf_op jit(solution)/shard_map/all_to_all | solution.py:189
  39.1 0.1 reshape.45
  39.2 4.0 %all-to-all-done.1.rows_ref = f32[4,16,640]{2,1,0:T(8,128)S(1)} async-done(((f32[4,16,640]{2,1,0:T(8,128)}), f32[4,16,640]{2,1,0:T(8,128)S(1)}, u32[]{:S(2)}, u32[]{:S(2)}) %all-to-all-start.1) | async-done | bytes 163872 | tf_op jit(solution)/shard_map/all_to_all | solution.py:189
  43.2 3.0 %shard_map.138 = bf16[4,128,512]{2,1,0:T(8,128)(2,1)} custom-call(s32[1]{0:T(128)} %bitcast.place_ref, bf16[128,512]{1,0:T(8,128)(2,1)S(1)} %copy-done.10, bf16[128,512]{1,0:T(8,128)(2,1)S(1)} %copy-done.11, bf16[128,512]{1,0:T(8,128)(2,1)S(1)} %copy-done.12, f32[16,512]{1,0:T(8,128)S(1)} %copy-done.4, f32[8,16,16]{2,1,0:T(8,128)S(1)} %bitcast.30, ...), custom_call_target="tpu_custom_call" | custom-call | flops 6291456 | bytes 524288 | tf_op jit(solution)/shard_map/pallas_call | solution.py:273
  46.2 5.5 %all-to-all-start.2 = ((bf16[4,128,512]{2,1,0:T(8,128)(2,1)}), bf16[4,128,512]{2,1,0:T(8,128)(2,1)S(1)}, u32[]{:S(2)}, u32[]{:S(2)}) async-start(bf16[4,128,512]{2,1,0:T(8,128)(2,1)} %shard_map.138), calls=%async_computation.2 | async-start | bytes 1048576 | tf_op jit(solution)/shard_map/all_to_all | solution.py:189
  51.7 6.0 %all-to-all-done.2.g_ref = bf16[4,128,512]{2,1,0:T(8,128)(2,1)S(1)} async-done(((bf16[4,128,512]{2,1,0:T(8,128)(2,1)}), bf16[4,128,512]{2,1,0:T(8,128)(2,1)S(1)}, u32[]{:S(2)}, u32[]{:S(2)}) %all-to-all-start.2) | async-done | bytes 524320 | tf_op jit(solution)/shard_map/all_to_all | solution.py:189
  57.7 1.2 copy-done.9
  59.0 0.7 shard_map.139
  59.7 2.1 collective-permute-start
  61.8 1.9 collective-permute-done
  63.6 1.0 add_convert_fusion
  64.6 15.7 %all-to-all-start.3 = ((bf16[32,8,1024]{2,1,0:T(8,128)(2,1)}), bf16[32,8,1024]{2,1,0:T(8,128)(2,1)S(1)}, u32[]{:S(2)}, u32[]{:S(2)}) async-start(bf16[32,8,1024]{2,1,0:T(8,128)(2,1)} %bitcast.8), calls=%async_computation.3 | async-start | bytes 1048576 | tf_op jit(solution)/shard_map/all_to_all | solution.py:308
  80.3 0.0 all-gather.4.cloned.1.call-start
  80.4 0.1 copy.33
  80.5 0.1 eq.48
  80.5 0.1 fusion.1
  80.7 0.2 select_reduce_fusion
  80.8 0.1 eq.52
  80.9 0.1 copy.34
  81.0 0.1 convert_convert_fusion
  81.1 0.1 fusion
  81.2 0.1 copy.36
  81.3 0.1 reshape.53
  81.4 0.1 copy.35
  81.5 1.5 copy-done.3
  83.0 2.2 %shard_map.140.w_ref = bf16[4096,512]{1,0:T(8,128)(2,1)S(1)} custom-call(bf16[224,4096]{1,0:T(8,128)(2,1)S(1)} %bitcast.26, bf16[224,4096]{1,0:T(8,128)(2,1)S(1)} %bitcast.27), custom_call_target="tpu_custom_call" | custom-call | flops 16777216 | bytes 16777216 | tf_op jit(solution)/shard_map/pallas_call | solution.py:300
  85.2 2.0 copy-done
  87.2 8.6 %all-to-all-done.3.got_ref = bf16[32,8,1024]{2,1,0:T(8,128)(2,1)S(1)} async-done(((bf16[32,8,1024]{2,1,0:T(8,128)(2,1)}), bf16[32,8,1024]{2,1,0:T(8,128)(2,1)S(1)}, u32[]{:S(2)}, u32[]{:S(2)}) %all-to-all-start.3) | async-done | bytes 524320 | tf_op jit(solution)/shard_map/all_to_all | solution.py:308
  95.8 0.7 shard_map.141
  96.6 0.1 reshape.49
  96.6 13.0 %all_to_all.35 = bf16[16,2,2304]{2,1,0:T(2,128)(2,1)S(1)} all-to-all(bf16[16,2,2304]{2,1,0:T(2,128)(2,1)S(1)} %reshape.49), channel_id=1, replica_groups=mesh['x'=4,'y'=8,'z'=8,'c'=2] {'z','c'}, dimensions={0} | all-to-all | bytes 294912 | tf_op jit(solution)/shard_map/all_to_all | solution.py:199
  109.7 0.7 all_gather_reshape.3
  110.4 0.0 all-gather.4.cloned.1.call-update
  110.4 0.1 reshape.51
  110.5 11.6 %all_to_all.36 = bf16[16,2,1920]{2,1,0:T(2,128)(2,1)S(1)} all-to-all(bf16[16,2,1920]{2,1,0:T(2,128)(2,1)S(1)} %reshape.51), channel_id=1, replica_groups=mesh['x'=4,'y'=8,'z'=8,'c'=2] {'z','c'}, dimensions={0} | all-to-all | bytes 245760 | tf_op jit(solution)/shard_map/all_to_all | solution.py:199
  122.1 12.8 %all_to_all.37.b0 = bf16[4,32,1920]{2,1,0:T(8,128)(2,1)S(1)} all-to-all(bf16[4,32,1920]{2,1,0:T(8,128)(2,1)S(1)} %broadcast_in_dim.25), channel_id=1, replica_groups=mesh['x'=4,'y'=8,'z'=8,'c'=2] {'x'}, dimensions={0} | all-to-all | bytes 983040 | tf_op jit(solution)/shard_map/all_to_all | solution.py:189
  134.9 2.3 %collective-permute-start.5 = (bf16[4,32,1920]{2,1,0:T(8,128)(2,1)S(1)}, bf16[4,32,1920]{2,1,0:T(8,128)(2,1)S(1)}, u32[]{:S(2)}, u32[]{:S(2)}) collective-permute-start(bf16[4,32,1920]{2,1,0:T(8,128)(2,1)S(1)} %all_to_all.37.b0), channel_id=1, source_target_pairs={{0,16},{16,32},{32,48},{48,64},{64,80},{80,96},{96,112},{112,0},{1... | collective-permute-start | bytes 1474568 | tf_op jit(solution)/shard_map/ppermute | solution.py:193
  137.3 7.4 %all-gather.4.cloned.1.call-done = bf16[8,32,2304]{2,1,0:T(8,128)(2,1)} async-done(((bf16[1,32,2304]{2,1,0:T(8,128)(2,1)}), bf16[8,32,2304]{2,1,0:T(8,128)(2,1)}) %all-gather.4.cloned.1.call-update) | async-done | bytes 1179664 | tf_op jit(solution)/shard_map/all_gather | solution.py:205
  144.7 2.4 %collective-permute-start.1 = (bf16[256,2304]{1,0:T(8,128)(2,1)}, bf16[256,2304]{1,0:T(8,128)(2,1)S(1)}, u32[]{:S(2)}, u32[]{:S(2)}) collective-permute-start(bf16[256,2304]{1,0:T(8,128)(2,1)} %bitcast.33), channel_id=1, source_target_pairs={{0,128},{128,256},{256,384},{384,0},{1,129},{129,257},{257,385},{3... | collective-permute-start | bytes 3538952 | tf_op jit(solution)/shard_map/ppermute | solution.py:193
  147.1 3.5 %collective-permute-start.3 = (bf16[256,2304]{1,0:T(8,128)(2,1)}, bf16[256,2304]{1,0:T(8,128)(2,1)S(1)}, u32[]{:S(2)}, u32[]{:S(2)}) collective-permute-start(bf16[256,2304]{1,0:T(8,128)(2,1)} %bitcast.34), channel_id=1, source_target_pairs={{0,384},{128,0},{256,128},{384,256},{1,385},{129,1},{257,129},{385... | collective-permute-start | bytes 3538952 | tf_op jit(solution)/shard_map/ppermute | solution.py:193
  150.7 3.6 %collective-permute-start.9 = (bf16[4,32,1920]{2,1,0:T(8,128)(2,1)S(1)}, bf16[4,32,1920]{2,1,0:T(8,128)(2,1)S(1)}, u32[]{:S(2)}, u32[]{:S(2)}) collective-permute-start(bf16[4,32,1920]{2,1,0:T(8,128)(2,1)S(1)} %all_to_all.37.b0), channel_id=1, source_target_pairs={{0,112},{16,0},{32,16},{48,32},{64,48},{80,64},{96,80},{112,96},{1... | collective-permute-start | bytes 1474568 | tf_op jit(solution)/shard_map/ppermute | solution.py:193
  154.3 2.2 %collective-permute-start.6 = (bf16[4,32,1920]{2,1,0:T(8,128)(2,1)S(1)}, bf16[4,32,1920]{2,1,0:T(8,128)(2,1)S(1)}, u32[]{:S(2)}, u32[]{:S(2)}) collective-permute-start(bf16[4,32,1920]{2,1,0:T(8,128)(2,1)S(1)} %collective-permute-done.5.b1), channel_id=1, source_target_pairs={{0,16},{16,32},{32,48},{48,64},{64,80},{80,96},{96,112},{112,0},{1... | collective-permute-start | bytes 1474568 | tf_op jit(solution)/shard_map/ppermute | solution.py:193
  156.6 6.6 %collective-permute-done.9.b7 = bf16[4,32,1920]{2,1,0:T(8,128)(2,1)S(1)} collective-permute-done((bf16[4,32,1920]{2,1,0:T(8,128)(2,1)S(1)}, bf16[4,32,1920]{2,1,0:T(8,128)(2,1)S(1)}, u32[]{:S(2)}, u32[]{:S(2)}) %collective-permute-start.9) | collective-permute-done | bytes 491552 | tf_op jit(solution)/shard_map/ppermute | solution.py:193
  163.1 3.1 %collective-permute-start.10 = (bf16[4,32,1920]{2,1,0:T(8,128)(2,1)S(1)}, bf16[4,32,1920]{2,1,0:T(8,128)(2,1)S(1)}, u32[]{:S(2)}, u32[]{:S(2)}) collective-permute-start(bf16[4,32,1920]{2,1,0:T(8,128)(2,1)S(1)} %collective-permute-done.9.b7), channel_id=1, source_target_pairs={{0,112},{16,0},{32,16},{48,32},{64,48},{80,64},{96,80},{112,96},{1... | collective-permute-start | bytes 1474568 | tf_op jit(solution)/shard_map/ppermute | solution.py:193
  166.3 0.7 collective-permute-done.6.b2
  166.9 2.0 collective-permute-start.7
  169.0 2.1 %collective-permute-done.1.a1 = bf16[256,2304]{1,0:T(8,128)(2,1)S(1)} collective-permute-done((bf16[256,2304]{1,0:T(8,128)(2,1)}, bf16[256,2304]{1,0:T(8,128)(2,1)S(1)}, u32[]{:S(2)}, u32[]{:S(2)}) %collective-permute-start.1) | collective-permute-done | bytes 1179680 | tf_op jit(solution)/shard_map/ppermute | solution.py:193
  171.1 2.5 %collective-permute-start.2 = (bf16[128,2304]{1,0:T(8,128)(2,1)S(1)}, bf16[128,2304]{1,0:T(8,128)(2,1)S(1)}, u32[]{:S(2)}, u32[]{:S(2)}) collective-permute-start(bf16[128,2304]{1,0:T(8,128)(2,1)S(1)} %slice.8), channel_id=1, source_target_pairs={{0,128},{128,256},{256,384},{384,0},{1,129},{129,257},{257,385},{3... | collective-permute-start | bytes 1769480 | tf_op jit(solution)/shard_map/ppermute | solution.py:193
  173.7 3.3 %collective-permute-start.4 = (bf16[128,2304]{1,0:T(8,128)(2,1)S(1)}, bf16[128,2304]{1,0:T(8,128)(2,1)S(1)}, u32[]{:S(2)}, u32[]{:S(2)}) collective-permute-start(bf16[128,2304]{1,0:T(8,128)(2,1)S(1)} %slice.9), channel_id=1, source_target_pairs={{0,384},{128,0},{256,128},{384,256},{1,385},{129,1},{257,129},{385... | collective-permute-start | bytes 1769480 | tf_op jit(solution)/shard_map/ppermute | solution.py:193
  177.0 3.5 %collective-permute-start.11 = (bf16[4,32,1920]{2,1,0:T(8,128)(2,1)S(1)}, bf16[4,32,1920]{2,1,0:T(8,128)(2,1)S(1)}, u32[]{:S(2)}, u32[]{:S(2)}) collective-permute-start(bf16[4,32,1920]{2,1,0:T(8,128)(2,1)S(1)} %collective-permute-done.10.b6), channel_id=1, source_target_pairs={{0,112},{16,0},{32,16},{48,32},{64,48},{80,64},{96,80},{112,96},{1... | collective-permute-start | bytes 1474568 | tf_op jit(solution)/shard_map/ppermute | solution.py:193
  180.6 2.3 %collective-permute-start.8 = (bf16[4,32,1920]{2,1,0:T(8,128)(2,1)S(1)}, bf16[4,32,1920]{2,1,0:T(8,128)(2,1)S(1)}, u32[]{:S(2)}, u32[]{:S(2)}) collective-permute-start(bf16[4,32,1920]{2,1,0:T(8,128)(2,1)S(1)} %collective-permute-done.7.b3), channel_id=1, source_target_pairs={{0,16},{16,32},{32,48},{48,64},{64,80},{80,96},{96,112},{112,0},{1... | collective-permute-start | bytes 1474568 | tf_op jit(solution)/shard_map/ppermute | solution.py:193
  182.9 0.1 pad_add_fusion.place_ref
  183.0 4.8 %collective-permute-done.11.b5 = bf16[4,32,1920]{2,1,0:T(8,128)(2,1)S(1)} collective-permute-done((bf16[4,32,1920]{2,1,0:T(8,128)(2,1)S(1)}, bf16[4,32,1920]{2,1,0:T(8,128)(2,1)S(1)}, u32[]{:S(2)}, u32[]{:S(2)}) %collective-permute-start.11) | collective-permute-done | bytes 491552 | tf_op jit(solution)/shard_map/ppermute | solution.py:193
  187.8 4.8 %collective-permute-done.8.b4 = bf16[4,32,1920]{2,1,0:T(8,128)(2,1)S(1)} collective-permute-done((bf16[4,32,1920]{2,1,0:T(8,128)(2,1)S(1)}, bf16[4,32,1920]{2,1,0:T(8,128)(2,1)S(1)}, u32[]{:S(2)}, u32[]{:S(2)}) %collective-permute-start.8) | collective-permute-done | bytes 491552 | tf_op jit(solution)/shard_map/ppermute | solution.py:193
  192.6 2.2 %copy-done.1 = bf16[4096,512]{1,0:T(8,128)(2,1)S(1)} copy-done((bf16[4096,512]{1,0:T(8,128)(2,1)S(1)}, bf16[4096,512]{1,0:T(8,128)(2,1)}, u32[]{:S(2)}) %copy-start.1) | copy-done | bytes 4194328
  194.7 6.4 %shard_map.142 = bf16[224,1024]{1,0:T(8,128)(2,1)} custom-call(s32[2]{0:T(128)S(1)} %pad_add_fusion.place_ref, bf16[256,2304]{1,0:T(8,128)(2,1)S(1)} %bitcast.35, bf16[256,2304]{1,0:T(8,128)(2,1)S(1)} %collective-permute-done.1.a1, bf16[128,2304]{1,0:T(8,128)(2,1)S(1)} %collective-permute-done.2.a20, bf16[128,2304]{1,0:T(8,128)(2,1)S(1)} %collective-permute-done.4.a21, ...), custom_call_target="tpu_custom_call" | custom-call | flops 3758096384 | bytes 8388608 | tf_op jit(solution)/shard_map/pallas_call | solution.py:342
  (47 shorter events, 0.3 us)
Async XLA Ops:
  6.5 51.2 %all-gather.6.cloned.1.call-start = ((), (), s32[]{:S(2)}) async-start(), calls=%async_computation.8 | async-start | bytes 1179648 | tf_op jit(solution)/shard_map/all_gather | solution.py:245
  7.3 31.9 %copy-start.14 = (f32[128,16]{0,1:T(8,128)S(1)}, f32[128,16]{0,1:T(8,128)}, u32[]{:S(2)}) copy-start(f32[128,16]{0,1:T(8,128)} %param.19) | copy-start | bytes 24580
  8.7 34.5 %copy-start.6 = (f32[8,16,16]{1,2,0:T(8,128)S(1)}, f32[8,16,16]{1,2,0:T(8,128)}, u32[]{:S(2)}) copy-start(f32[8,16,16]{1,2,0:T(8,128)} %copy.41) | copy-start | bytes 24580
  8.7 34.5 %copy-start.10 = (bf16[128,512]{1,0:T(8,128)(2,1)S(1)}, bf16[128,512]{1,0:T(8,128)(2,1)}, u32[]{:S(2)}) copy-start(bf16[128,512]{1,0:T(8,128)(2,1)} %x_ref.3) | copy-start | bytes 393220
  8.7 34.5 %copy-start.11 = (bf16[128,512]{1,0:T(8,128)(2,1)S(1)}, bf16[128,512]{1,0:T(8,128)(2,1)}, u32[]{:S(2)}) copy-start(bf16[128,512]{1,0:T(8,128)(2,1)} %d_ref.3) | copy-start | bytes 393220
  8.7 34.5 %copy-start.12 = (bf16[128,512]{1,0:T(8,128)(2,1)S(1)}, bf16[128,512]{1,0:T(8,128)(2,1)}, u32[]{:S(2)}) copy-start(bf16[128,512]{1,0:T(8,128)(2,1)} %z_ref.1) | copy-start | bytes 393220
  8.7 34.5 %copy-start.13 = (f32[512]{0:T(512)S(1)}, f32[512]{0:T(512)}, u32[]{:S(2)}) copy-start(f32[512]{0:T(512)} %param.20) | copy-start | bytes 6148
  10.1 23.5 %copy-start.4 = (f32[16,512]{1,0:T(8,128)S(1)}, f32[16,512]{1,0:T(8,128)}, u32[]{:S(2)}) copy-start(f32[16,512]{1,0:T(8,128)} %multiply_bitcast_fusion.rate_ref) | copy-start | bytes 98308
  13.2 20.4 %all-to-all-start = ((f32[8,16,640]{2,1,0:T(8,128)}), f32[8,16,640]{2,1,0:T(8,128)S(1)}, u32[]{:S(2)}, u32[]{:S(2)}) async-start(f32[8,16,640]{2,1,0:T(8,128)} %shard_map.136), calls=%async_computation | async-start | bytes 655360 | tf_op jit(solution)/shard_map/all_to_all | solution.py:189
  34.3 8.9 %all-to-all-start.1 = ((f32[4,16,640]{2,1,0:T(8,128)}), f32[4,16,640]{2,1,0:T(8,128)S(1)}, u32[]{:S(2)}, u32[]{:S(2)}) async-start(f32[4,16,640]{2,1,0:T(8,128)} %get-tuple-element.17), calls=%async_computation.1 | async-start | bytes 327680 | tf_op jit(solution)/shard_map/all_to_all | solution.py:189
  46.2 11.5 %all-to-all-start.2 = ((bf16[4,128,512]{2,1,0:T(8,128)(2,1)}), bf16[4,128,512]{2,1,0:T(8,128)(2,1)S(1)}, u32[]{:S(2)}, u32[]{:S(2)}) async-start(bf16[4,128,512]{2,1,0:T(8,128)(2,1)} %shard_map.138), calls=%async_computation.2 | async-start | bytes 1048576 | tf_op jit(solution)/shard_map/all_to_all | solution.py:189
  57.7 1.2 copy-start.9
  59.7 20.7 %copy-start.15 = (s32[8,2]{0,1:T(2,128)S(1)}, s32[8,2]{0,1:T(2,128)}, u32[]{:S(2)}) copy-start(s32[8,2]{0,1:T(2,128)} %param.24) | copy-start | bytes 196
  59.7 21.3 %copy-start.16 = (bf16[8,2]{0,1:T(2,128)(2,1)S(1)}, bf16[8,2]{0,1:T(2,128)(2,1)}, u32[]{:S(2)}) copy-start(bf16[8,2]{0,1:T(2,128)(2,1)} %param.25) | copy-start | bytes 100
  59.7 21.8 %copy-start.2 = (bf16[1,224,4096]{2,1,0:T(8,128)(2,1)S(1)}, bf16[1,224,4096]{2,1,0:T(8,128)(2,1)}, u32[]{:S(2)}) copy-start(bf16[1,224,4096]{2,1,0:T(8,128)(2,1)} %param.26) | copy-start | bytes 5505028
  59.7 3.9 %collective-permute-start = (bf16[4,8,8,1024]{3,2,1,0:T(8,128)(2,1)S(1)}, bf16[4,8,8,1024]{3,2,1,0:T(8,128)(2,1)S(1)}, u32[]{:S(2)}, u32[]{:S(2)}) collective-permute-start(bf16[4,8,8,1024]{3,2,1,0:T(8,128)(2,1)S(1)} %get-tuple-element.19), channel_id=1, source_target_pairs={{0,1},{1,0},{2,3},{3,2},{4,5},{5,4},{6,7},{7,6},{8,9},{9,8},{10,11... | collective-permute-start | bytes 1572872 | tf_op jit(solution)/shard_map/ppermute | solution.py:193
  64.6 31.2 %all-to-all-start.3 = ((bf16[32,8,1024]{2,1,0:T(8,128)(2,1)}), bf16[32,8,1024]{2,1,0:T(8,128)(2,1)S(1)}, u32[]{:S(2)}, u32[]{:S(2)}) async-start(bf16[32,8,1024]{2,1,0:T(8,128)(2,1)} %bitcast.8), calls=%async_computation.3 | async-start | bytes 1048576 | tf_op jit(solution)/shard_map/all_to_all | solution.py:308
  80.3 64.4 %all-gather.4.cloned.1.call-start = ((), (), s32[]{:S(2)}) async-start(), calls=%async_computation.7 | async-start | bytes 1327104 | tf_op jit(solution)/shard_map/all_gather | solution.py:205
  81.5 1.5 copy-start.3
  83.0 12.8 %copy-start.5 = (bf16[8,4096]{1,0:T(8,128)(2,1)S(1)}, bf16[8,4096]{1,0:T(8,128)(2,1)}, u32[]{:S(2)}) copy-start(bf16[8,4096]{1,0:T(8,128)(2,1)} %stream_ref.1) | copy-start | bytes 196612
  83.0 12.8 %copy-start.7 = (f32[4096]{0:T(1024)S(1)}, f32[4096]{0:T(1024)}, u32[]{:S(2)}) copy-start(f32[4096]{0:T(1024)} %param.23) | copy-start | bytes 49156
  85.2 2.0 copy-start
  134.9 19.4 %collective-permute-start.5 = (bf16[4,32,1920]{2,1,0:T(8,128)(2,1)S(1)}, bf16[4,32,1920]{2,1,0:T(8,128)(2,1)S(1)}, u32[]{:S(2)}, u32[]{:S(2)}) collective-permute-start(bf16[4,32,1920]{2,1,0:T(8,128)(2,1)S(1)} %all_to_all.37.b0), channel_id=1, source_target_pairs={{0,16},{16,32},{32,48},{48,64},{64,80},{80,96},{96,112},{112,0},{1... | collective-permute-start | bytes 1474568 | tf_op jit(solution)/shard_map/ppermute | solution.py:193
  144.7 47.8 %copy-start.8 = (bf16[8,32,2304]{2,1,0:T(8,128)(2,1)S(1)}, bf16[8,32,2304]{2,1,0:T(8,128)(2,1)}, u32[]{:S(2)}) copy-start(bf16[8,32,2304]{2,1,0:T(8,128)(2,1)} %all-gather.4.cloned.1.call-done) | copy-start | bytes 3538948
  144.7 26.4 %collective-permute-start.1 = (bf16[256,2304]{1,0:T(8,128)(2,1)}, bf16[256,2304]{1,0:T(8,128)(2,1)S(1)}, u32[]{:S(2)}, u32[]{:S(2)}) collective-permute-start(bf16[256,2304]{1,0:T(8,128)(2,1)} %bitcast.33), channel_id=1, source_target_pairs={{0,128},{128,256},{256,384},{384,0},{1,129},{129,257},{257,385},{3... | collective-permute-start | bytes 3538952 | tf_op jit(solution)/shard_map/ppermute | solution.py:193
  147.1 26.5 %collective-permute-start.3 = (bf16[256,2304]{1,0:T(8,128)(2,1)}, bf16[256,2304]{1,0:T(8,128)(2,1)S(1)}, u32[]{:S(2)}, u32[]{:S(2)}) collective-permute-start(bf16[256,2304]{1,0:T(8,128)(2,1)} %bitcast.34), channel_id=1, source_target_pairs={{0,384},{128,0},{256,128},{384,256},{1,385},{129,1},{257,129},{385... | collective-permute-start | bytes 3538952 | tf_op jit(solution)/shard_map/ppermute | solution.py:193
  150.7 12.4 %collective-permute-start.9 = (bf16[4,32,1920]{2,1,0:T(8,128)(2,1)S(1)}, bf16[4,32,1920]{2,1,0:T(8,128)(2,1)S(1)}, u32[]{:S(2)}, u32[]{:S(2)}) collective-permute-start(bf16[4,32,1920]{2,1,0:T(8,128)(2,1)S(1)} %all_to_all.37.b0), channel_id=1, source_target_pairs={{0,112},{16,0},{32,16},{48,32},{64,48},{80,64},{96,80},{112,96},{1... | collective-permute-start | bytes 1474568 | tf_op jit(solution)/shard_map/ppermute | solution.py:193
  154.3 12.6 %collective-permute-start.6 = (bf16[4,32,1920]{2,1,0:T(8,128)(2,1)S(1)}, bf16[4,32,1920]{2,1,0:T(8,128)(2,1)S(1)}, u32[]{:S(2)}, u32[]{:S(2)}) collective-permute-start(bf16[4,32,1920]{2,1,0:T(8,128)(2,1)S(1)} %collective-permute-done.5.b1), channel_id=1, source_target_pairs={{0,16},{16,32},{32,48},{48,64},{64,80},{80,96},{96,112},{112,0},{1... | collective-permute-start | bytes 1474568 | tf_op jit(solution)/shard_map/ppermute | solution.py:193
  163.1 13.9 %collective-permute-start.10 = (bf16[4,32,1920]{2,1,0:T(8,128)(2,1)S(1)}, bf16[4,32,1920]{2,1,0:T(8,128)(2,1)S(1)}, u32[]{:S(2)}, u32[]{:S(2)}) collective-permute-start(bf16[4,32,1920]{2,1,0:T(8,128)(2,1)S(1)} %collective-permute-done.9.b7), channel_id=1, source_target_pairs={{0,112},{16,0},{32,16},{48,32},{64,48},{80,64},{96,80},{112,96},{1... | collective-permute-start | bytes 1474568 | tf_op jit(solution)/shard_map/ppermute | solution.py:193
  166.9 13.7 %collective-permute-start.7 = (bf16[4,32,1920]{2,1,0:T(8,128)(2,1)S(1)}, bf16[4,32,1920]{2,1,0:T(8,128)(2,1)S(1)}, u32[]{:S(2)}, u32[]{:S(2)}) collective-permute-start(bf16[4,32,1920]{2,1,0:T(8,128)(2,1)S(1)} %collective-permute-done.6.b2), channel_id=1, source_target_pairs={{0,16},{16,32},{32,48},{48,64},{64,80},{80,96},{96,112},{112,0},{1... | collective-permute-start | bytes 1474568 | tf_op jit(solution)/shard_map/ppermute | solution.py:193
  171.1 21.4 %collective-permute-start.2 = (bf16[128,2304]{1,0:T(8,128)(2,1)S(1)}, bf16[128,2304]{1,0:T(8,128)(2,1)S(1)}, u32[]{:S(2)}, u32[]{:S(2)}) collective-permute-start(bf16[128,2304]{1,0:T(8,128)(2,1)S(1)} %slice.8), channel_id=1, source_target_pairs={{0,128},{128,256},{256,384},{384,0},{1,129},{129,257},{257,385},{3... | collective-permute-start | bytes 1769480 | tf_op jit(solution)/shard_map/ppermute | solution.py:193
  173.7 18.8 %collective-permute-start.4 = (bf16[128,2304]{1,0:T(8,128)(2,1)S(1)}, bf16[128,2304]{1,0:T(8,128)(2,1)S(1)}, u32[]{:S(2)}, u32[]{:S(2)}) collective-permute-start(bf16[128,2304]{1,0:T(8,128)(2,1)S(1)} %slice.9), channel_id=1, source_target_pairs={{0,384},{128,0},{256,128},{384,256},{1,385},{129,1},{257,129},{385... | collective-permute-start | bytes 1769480 | tf_op jit(solution)/shard_map/ppermute | solution.py:193
  177.0 10.7 %collective-permute-start.11 = (bf16[4,32,1920]{2,1,0:T(8,128)(2,1)S(1)}, bf16[4,32,1920]{2,1,0:T(8,128)(2,1)S(1)}, u32[]{:S(2)}, u32[]{:S(2)}) collective-permute-start(bf16[4,32,1920]{2,1,0:T(8,128)(2,1)S(1)} %collective-permute-done.10.b6), channel_id=1, source_target_pairs={{0,112},{16,0},{32,16},{48,32},{64,48},{80,64},{96,80},{112,96},{1... | collective-permute-start | bytes 1474568 | tf_op jit(solution)/shard_map/ppermute | solution.py:193
  180.6 11.9 %collective-permute-start.8 = (bf16[4,32,1920]{2,1,0:T(8,128)(2,1)S(1)}, bf16[4,32,1920]{2,1,0:T(8,128)(2,1)S(1)}, u32[]{:S(2)}, u32[]{:S(2)}) collective-permute-start(bf16[4,32,1920]{2,1,0:T(8,128)(2,1)S(1)} %collective-permute-done.7.b3), channel_id=1, source_target_pairs={{0,16},{16,32},{32,48},{48,64},{64,80},{80,96},{96,112},{112,0},{1... | collective-permute-start | bytes 1474568 | tf_op jit(solution)/shard_map/ppermute | solution.py:193
  192.6 2.2 %copy-start.1 = (bf16[4096,512]{1,0:T(8,128)(2,1)S(1)}, bf16[4096,512]{1,0:T(8,128)(2,1)}, u32[]{:S(2)}) copy-start(bf16[4096,512]{1,0:T(8,128)(2,1)} %copy-done) | copy-start | bytes 12582916
Sparse Core Ops, SparseCore 0:
  9.4 45.6 all-gather.5
  110.5 34.1 all-gather.3

commit v4 on v3

--- a/solution.py
+++ b/solution.py
@@ -36,8 +36,13 @@
     return part[:, :width], jnp.concatenate(sums, axis=1)
 
 
+def columns(ref, i):
+    tokens = ref.shape[1]
+    return pltpu.roll(ref[...], lax.rem(tokens - i * SPAN, tokens), 1)
+
+
 def last_kernel(x_ref, d_ref, rate_ref, b_ref, part_ref):
-    rate = rate_ref[...]
+    rate = rate_ref[...] * -LOG2E
     states, width = rate.shape
 
     def some(i, carry):
@@ -45,7 +50,7 @@
         rows = pl.ds(pl.multiple_of(i * SPAN, SPAN), SPAN)
         dt = softplus(d_ref[rows, :].astype(jnp.float32))
         u = dt * x_ref[rows, :].astype(jnp.float32)
-        b = b_ref[i]
+        b = columns(b_ref, i)
         for t in range(SPAN):
             step = dt[t : t + 1, :]
             state = jnp.exp2(rate * step) * state + b[:, t : t + 1] * u[t : t + 1, :]
@@ -59,7 +64,7 @@
 
 
 def row_kernel(y_ref, parts_ref, rate_ref, near_ref, row_ref):
-    rate = rate_ref[...]
+    rate = rate_ref[...] * -LOG2E
     states, width = rate.shape
     y = y_ref[0]
     state, total = jnp.zeros((states, width), jnp.float32), jnp.zeros((1, width), jnp.float32)
@@ -76,7 +81,7 @@
 
 
 def gated_kernel(place_ref, x_ref, d_ref, z_ref, rate_ref, b_ref, c_ref, skip_ref, near_ref, rows_ref, out_ref):
-    rate = rate_ref[...]
+    rate = rate_ref[...] * -LOG2E
     states, width = rate.shape
     place = lax.broadcasted_iota(jnp.int32, (SPAN, width), 0)
     start = jnp.zeros((states, width), jnp.float32)
@@ -91,7 +96,7 @@
         dt = softplus(d_ref[rows, :].astype(jnp.float32))
         x = x_ref[rows, :].astype(jnp.float32)
         u = dt * x
-        b, c = b_ref[i], c_ref[i]
+        b, c = columns(b_ref, i), columns(c_ref, i)
         ssm = jnp.zeros((SPAN, width), jnp.float32)
         for t in range(SPAN):
             step = dt[t : t + 1, :]
@@ -160,7 +165,13 @@
     lax.fori_loop(0, wg_ref.shape[1] // TURN, some, 0)
 
 
-def experts_kernel(place_ref, a0, a1, a20, a21, a3, b0, b1, b2, b3, b4, b5, b6, b7, w_ref, out_ref, b):
+def early_kernel(a0, a1, a3, w_ref, out_ref):
+    wide = a0.shape[1] - PAD
+    for k, ref in enumerate((a0, a1, a3)):
+        out_ref[k] = jnp.dot(ref[:, :wide], w_ref[:wide, :], preferred_element_type=jnp.float32)
+
+
+def experts_kernel(place_ref, p_ref, a0, a1, a20, a21, a3, b0, b1, b2, b3, b4, b5, b6, b7, w_ref, out_ref, b):
     my_x, my_y = place_ref[0], place_ref[1]
     units = out_ref.shape[0]
     block = w_ref.shape[1] // 2
@@ -172,13 +183,15 @@
         for dy, ref in enumerate((b0, b1, b2, b3, b4, b5, b6, b7)):
             y = lax.rem(my_y - dy + NY, NY)
             b[pl.ds(pl.multiple_of(y * slots, slots), slots), :] = ref[x]
+        p = jnp.dot(b[...], w_ref[wide:, :], preferred_element_type=jnp.float32)
         if dx == 2:
             first = jnp.concatenate([a20[...], a21[...]], axis=0)
+            p = p + jnp.dot(first[:, :wide], w_ref[:wide, :], preferred_element_type=jnp.float32)
+            gate = first[:, wide:]
         else:
-            first = (a0, a1, None, a3)[dx][...]
-        p = jnp.dot(first[:, :wide], w_ref[:wide, :], preferred_element_type=jnp.float32)
-        p = p + jnp.dot(b[...], w_ref[wide:, :], preferred_element_type=jnp.float32)
-        gate = first[:, wide:].astype(jnp.float32)[:, 0:1]
+            p = p + p_ref[min(dx, 2)]
+            gate = (a0, a1, None, a3)[dx][:, wide:]
+        gate = gate.astype(jnp.float32)[:, 0:1]
         hidden, upward = p[:, :block], p[:, block:]
         value = hidden / (1.0 + jnp.exp(-hidden)) * upward * gate
         to = pl.ds(pl.multiple_of(x * group, group), group)
@@ -242,13 +255,10 @@
     n_experts = n_z * 2
     small = pltpu.CompilerParams(vmem_limit_bytes=12 * MIB)
 
-    columns = lax.all_gather(out_weight, "y")
+    gathered = lax.all_gather(out_weight, "y")
     place = jnp.stack([lax.axis_index("x"), lax.axis_index("y")]).astype(jnp.int32)
 
-    rate = decay_rate.T * -LOG2E
-    spans = tokens // SPAN
-    b3 = b_proj.reshape(spans, SPAN, states).transpose(0, 2, 1)
-    c3 = c_proj.reshape(spans, SPAN, states).transpose(0, 2, 1)
+    rate, b_t, c_t = decay_rate.T, b_proj.T, c_proj.T
     work = tokens * width * states
     lanes = min(PAD, width)
     part = pl.pallas_call(
@@ -258,7 +268,7 @@
         out_specs=VMEM,
         compiler_params=pltpu.CompilerParams(vmem_limit_bytes=56 * MIB),
         cost_estimate=pl.CostEstimate(flops=4 * work, bytes_accessed=1 << 18, transcendentals=work),
-    )(conv_out, delta_raw, rate, b3)
+    )(conv_out, delta_raw, rate, b_t)
     part_shape = jax.ShapeDtypeStruct(part.shape[1:], jnp.float32)
     row_shape = jax.ShapeDtypeStruct((NX,) + part.shape[1:], jnp.float32)
     near, row = pl.pallas_call(
@@ -277,7 +287,7 @@
         out_specs=VMEM,
         compiler_params=small,
         cost_estimate=pl.CostEstimate(flops=6 * work, bytes_accessed=1 << 19, transcendentals=work),
-    )(place[:1], conv_out, delta_raw, gate_z, rate, b3, c3, skip_gain[None, :], near, rows_before)
+    )(place[:1], conv_out, delta_raw, gate_z, rate, b_t, c_t, skip_gain[None, :], near, rows_before)
 
     core = lax.axis_index("c").astype(jnp.int32).reshape(1)
     shape = (NX, n_z, tok_rows, features // NX)
@@ -290,7 +300,7 @@
         cost_estimate=pl.CostEstimate(
             flops=2 * tokens * width * features, bytes_accessed=width * features * 2, transcendentals=0
         ),
-    )(core, spread(gated, "x"), columns)
+    )(core, spread(gated, "x"), gathered)
     theirs = ring(other, "c", 2, 1)
     both = (own + theirs.astype(jnp.float32)).astype(jnp.bfloat16)
     both = both.reshape(NX * n_z, tok_rows, features // NX)
@@ -339,10 +349,21 @@
     a_parts, b_parts = everywhere(a_rows, b_rows, n_experts)
 
     total = NX * NY * slots
+    a0, a1, _, _, a3 = a_parts
+    early = pl.pallas_call(
+        early_kernel,
+        out_shape=jax.ShapeDtypeStruct((3, NY * slots, 2 * block), jnp.float32),
+        in_specs=[VMEM] * 4,
+        out_specs=VMEM,
+        compiler_params=pltpu.CompilerParams(vmem_limit_bytes=20 * MIB),
+        cost_estimate=pl.CostEstimate(
+            flops=4 * block * 3 * NY * slots * wide, bytes_accessed=8 * MIB, transcendentals=0
+        ),
+    )(a0, a1, a3, turned)
     result = pl.pallas_call(
         experts_kernel,
         out_shape=jax.ShapeDtypeStruct((hidden_units, total), jnp.bfloat16),
-        in_specs=[SMEM] + [VMEM] * 14,
+        in_specs=[SMEM] + [VMEM] * 15,
         out_specs=VMEM,
         scratch_shapes=[pltpu.VMEM((NY * slots, features - wide), jnp.bfloat16)],
         compiler_params=pltpu.CompilerParams(vmem_limit_bytes=28 * MIB),
@@ -351,7 +372,7 @@
             bytes_accessed=total * features * 2,
             transcendentals=hidden_units * total,
         ),
-    )(place, *a_parts, *b_parts, turned)
+    )(place, early, *a_parts, *b_parts, turned)
     return result[None]
 
 

time: 210 us -> 204 us (0.971)
  waiting for transfers between devices: 60.9 us -> 55.5 us
    ppermute x12, waiting for transfers between devices: 20.8 us -> 15.3 us  [ring(): return lax.ppermute(a, axis, [(i, (i + hop) % size) for i in range(size)])]
    ppermute x12, starting transfers between devices: 33 us -> 35.8 us  [ring(): return lax.ppermute(a, axis, [(i, (i + hop) % size) for i in range(size)])]
    unnamed x35 -> x37, local copies, waits for them, and re-layouts: 7 us -> 7 us
  transfers between devices with their start and end apart: 18 -> 18, of which waited for: 11 -> 10; matrix products, arithmetic and copies ran while one was open for 2% -> 1% of each run, Pallas kernels for 4% -> 6%
where the time goes in v4:
time: 204 us; the launch traced here: 203 us
  starting transfers between devices  68 us (33%)
  waiting for transfers between devices  55.5 us (27%)
  blocking collectives  37.4 us (18%)
  Pallas kernels  18 us (9%)
  between operations  13.8 us (7%)
  local copies, waits for them, and re-layouts  8.5 us (4%)
    ppermute x12, starting transfers between devices, ring(): return lax.ppermute(a, axis, [(i, (i + hop) % size) for i in range(size)])  35.8 us
    all_to_all x2, blocking collectives, dispatched(): lax.all_to_all(rows, EXP, split_axis=0, concat_axis=0, tiled=True)  24.6 us
    all_to_all x3, waiting for transfers between devices, spread(): return lax.all_to_all(copies, axis, split_axis=0, concat_axis=0, tiled=True)  23.4 us
    all_to_all x3, starting transfers between devices, spread(): return lax.all_to_all(copies, axis, split_axis=0, concat_axis=0, tiled=True)  17.4 us
    ppermute x12, waiting for transfers between devices, ring(): return lax.ppermute(a, axis, [(i, (i + hop) % size) for i in range(size)])  15.3 us
    all_to_all x1, starting transfers between devices, body(): lax.all_to_all(both, ('x', 'z'), split_axis=0, concat_axis=0, tiled=True)  14.8 us
    all_to_all x1, blocking collectives, spread(): return lax.all_to_all(copies, axis, split_axis=0, concat_axis=0, tiled=True)  12.8 us
    all_to_all x1, waiting for transfers between devices, body(): lax.all_to_all(both, ('x', 'z'), split_axis=0, concat_axis=0, tiled=True)  8.62 us
  transfers between devices with their start and end apart: 18, of which 10 were waited for; matrix products, arithmetic and copies ran while one was open for 1% of the time, Pallas kernels for 6%

profile of v4, /device:TPU:6, one launch (start us, length us, event | category | flops | bytes accessed | tf_op | source)
XLA Modules:
  0.0 202.7 jit_solution(5583121591250847707)
XLA Ops:
  6.5 0.7 all-gather.6.cloned.1.call-update
  7.3 3.5 %shard_map.136 = f32[8,16,640]{2,1,0:T(8,128)} custom-call(bf16[128,512]{1,0:T(8,128)(2,1)} %x_ref.3, bf16[128,512]{1,0:T(8,128)(2,1)} %d_ref.3, f32[16,512]{1,0:T(8,128)} %bitcast.24, f32[16,128]{1,0:T(8,128)} %bitcast.29), custom_call_target="tpu_custom_call" | custom-call | flops 4194304 | bytes 262144 | tf_op jit(solution)/shard_map/pallas_call | solution.py:264
  10.8 7.1 %all-to-all-start = ((f32[8,16,640]{2,1,0:T(8,128)}), f32[8,16,640]{2,1,0:T(8,128)S(1)}, u32[]{:S(2)}, u32[]{:S(2)}) async-start(f32[8,16,640]{2,1,0:T(8,128)} %shard_map.136), calls=%async_computation | async-start | bytes 655360 | tf_op jit(solution)/shard_map/all_to_all | solution.py:202
  17.9 13.3 %all-to-all-done.parts_ref = f32[8,16,640]{2,1,0:T(8,128)S(1)} async-done(((f32[8,16,640]{2,1,0:T(8,128)}), f32[8,16,640]{2,1,0:T(8,128)S(1)}, u32[]{:S(2)}, u32[]{:S(2)}) %all-to-all-start) | async-done | bytes 327712 | tf_op jit(solution)/shard_map/all_to_all | solution.py:202
  31.2 0.7 shard_map.137
  31.9 4.8 %all-to-all-start.1 = ((f32[4,16,640]{2,1,0:T(8,128)}), f32[4,16,640]{2,1,0:T(8,128)S(1)}, u32[]{:S(2)}, u32[]{:S(2)}) async-start(f32[4,16,640]{2,1,0:T(8,128)} %get-tuple-element.17), calls=%async_computation.1 | async-start | bytes 327680 | tf_op jit(solution)/shard_map/all_to_all | solution.py:202
  36.7 4.1 %all-to-all-done.1.rows_ref = f32[4,16,640]{2,1,0:T(8,128)S(1)} async-done(((f32[4,16,640]{2,1,0:T(8,128)}), f32[4,16,640]{2,1,0:T(8,128)S(1)}, u32[]{:S(2)}, u32[]{:S(2)}) %all-to-all-start.1) | async-done | bytes 163872 | tf_op jit(solution)/shard_map/all_to_all | solution.py:202
  40.8 3.5 %shard_map.138 = bf16[4,128,512]{2,1,0:T(8,128)(2,1)} custom-call(s32[1]{0:T(128)} %bitcast.place_ref, bf16[128,512]{1,0:T(8,128)(2,1)S(1)} %copy-done.10, bf16[128,512]{1,0:T(8,128)(2,1)S(1)} %copy-done.11, bf16[128,512]{1,0:T(8,128)(2,1)S(1)} %copy-done.12, f32[16,512]{1,0:T(8,128)S(1)} %bitcast.26, f32[16,128]{1,0:T(8,128)S(1)} %bitcast.30, ...), custom_call_target="tpu_custom_call" | custom-call | flops 6291456 | bytes 524288 | tf_op jit(solution)/shard_map/pallas_call | solution.py:283
  44.3 5.5 %all-to-all-start.2 = ((bf16[4,128,512]{2,1,0:T(8,128)(2,1)}), bf16[4,128,512]{2,1,0:T(8,128)(2,1)S(1)}, u32[]{:S(2)}, u32[]{:S(2)}) async-start(bf16[4,128,512]{2,1,0:T(8,128)(2,1)} %shard_map.138), calls=%async_computation.2 | async-start | bytes 1048576 | tf_op jit(solution)/shard_map/all_to_all | solution.py:202
  49.8 6.0 %all-to-all-done.2.g_ref = bf16[4,128,512]{2,1,0:T(8,128)(2,1)S(1)} async-done(((bf16[4,128,512]{2,1,0:T(8,128)(2,1)}), bf16[4,128,512]{2,1,0:T(8,128)(2,1)S(1)}, u32[]{:S(2)}, u32[]{:S(2)}) %all-to-all-start.2) | async-done | bytes 524320 | tf_op jit(solution)/shard_map/all_to_all | solution.py:202
  55.8 1.2 copy-done.9
  57.0 0.7 shard_map.139
  57.8 1.9 collective-permute-start
  59.7 1.9 collective-permute-done
  61.6 1.0 add_convert_fusion
  62.5 14.8 %all-to-all-start.3 = ((bf16[32,8,1024]{2,1,0:T(8,128)(2,1)}), bf16[32,8,1024]{2,1,0:T(8,128)(2,1)S(1)}, u32[]{:S(2)}, u32[]{:S(2)}) async-start(bf16[32,8,1024]{2,1,0:T(8,128)(2,1)} %bitcast.8), calls=%async_computation.3 | async-start | bytes 1048576 | tf_op jit(solution)/shard_map/all_to_all | solution.py:318
  77.3 0.0 all-gather.4.cloned.1.call-start
  77.4 0.1 copy.27
  77.5 0.1 eq.48
  77.5 0.1 fusion.1
  77.6 0.2 select_reduce_fusion
  77.8 0.1 eq.52
  77.9 0.1 copy.28
  78.0 0.1 convert_convert_fusion
  78.1 0.1 fusion
  78.2 0.1 copy.30
  78.3 0.1 reshape.45
  78.4 0.1 copy.29
  78.5 0.0 copy-start.5
  78.5 1.5 copy-done.5
  80.0 2.2 %shard_map.140.w_ref = bf16[4096,512]{1,0:T(8,128)(2,1)S(1)} custom-call(bf16[224,4096]{1,0:T(8,128)(2,1)S(1)} %bitcast.21, bf16[224,4096]{1,0:T(8,128)(2,1)S(1)} %bitcast.22), custom_call_target="tpu_custom_call" | custom-call | flops 16777216 | bytes 16777216 | tf_op jit(solution)/shard_map/pallas_call | solution.py:310
  82.2 2.0 copy-done
  84.2 8.6 %all-to-all-done.3.got_ref = bf16[32,8,1024]{2,1,0:T(8,128)(2,1)S(1)} async-done(((bf16[32,8,1024]{2,1,0:T(8,128)(2,1)}), bf16[32,8,1024]{2,1,0:T(8,128)(2,1)S(1)}, u32[]{:S(2)}, u32[]{:S(2)}) %all-to-all-start.3) | async-done | bytes 524320 | tf_op jit(solution)/shard_map/all_to_all | solution.py:318
  92.8 0.7 shard_map.141
  93.5 0.1 reshape.41
  93.6 13.0 %all_to_all.35 = bf16[16,2,2304]{2,1,0:T(2,128)(2,1)S(1)} all-to-all(bf16[16,2,2304]{2,1,0:T(2,128)(2,1)S(1)} %reshape.41), channel_id=1, replica_groups=mesh['x'=4,'y'=8,'z'=8,'c'=2] {'z','c'}, dimensions={0} | all-to-all | bytes 294912 | tf_op jit(solution)/shard_map/all_to_all | solution.py:212
  106.6 0.7 all_gather_reshape.3
  107.4 0.0 all-gather.4.cloned.1.call-update
  107.4 0.1 reshape.43
  107.4 11.6 %all_to_all.36 = bf16[16,2,1920]{2,1,0:T(2,128)(2,1)S(1)} all-to-all(bf16[16,2,1920]{2,1,0:T(2,128)(2,1)S(1)} %reshape.43), channel_id=1, replica_groups=mesh['x'=4,'y'=8,'z'=8,'c'=2] {'z','c'}, dimensions={0} | all-to-all | bytes 245760 | tf_op jit(solution)/shard_map/all_to_all | solution.py:212
  119.1 12.8 %all_to_all.37.b0 = bf16[4,32,1920]{2,1,0:T(8,128)(2,1)S(1)} all-to-all(bf16[4,32,1920]{2,1,0:T(8,128)(2,1)S(1)} %broadcast_in_dim.25), channel_id=1, replica_groups=mesh['x'=4,'y'=8,'z'=8,'c'=2] {'x'}, dimensions={0} | all-to-all | bytes 983040 | tf_op jit(solution)/shard_map/all_to_all | solution.py:202
  131.9 2.0 collective-permute-start.5
  133.9 7.6 %all-gather.4.cloned.1.call-done = bf16[8,32,2304]{2,1,0:T(8,128)(2,1)} async-done(((bf16[1,32,2304]{2,1,0:T(8,128)(2,1)}), bf16[8,32,2304]{2,1,0:T(8,128)(2,1)}) %all-gather.4.cloned.1.call-update) | async-done | bytes 1179664 | tf_op jit(solution)/shard_map/all_gather | solution.py:218
  141.4 2.9 %collective-permute-start.2 = (bf16[256,2304]{1,0:T(8,128)(2,1)}, bf16[256,2304]{1,0:T(8,128)(2,1)S(1)}, u32[]{:S(2)}, u32[]{:S(2)}) collective-permute-start(bf16[256,2304]{1,0:T(8,128)(2,1)} %bitcast.17), channel_id=1, source_target_pairs={{0,384},{128,0},{256,128},{384,256},{1,385},{129,1},{257,129},{385... | collective-permute-start | bytes 3538952 | tf_op jit(solution)/shard_map/ppermute | solution.py:206
  144.4 4.2 %collective-permute-start.1 = (bf16[256,2304]{1,0:T(8,128)(2,1)}, bf16[256,2304]{1,0:T(8,128)(2,1)S(1)}, u32[]{:S(2)}, u32[]{:S(2)}) collective-permute-start(bf16[256,2304]{1,0:T(8,128)(2,1)} %bitcast.18), channel_id=1, source_target_pairs={{0,128},{128,256},{256,384},{384,0},{1,129},{129,257},{257,385},{3... | collective-permute-start | bytes 3538952 | tf_op jit(solution)/shard_map/ppermute | solution.py:206
  148.6 3.7 %collective-permute-start.9 = (bf16[4,32,1920]{2,1,0:T(8,128)(2,1)S(1)}, bf16[4,32,1920]{2,1,0:T(8,128)(2,1)S(1)}, u32[]{:S(2)}, u32[]{:S(2)}) collective-permute-start(bf16[4,32,1920]{2,1,0:T(8,128)(2,1)S(1)} %all_to_all.37.b0), channel_id=1, source_target_pairs={{0,112},{16,0},{32,16},{48,32},{64,48},{80,64},{96,80},{112,96},{1... | collective-permute-start | bytes 1474568 | tf_op jit(solution)/shard_map/ppermute | solution.py:206
  152.3 2.2 %collective-permute-start.6 = (bf16[4,32,1920]{2,1,0:T(8,128)(2,1)S(1)}, bf16[4,32,1920]{2,1,0:T(8,128)(2,1)S(1)}, u32[]{:S(2)}, u32[]{:S(2)}) collective-permute-start(bf16[4,32,1920]{2,1,0:T(8,128)(2,1)S(1)} %collective-permute-done.5.b1), channel_id=1, source_target_pairs={{0,16},{16,32},{32,48},{48,64},{64,80},{80,96},{96,112},{112,0},{1... | collective-permute-start | bytes 1474568 | tf_op jit(solution)/shard_map/ppermute | solution.py:206
  154.5 6.5 %collective-permute-done.9.b7 = bf16[4,32,1920]{2,1,0:T(8,128)(2,1)S(1)} collective-permute-done((bf16[4,32,1920]{2,1,0:T(8,128)(2,1)S(1)}, bf16[4,32,1920]{2,1,0:T(8,128)(2,1)S(1)}, u32[]{:S(2)}, u32[]{:S(2)}) %collective-permute-start.9) | collective-permute-done | bytes 491552 | tf_op jit(solution)/shard_map/ppermute | solution.py:206
  161.0 3.2 %collective-permute-start.10 = (bf16[4,32,1920]{2,1,0:T(8,128)(2,1)S(1)}, bf16[4,32,1920]{2,1,0:T(8,128)(2,1)S(1)}, u32[]{:S(2)}, u32[]{:S(2)}) collective-permute-start(bf16[4,32,1920]{2,1,0:T(8,128)(2,1)S(1)} %collective-permute-done.9.b7), channel_id=1, source_target_pairs={{0,112},{16,0},{32,16},{48,32},{64,48},{80,64},{96,80},{112,96},{1... | collective-permute-start | bytes 1474568 | tf_op jit(solution)/shard_map/ppermute | solution.py:206
  164.2 0.0 collective-permute-done.6.b2
  164.2 2.6 %collective-permute-start.7 = (bf16[4,32,1920]{2,1,0:T(8,128)(2,1)S(1)}, bf16[4,32,1920]{2,1,0:T(8,128)(2,1)S(1)}, u32[]{:S(2)}, u32[]{:S(2)}) collective-permute-start(bf16[4,32,1920]{2,1,0:T(8,128)(2,1)S(1)} %collective-permute-done.6.b2), channel_id=1, source_target_pairs={{0,16},{16,32},{32,48},{48,64},{64,80},{80,96},{96,112},{112,0},{1... | collective-permute-start | bytes 1474568 | tf_op jit(solution)/shard_map/ppermute | solution.py:206
  166.8 1.1 collective-permute-done.2.a3
  168.0 2.0 collective-permute-start.4
  170.0 5.1 %collective-permute-start.3 = (bf16[128,2304]{1,0:T(8,128)(2,1)S(1)}, bf16[128,2304]{1,0:T(8,128)(2,1)S(1)}, u32[]{:S(2)}, u32[]{:S(2)}) collective-permute-start(bf16[128,2304]{1,0:T(8,128)(2,1)S(1)} %slice.8), channel_id=1, source_target_pairs={{0,128},{128,256},{256,384},{384,0},{1,129},{129,257},{257,385},{3... | collective-permute-start | bytes 1769480 | tf_op jit(solution)/shard_map/ppermute | solution.py:206
  175.1 4.1 %collective-permute-start.11 = (bf16[4,32,1920]{2,1,0:T(8,128)(2,1)S(1)}, bf16[4,32,1920]{2,1,0:T(8,128)(2,1)S(1)}, u32[]{:S(2)}, u32[]{:S(2)}) collective-permute-start(bf16[4,32,1920]{2,1,0:T(8,128)(2,1)S(1)} %collective-permute-done.10.b6), channel_id=1, source_target_pairs={{0,112},{16,0},{32,16},{48,32},{64,48},{80,64},{96,80},{112,96},{1... | collective-permute-start | bytes 1474568 | tf_op jit(solution)/shard_map/ppermute | solution.py:206
  179.2 0.0 collective-permute-done.7.b3
  179.3 1.9 collective-permute-start.8
  181.2 0.1 pad_add_fusion.place_ref
  181.3 2.2 %copy-done.1 = bf16[4096,512]{1,0:T(8,128)(2,1)S(1)} copy-done((bf16[4096,512]{1,0:T(8,128)(2,1)S(1)}, bf16[4096,512]{1,0:T(8,128)(2,1)}, u32[]{:S(2)}) %copy-start.1) | copy-done | bytes 4194328
  183.5 2.0 shard_map.142.p_ref
  185.4 0.4 collective-permute-done.11.b5
  185.9 5.3 %collective-permute-done.8.b4 = bf16[4,32,1920]{2,1,0:T(8,128)(2,1)S(1)} collective-permute-done((bf16[4,32,1920]{2,1,0:T(8,128)(2,1)S(1)}, bf16[4,32,1920]{2,1,0:T(8,128)(2,1)S(1)}, u32[]{:S(2)}, u32[]{:S(2)}) %collective-permute-start.8) | collective-permute-done | bytes 491552 | tf_op jit(solution)/shard_map/ppermute | solution.py:206
  191.2 0.0 collective-permute-done.4.a21
  191.2 4.6 %shard_map.143 = bf16[224,1024]{1,0:T(8,128)(2,1)} custom-call(s32[2]{0:T(128)S(1)} %pad_add_fusion.place_ref, f32[3,256,512]{2,1,0:T(8,128)S(1)} %shard_map.142.p_ref, bf16[256,2304]{1,0:T(8,128)(2,1)S(1)} %bitcast.20, bf16[256,2304]{1,0:T(8,128)(2,1)S(1)} %collective-permute-done.1.a1, bf16[128,2304]{1,0:T(8,128)(2,1)S(1)} %collective-permute-done.3.a20, ...), custom_call_target="tpu_custom_call" | custom-call | flops 3758096384 | bytes 8388608 | tf_op jit(solution)/shard_map/pallas_call | solution.py:363
  (45 shorter events, 0.3 us)
Async XLA Ops:
  6.5 24.6 %copy-start.7 = (f32[512,16]{0,1:T(8,128)S(1)}, f32[512,16]{0,1:T(8,128)}, u32[]{:S(2)}) copy-start(f32[512,16]{0,1:T(8,128)} %param.17) | copy-start | bytes 98308
  6.5 49.3 %all-gather.6.cloned.1.call-start = ((), (), s32[]{:S(2)}) async-start(), calls=%async_computation.8 | async-start | bytes 1179648 | tf_op jit(solution)/shard_map/all_gather | solution.py:258
  7.3 33.5 %copy-start.10 = (bf16[128,512]{1,0:T(8,128)(2,1)S(1)}, bf16[128,512]{1,0:T(8,128)(2,1)}, u32[]{:S(2)}) copy-start(bf16[128,512]{1,0:T(8,128)(2,1)} %x_ref.3) | copy-start | bytes 393220
  7.3 33.5 %copy-start.11 = (bf16[128,512]{1,0:T(8,128)(2,1)S(1)}, bf16[128,512]{1,0:T(8,128)(2,1)}, u32[]{:S(2)}) copy-start(bf16[128,512]{1,0:T(8,128)(2,1)} %d_ref.3) | copy-start | bytes 393220
  7.3 33.5 %copy-start.12 = (bf16[128,512]{1,0:T(8,128)(2,1)S(1)}, bf16[128,512]{1,0:T(8,128)(2,1)}, u32[]{:S(2)}) copy-start(bf16[128,512]{1,0:T(8,128)(2,1)} %z_ref.1) | copy-start | bytes 393220
  7.3 33.5 %copy-start.13 = (f32[128,16]{0,1:T(8,128)S(1)}, f32[128,16]{0,1:T(8,128)}, u32[]{:S(2)}) copy-start(f32[128,16]{0,1:T(8,128)} %param.18) | copy-start | bytes 24580
  7.3 33.5 %copy-start.14 = (f32[128,16]{0,1:T(8,128)S(1)}, f32[128,16]{0,1:T(8,128)}, u32[]{:S(2)}) copy-start(f32[128,16]{0,1:T(8,128)} %param.19) | copy-start | bytes 24580
  7.3 33.5 %copy-start.15 = (f32[512]{0:T(512)S(1)}, f32[512]{0:T(512)}, u32[]{:S(2)}) copy-start(f32[512]{0:T(512)} %param.20) | copy-start | bytes 6148
  10.8 20.4 %all-to-all-start = ((f32[8,16,640]{2,1,0:T(8,128)}), f32[8,16,640]{2,1,0:T(8,128)S(1)}, u32[]{:S(2)}, u32[]{:S(2)}) async-start(f32[8,16,640]{2,1,0:T(8,128)} %shard_map.136), calls=%async_computation | async-start | bytes 655360 | tf_op jit(solution)/shard_map/all_to_all | solution.py:202
  31.9 8.9 %all-to-all-start.1 = ((f32[4,16,640]{2,1,0:T(8,128)}), f32[4,16,640]{2,1,0:T(8,128)S(1)}, u32[]{:S(2)}, u32[]{:S(2)}) async-start(f32[4,16,640]{2,1,0:T(8,128)} %get-tuple-element.17), calls=%async_computation.1 | async-start | bytes 327680 | tf_op jit(solution)/shard_map/all_to_all | solution.py:202
  44.3 11.5 %all-to-all-start.2 = ((bf16[4,128,512]{2,1,0:T(8,128)(2,1)}), bf16[4,128,512]{2,1,0:T(8,128)(2,1)S(1)}, u32[]{:S(2)}, u32[]{:S(2)}) async-start(bf16[4,128,512]{2,1,0:T(8,128)(2,1)} %shard_map.138), calls=%async_computation.2 | async-start | bytes 1048576 | tf_op jit(solution)/shard_map/all_to_all | solution.py:202
  55.8 1.2 copy-start.9
  57.8 3.8 %collective-permute-start = (bf16[4,8,8,1024]{3,2,1,0:T(8,128)(2,1)S(1)}, bf16[4,8,8,1024]{3,2,1,0:T(8,128)(2,1)S(1)}, u32[]{:S(2)}, u32[]{:S(2)}) collective-permute-start(bf16[4,8,8,1024]{3,2,1,0:T(8,128)(2,1)S(1)} %get-tuple-element.19), channel_id=1, source_target_pairs={{0,1},{1,0},{2,3},{3,2},{4,5},{5,4},{6,7},{7,6},{8,9},{9,8},{10,11... | collective-permute-start | bytes 1572872 | tf_op jit(solution)/shard_map/ppermute | solution.py:206
  61.6 15.8 %copy-start.17 = (bf16[8,2]{0,1:T(2,128)(2,1)S(1)}, bf16[8,2]{0,1:T(2,128)(2,1)}, u32[]{:S(2)}) copy-start(bf16[8,2]{0,1:T(2,128)(2,1)} %param.25) | copy-start | bytes 100
  61.6 15.8 %copy-start.16 = (s32[8,2]{0,1:T(2,128)S(1)}, s32[8,2]{0,1:T(2,128)}, u32[]{:S(2)}) copy-start(s32[8,2]{0,1:T(2,128)} %param.24) | copy-start | bytes 196
  61.6 16.9 %copy-start.4 = (bf16[1,224,4096]{2,1,0:T(8,128)(2,1)S(1)}, bf16[1,224,4096]{2,1,0:T(8,128)(2,1)}, u32[]{:S(2)}) copy-start(bf16[1,224,4096]{2,1,0:T(8,128)(2,1)} %param.26) | copy-start | bytes 5505028
  62.5 30.3 %all-to-all-start.3 = ((bf16[32,8,1024]{2,1,0:T(8,128)(2,1)}), bf16[32,8,1024]{2,1,0:T(8,128)(2,1)S(1)}, u32[]{:S(2)}, u32[]{:S(2)}) async-start(bf16[32,8,1024]{2,1,0:T(8,128)(2,1)} %bitcast.8), calls=%async_computation.3 | async-start | bytes 1048576 | tf_op jit(solution)/shard_map/all_to_all | solution.py:318
  77.3 64.1 %all-gather.4.cloned.1.call-start = ((), (), s32[]{:S(2)}) async-start(), calls=%async_computation.7 | async-start | bytes 1327104 | tf_op jit(solution)/shard_map/all_gather | solution.py:218
  78.5 1.5 copy-start.5
  80.0 12.8 %copy-start.6 = (bf16[8,4096]{1,0:T(8,128)(2,1)S(1)}, bf16[8,4096]{1,0:T(8,128)(2,1)}, u32[]{:S(2)}) copy-start(bf16[8,4096]{1,0:T(8,128)(2,1)} %stream_ref.1) | copy-start | bytes 196612
  80.0 12.8 %copy-start.8 = (f32[4096]{0:T(1024)S(1)}, f32[4096]{0:T(1024)}, u32[]{:S(2)}) copy-start(f32[4096]{0:T(1024)} %param.23) | copy-start | bytes 49156
  82.2 2.0 copy-start
  131.9 20.4 %collective-permute-start.5 = (bf16[4,32,1920]{2,1,0:T(8,128)(2,1)S(1)}, bf16[4,32,1920]{2,1,0:T(8,128)(2,1)S(1)}, u32[]{:S(2)}, u32[]{:S(2)}) collective-permute-start(bf16[4,32,1920]{2,1,0:T(8,128)(2,1)S(1)} %all_to_all.37.b0), channel_id=1, source_target_pairs={{0,16},{16,32},{32,48},{48,64},{64,80},{80,96},{96,112},{112,0},{1... | collective-permute-start | bytes 1474568 | tf_op jit(solution)/shard_map/ppermute | solution.py:206
  141.4 39.8 %copy-start.3 = (bf16[8,32,2304]{2,1,0:T(8,128)(2,1)S(1)}, bf16[8,32,2304]{2,1,0:T(8,128)(2,1)}, u32[]{:S(2)}) copy-start(bf16[8,32,2304]{2,1,0:T(8,128)(2,1)} %all-gather.4.cloned.1.call-done) | copy-start | bytes 3538948
  141.4 26.5 %collective-permute-start.2 = (bf16[256,2304]{1,0:T(8,128)(2,1)}, bf16[256,2304]{1,0:T(8,128)(2,1)S(1)}, u32[]{:S(2)}, u32[]{:S(2)}) collective-permute-start(bf16[256,2304]{1,0:T(8,128)(2,1)} %bitcast.17), channel_id=1, source_target_pairs={{0,384},{128,0},{256,128},{384,256},{1,385},{129,1},{257,129},{385... | collective-permute-start | bytes 3538952 | tf_op jit(solution)/shard_map/ppermute | solution.py:206
  144.4 25.6 %collective-permute-start.1 = (bf16[256,2304]{1,0:T(8,128)(2,1)}, bf16[256,2304]{1,0:T(8,128)(2,1)S(1)}, u32[]{:S(2)}, u32[]{:S(2)}) collective-permute-start(bf16[256,2304]{1,0:T(8,128)(2,1)} %bitcast.18), channel_id=1, source_target_pairs={{0,128},{128,256},{256,384},{384,0},{1,129},{129,257},{257,385},{3... | collective-permute-start | bytes 3538952 | tf_op jit(solution)/shard_map/ppermute | solution.py:206
  148.6 12.4 %collective-permute-start.9 = (bf16[4,32,1920]{2,1,0:T(8,128)(2,1)S(1)}, bf16[4,32,1920]{2,1,0:T(8,128)(2,1)S(1)}, u32[]{:S(2)}, u32[]{:S(2)}) collective-permute-start(bf16[4,32,1920]{2,1,0:T(8,128)(2,1)S(1)} %all_to_all.37.b0), channel_id=1, source_target_pairs={{0,112},{16,0},{32,16},{48,32},{64,48},{80,64},{96,80},{112,96},{1... | collective-permute-start | bytes 1474568 | tf_op jit(solution)/shard_map/ppermute | solution.py:206
  152.3 11.9 %collective-permute-start.6 = (bf16[4,32,1920]{2,1,0:T(8,128)(2,1)S(1)}, bf16[4,32,1920]{2,1,0:T(8,128)(2,1)S(1)}, u32[]{:S(2)}, u32[]{:S(2)}) collective-permute-start(bf16[4,32,1920]{2,1,0:T(8,128)(2,1)S(1)} %collective-permute-done.5.b1), channel_id=1, source_target_pairs={{0,16},{16,32},{32,48},{48,64},{64,80},{80,96},{96,112},{112,0},{1... | collective-permute-start | bytes 1474568 | tf_op jit(solution)/shard_map/ppermute | solution.py:206
  161.0 14.1 %collective-permute-start.10 = (bf16[4,32,1920]{2,1,0:T(8,128)(2,1)S(1)}, bf16[4,32,1920]{2,1,0:T(8,128)(2,1)S(1)}, u32[]{:S(2)}, u32[]{:S(2)}) collective-permute-start(bf16[4,32,1920]{2,1,0:T(8,128)(2,1)S(1)} %collective-permute-done.9.b7), channel_id=1, source_target_pairs={{0,112},{16,0},{32,16},{48,32},{64,48},{80,64},{96,80},{112,96},{1... | collective-permute-start | bytes 1474568 | tf_op jit(solution)/shard_map/ppermute | solution.py:206
  164.2 15.0 %collective-permute-start.7 = (bf16[4,32,1920]{2,1,0:T(8,128)(2,1)S(1)}, bf16[4,32,1920]{2,1,0:T(8,128)(2,1)S(1)}, u32[]{:S(2)}, u32[]{:S(2)}) collective-permute-start(bf16[4,32,1920]{2,1,0:T(8,128)(2,1)S(1)} %collective-permute-done.6.b2), channel_id=1, source_target_pairs={{0,16},{16,32},{32,48},{48,64},{64,80},{80,96},{96,112},{112,0},{1... | collective-permute-start | bytes 1474568 | tf_op jit(solution)/shard_map/ppermute | solution.py:206
  168.0 23.2 %collective-permute-start.4 = (bf16[128,2304]{1,0:T(8,128)(2,1)S(1)}, bf16[128,2304]{1,0:T(8,128)(2,1)S(1)}, u32[]{:S(2)}, u32[]{:S(2)}) collective-permute-start(bf16[128,2304]{1,0:T(8,128)(2,1)S(1)} %slice.9), channel_id=1, source_target_pairs={{0,384},{128,0},{256,128},{384,256},{1,385},{129,1},{257,129},{385... | collective-permute-start | bytes 1769480 | tf_op jit(solution)/shard_map/ppermute | solution.py:206
  170.0 21.2 %collective-permute-start.3 = (bf16[128,2304]{1,0:T(8,128)(2,1)S(1)}, bf16[128,2304]{1,0:T(8,128)(2,1)S(1)}, u32[]{:S(2)}, u32[]{:S(2)}) collective-permute-start(bf16[128,2304]{1,0:T(8,128)(2,1)S(1)} %slice.8), channel_id=1, source_target_pairs={{0,128},{128,256},{256,384},{384,0},{1,129},{129,257},{257,385},{3... | collective-permute-start | bytes 1769480 | tf_op jit(solution)/shard_map/ppermute | solution.py:206
  175.1 10.7 %collective-permute-start.11 = (bf16[4,32,1920]{2,1,0:T(8,128)(2,1)S(1)}, bf16[4,32,1920]{2,1,0:T(8,128)(2,1)S(1)}, u32[]{:S(2)}, u32[]{:S(2)}) collective-permute-start(bf16[4,32,1920]{2,1,0:T(8,128)(2,1)S(1)} %collective-permute-done.10.b6), channel_id=1, source_target_pairs={{0,112},{16,0},{32,16},{48,32},{64,48},{80,64},{96,80},{112,96},{1... | collective-permute-start | bytes 1474568 | tf_op jit(solution)/shard_map/ppermute | solution.py:206
  179.3 11.9 %collective-permute-start.8 = (bf16[4,32,1920]{2,1,0:T(8,128)(2,1)S(1)}, bf16[4,32,1920]{2,1,0:T(8,128)(2,1)S(1)}, u32[]{:S(2)}, u32[]{:S(2)}) collective-permute-start(bf16[4,32,1920]{2,1,0:T(8,128)(2,1)S(1)} %collective-permute-done.7.b3), channel_id=1, source_target_pairs={{0,16},{16,32},{32,48},{48,64},{64,80},{80,96},{96,112},{112,0},{1... | collective-permute-start | bytes 1474568 | tf_op jit(solution)/shard_map/ppermute | solution.py:206
  181.3 2.2 %copy-start.1 = (bf16[4096,512]{1,0:T(8,128)(2,1)S(1)}, bf16[4096,512]{1,0:T(8,128)(2,1)}, u32[]{:S(2)}) copy-start(bf16[4096,512]{1,0:T(8,128)(2,1)} %copy-done) | copy-start | bytes 12582916
  183.5 7.7 %copy-start.2 = (bf16[4096,512]{1,0:T(8,128)(2,1)S(1)}, bf16[4096,512]{1,0:T(8,128)(2,1)}, u32[]{:S(2)}) copy-start(bf16[4096,512]{1,0:T(8,128)(2,1)} %copy-done) | copy-start | bytes 12582916
Sparse Core Ops, SparseCore 0:
  9.4 45.4 all-gather.5
  107.5 33.8 all-gather.3

commit v5 on v4

--- a/solution.py
+++ b/solution.py
@@ -165,34 +165,52 @@
     lax.fori_loop(0, wg_ref.shape[1] // TURN, some, 0)
 
 
-def early_kernel(a0, a1, a3, w_ref, out_ref):
+def block_rows(y, dy, slots):
+    return pl.ds(pl.multiple_of(lax.rem(y - dy + NY, NY) * slots, slots), slots)
+
+
+def early_kernel(place_ref, a0, a1, a3, b0, b1, b2, b6, b7, w_ref, out_ref, b):
+    my_x, my_y = place_ref[0], place_ref[1]
     wide = a0.shape[1] - PAD
-    for k, ref in enumerate((a0, a1, a3)):
-        out_ref[k] = jnp.dot(ref[:, :wide], w_ref[:wide, :], preferred_element_type=jnp.float32)
-
-
-def experts_kernel(place_ref, p_ref, a0, a1, a20, a21, a3, b0, b1, b2, b3, b4, b5, b6, b7, w_ref, out_ref, b):
+    slots = b0.shape[1]
+    for dx in range(NX):
+        x = lax.rem(my_x - dx + NX, NX)
+        if dx == 2:
+            out_ref[dx] = jnp.zeros(out_ref.shape[1:], jnp.float32)
+        else:
+            a = (a0, a1, None, a3)[dx]
+            out_ref[dx] = jnp.dot(a[:, :wide], w_ref[:wide, :], preferred_element_type=jnp.float32)
+        for k, ref in enumerate((b0, b1, b2, b6, b7)):
+            b[k * slots : (k + 1) * slots, :] = ref[x]
+        p = jnp.dot(b[...], w_ref[wide:, :], preferred_element_type=jnp.float32)
+        for k, dy in enumerate((0, 1, 2, 6, 7)):
+            out_ref[dx, block_rows(my_y, dy, slots), :] += p[k * slots : (k + 1) * slots]
+
+
+def experts_kernel(place_ref, p_ref, a0, a1, a20, a21, a3, b3, b4, b5, w_ref, out_ref, b, sums):
     my_x, my_y = place_ref[0], place_ref[1]
     units = out_ref.shape[0]
     block = w_ref.shape[1] // 2
-    slots = b0.shape[1]
+    slots = b3.shape[1]
     wide = a0.shape[1] - PAD
     group = NY * slots
     for dx in range(NX):
         x = lax.rem(my_x - dx + NX, NX)
-        for dy, ref in enumerate((b0, b1, b2, b3, b4, b5, b6, b7)):
-            y = lax.rem(my_y - dy + NY, NY)
-            b[pl.ds(pl.multiple_of(y * slots, slots), slots), :] = ref[x]
+        for k, ref in enumerate((b3, b4, b5)):
+            b[k * slots : (k + 1) * slots, :] = ref[x]
         p = jnp.dot(b[...], w_ref[wide:, :], preferred_element_type=jnp.float32)
         if dx == 2:
             first = jnp.concatenate([a20[...], a21[...]], axis=0)
-            p = p + jnp.dot(first[:, :wide], w_ref[:wide, :], preferred_element_type=jnp.float32)
+            early = jnp.dot(first[:, :wide], w_ref[:wide, :], preferred_element_type=jnp.float32)
+            sums[...] = p_ref[dx] + early
             gate = first[:, wide:]
         else:
-            p = p + p_ref[min(dx, 2)]
+            sums[...] = p_ref[dx]
             gate = (a0, a1, None, a3)[dx][:, wide:]
+        for k, dy in enumerate((3, 4, 5)):
+            sums[block_rows(my_y, dy, slots), :] += p[k * slots : (k + 1) * slots]
         gate = gate.astype(jnp.float32)[:, 0:1]
-        hidden, upward = p[:, :block], p[:, block:]
+        hidden, upward = sums[:, :block], sums[:, block:]
         value = hidden / (1.0 + jnp.exp(-hidden)) * upward * gate
         to = pl.ds(pl.multiple_of(x * group, group), group)
         out_ref[:, to] = value.T[:units].astype(jnp.bfloat16)
@@ -350,29 +368,34 @@
 
     total = NX * NY * slots
     a0, a1, _, _, a3 = a_parts
+    late = b_parts[3:-2]
     early = pl.pallas_call(
         early_kernel,
-        out_shape=jax.ShapeDtypeStruct((3, NY * slots, 2 * block), jnp.float32),
-        in_specs=[VMEM] * 4,
+        out_shape=jax.ShapeDtypeStruct((NX, NY * slots, 2 * block), jnp.float32),
+        in_specs=[SMEM] + [VMEM] * 9,
         out_specs=VMEM,
+        scratch_shapes=[pltpu.VMEM((5 * slots, features - wide), jnp.bfloat16)],
         compiler_params=pltpu.CompilerParams(vmem_limit_bytes=20 * MIB),
         cost_estimate=pl.CostEstimate(
-            flops=4 * block * 3 * NY * slots * wide, bytes_accessed=8 * MIB, transcendentals=0
+            flops=4 * block * total * features * 2 // 3, bytes_accessed=8 * MIB, transcendentals=0
         ),
-    )(a0, a1, a3, turned)
+    )(place, a0, a1, a3, *b_parts[:3], *b_parts[-2:], turned)
     result = pl.pallas_call(
         experts_kernel,
         out_shape=jax.ShapeDtypeStruct((hidden_units, total), jnp.bfloat16),
-        in_specs=[SMEM] + [VMEM] * 15,
+        in_specs=[SMEM] + [VMEM] * (7 + len(late)),
         out_specs=VMEM,
-        scratch_shapes=[pltpu.VMEM((NY * slots, features - wide), jnp.bfloat16)],
+        scratch_shapes=[
+            pltpu.VMEM((3 * slots, features - wide), jnp.bfloat16),
+            pltpu.VMEM((NY * slots, 2 * block), jnp.float32),
+        ],
         compiler_params=pltpu.CompilerParams(vmem_limit_bytes=28 * MIB),
         cost_estimate=pl.CostEstimate(
-            flops=4 * hidden_units * total * features,
+            flops=4 * block * total * features // 3,
             bytes_accessed=total * features * 2,
             transcendentals=hidden_units * total,
         ),
-    )(place, early, *a_parts, *b_parts, turned)
+    )(place, early, *a_parts, *late, turned)
     return result[None]
 
 

time: 204 us -> 202 us (level)
  starting transfers between devices: 68 us -> 64.7 us
    ppermute x12, starting transfers between devices: 35.8 us -> 32.6 us  [ring(): return lax.ppermute(a, axis, [(i, (i + hop) % size) for i in range(size)])]
  transfers between devices with their start and end apart: 18 -> 18, of which waited for: 10 -> 10; matrix products, arithmetic and copies ran while one was open for 1% -> 1% of each run, Pallas kernels for 6% -> 7%
where the time goes in v5:
time: 202 us; the launch traced here: 200 us
  starting transfers between devices  64.7 us (32%)
  waiting for transfers between devices  54.6 us (27%)
  blocking collectives  37.4 us (19%)
  Pallas kernels  19.1 us (9%)
  between operations  13.8 us (7%)
  local copies, waits for them, and re-layouts  8.51 us (4%)
    ppermute x12, starting transfers between devices, ring(): return lax.ppermute(a, axis, [(i, (i + hop) % size) for i in range(size)])  32.6 us
    all_to_all x2, blocking collectives, dispatched(): lax.all_to_all(rows, EXP, split_axis=0, concat_axis=0, tiled=True)  24.6 us
    all_to_all x3, waiting for transfers between devices, spread(): return lax.all_to_all(copies, axis, split_axis=0, concat_axis=0, tiled=True)  23.4 us
    all_to_all x3, starting transfers between devices, spread(): return lax.all_to_all(copies, axis, split_axis=0, concat_axis=0, tiled=True)  17.4 us
    all_to_all x1, starting transfers between devices, body(): lax.all_to_all(both, ('x', 'z'), split_axis=0, concat_axis=0, tiled=True)  14.7 us
    ppermute x12, waiting for transfers between devices, ring(): return lax.ppermute(a, axis, [(i, (i + hop) % size) for i in range(size)])  14.3 us
    all_to_all x1, blocking collectives, spread(): return lax.all_to_all(copies, axis, split_axis=0, concat_axis=0, tiled=True)  12.8 us
    all_to_all x1, waiting for transfers between devices, body(): lax.all_to_all(both, ('x', 'z'), split_axis=0, concat_axis=0, tiled=True)  8.62 us
  transfers between devices with their start and end apart: 18, of which 10 were waited for; matrix products, arithmetic and copies ran while one was open for 1% of the time, Pallas kernels for 7%

profile of v5, /device:TPU:6, one launch (start us, length us, event | category | flops | bytes accessed | tf_op | source)
XLA Modules:
  0.0 199.6 jit_solution(13677718291484006378)
XLA Ops:
  6.6 0.0 all-gather.6.cloned.1.call-start
  6.6 0.7 all-gather.6.cloned.1.call-update
  7.3 3.4 %shard_map.136 = f32[8,16,640]{2,1,0:T(8,128)} custom-call(bf16[128,512]{1,0:T(8,128)(2,1)} %x_ref.3, bf16[128,512]{1,0:T(8,128)(2,1)} %d_ref.3, f32[16,512]{1,0:T(8,128)} %bitcast.24, f32[16,128]{1,0:T(8,128)} %bitcast.29), custom_call_target="tpu_custom_call" | custom-call | flops 4194304 | bytes 262144 | tf_op jit(solution)/shard_map/pallas_call | solution.py:282
  10.7 7.1 %all-to-all-start = ((f32[8,16,640]{2,1,0:T(8,128)}), f32[8,16,640]{2,1,0:T(8,128)S(1)}, u32[]{:S(2)}, u32[]{:S(2)}) async-start(f32[8,16,640]{2,1,0:T(8,128)} %shard_map.136), calls=%async_computation | async-start | bytes 655360 | tf_op jit(solution)/shard_map/all_to_all | solution.py:220
  17.8 13.3 %all-to-all-done.parts_ref = f32[8,16,640]{2,1,0:T(8,128)S(1)} async-done(((f32[8,16,640]{2,1,0:T(8,128)}), f32[8,16,640]{2,1,0:T(8,128)S(1)}, u32[]{:S(2)}, u32[]{:S(2)}) %all-to-all-start) | async-done | bytes 327712 | tf_op jit(solution)/shard_map/all_to_all | solution.py:220
  31.1 0.7 shard_map.137
  31.8 4.8 %all-to-all-start.1 = ((f32[4,16,640]{2,1,0:T(8,128)}), f32[4,16,640]{2,1,0:T(8,128)S(1)}, u32[]{:S(2)}, u32[]{:S(2)}) async-start(f32[4,16,640]{2,1,0:T(8,128)} %get-tuple-element.17), calls=%async_computation.1 | async-start | bytes 327680 | tf_op jit(solution)/shard_map/all_to_all | solution.py:220
  36.6 4.1 %all-to-all-done.1.rows_ref = f32[4,16,640]{2,1,0:T(8,128)S(1)} async-done(((f32[4,16,640]{2,1,0:T(8,128)}), f32[4,16,640]{2,1,0:T(8,128)S(1)}, u32[]{:S(2)}, u32[]{:S(2)}) %all-to-all-start.1) | async-done | bytes 163872 | tf_op jit(solution)/shard_map/all_to_all | solution.py:220
  40.7 3.5 %shard_map.138 = bf16[4,128,512]{2,1,0:T(8,128)(2,1)} custom-call(s32[1]{0:T(128)} %bitcast.place_ref, bf16[128,512]{1,0:T(8,128)(2,1)S(1)} %copy-done.10, bf16[128,512]{1,0:T(8,128)(2,1)S(1)} %copy-done.11, bf16[128,512]{1,0:T(8,128)(2,1)S(1)} %copy-done.12, f32[16,512]{1,0:T(8,128)S(1)} %bitcast.26, f32[16,128]{1,0:T(8,128)S(1)} %bitcast.30, ...), custom_call_target="tpu_custom_call" | custom-call | flops 6291456 | bytes 524288 | tf_op jit(solution)/shard_map/pallas_call | solution.py:301
  44.2 5.5 %all-to-all-start.2 = ((bf16[4,128,512]{2,1,0:T(8,128)(2,1)}), bf16[4,128,512]{2,1,0:T(8,128)(2,1)S(1)}, u32[]{:S(2)}, u32[]{:S(2)}) async-start(bf16[4,128,512]{2,1,0:T(8,128)(2,1)} %shard_map.138), calls=%async_computation.2 | async-start | bytes 1048576 | tf_op jit(solution)/shard_map/all_to_all | solution.py:220
  49.7 6.0 %all-to-all-done.2.g_ref = bf16[4,128,512]{2,1,0:T(8,128)(2,1)S(1)} async-done(((bf16[4,128,512]{2,1,0:T(8,128)(2,1)}), bf16[4,128,512]{2,1,0:T(8,128)(2,1)S(1)}, u32[]{:S(2)}, u32[]{:S(2)}) %all-to-all-start.2) | async-done | bytes 524320 | tf_op jit(solution)/shard_map/all_to_all | solution.py:220
  55.7 1.2 copy-done.9
  56.9 0.7 shard_map.139
  57.7 0.0 copy-start.17
  57.7 0.0 copy-start.4
  57.7 2.1 %collective-permute-start = (bf16[4,8,8,1024]{3,2,1,0:T(8,128)(2,1)S(1)}, bf16[4,8,8,1024]{3,2,1,0:T(8,128)(2,1)S(1)}, u32[]{:S(2)}, u32[]{:S(2)}) collective-permute-start(bf16[4,8,8,1024]{3,2,1,0:T(8,128)(2,1)S(1)} %get-tuple-element.19), channel_id=1, source_target_pairs={{0,1},{1,0},{2,3},{3,2},{4,5},{5,4},{6,7},{7,6},{8,9},{9,8},{10,11... | collective-permute-start | bytes 1572872 | tf_op jit(solution)/shard_map/ppermute | solution.py:224
  59.7 1.9 collective-permute-done
  61.6 1.0 add_convert_fusion
  62.6 14.7 %all-to-all-start.3 = ((bf16[32,8,1024]{2,1,0:T(8,128)(2,1)}), bf16[32,8,1024]{2,1,0:T(8,128)(2,1)S(1)}, u32[]{:S(2)}, u32[]{:S(2)}) async-start(bf16[32,8,1024]{2,1,0:T(8,128)(2,1)} %bitcast.8), calls=%async_computation.3 | async-start | bytes 1048576 | tf_op jit(solution)/shard_map/all_to_all | solution.py:336
  77.3 0.0 all-gather.4.cloned.1.call-start
  77.3 0.1 copy.27
  77.4 0.1 eq.48
  77.5 0.1 fusion.1
  77.6 0.2 select_reduce_fusion
  77.8 0.1 eq.52
  77.9 0.1 copy.28
  78.0 0.1 convert_convert_fusion
  78.0 0.1 fusion
  78.1 0.1 copy.29
  78.2 0.1 copy.30
  78.3 0.1 reshape.45
  78.4 0.0 copy-start.5
  78.4 1.5 copy-done.5
  79.9 2.2 %shard_map.140.w_ref = bf16[4096,512]{1,0:T(8,128)(2,1)S(1)} custom-call(bf16[224,4096]{1,0:T(8,128)(2,1)S(1)} %bitcast.21, bf16[224,4096]{1,0:T(8,128)(2,1)S(1)} %bitcast.22), custom_call_target="tpu_custom_call" | custom-call | flops 16777216 | bytes 16777216 | tf_op jit(solution)/shard_map/pallas_call | solution.py:328
  82.2 2.0 copy-done
  84.1 8.6 %all-to-all-done.3.got_ref = bf16[32,8,1024]{2,1,0:T(8,128)(2,1)S(1)} async-done(((bf16[32,8,1024]{2,1,0:T(8,128)(2,1)}), bf16[32,8,1024]{2,1,0:T(8,128)(2,1)S(1)}, u32[]{:S(2)}, u32[]{:S(2)}) %all-to-all-start.3) | async-done | bytes 524320 | tf_op jit(solution)/shard_map/all_to_all | solution.py:336
  92.8 0.7 shard_map.141
  93.5 0.1 reshape.41
  93.6 13.0 %all_to_all.35 = bf16[16,2,2304]{2,1,0:T(2,128)(2,1)S(1)} all-to-all(bf16[16,2,2304]{2,1,0:T(2,128)(2,1)S(1)} %reshape.41), channel_id=1, replica_groups=mesh['x'=4,'y'=8,'z'=8,'c'=2] {'z','c'}, dimensions={0} | all-to-all | bytes 294912 | tf_op jit(solution)/shard_map/all_to_all | solution.py:230
  106.6 0.7 all_gather_reshape.3
  107.3 0.0 all-gather.4.cloned.1.call-update
  107.3 0.1 reshape.43
  107.4 11.6 %all_to_all.36 = bf16[16,2,1920]{2,1,0:T(2,128)(2,1)S(1)} all-to-all(bf16[16,2,1920]{2,1,0:T(2,128)(2,1)S(1)} %reshape.43), channel_id=1, replica_groups=mesh['x'=4,'y'=8,'z'=8,'c'=2] {'z','c'}, dimensions={0} | all-to-all | bytes 245760 | tf_op jit(solution)/shard_map/all_to_all | solution.py:230
  119.1 12.8 %all_to_all.37.b0 = bf16[4,32,1920]{2,1,0:T(8,128)(2,1)S(1)} all-to-all(bf16[4,32,1920]{2,1,0:T(8,128)(2,1)S(1)} %broadcast_in_dim.25), channel_id=1, replica_groups=mesh['x'=4,'y'=8,'z'=8,'c'=2] {'x'}, dimensions={0} | all-to-all | bytes 983040 | tf_op jit(solution)/shard_map/all_to_all | solution.py:220
  131.9 1.9 collective-permute-start.3
  133.8 7.6 %all-gather.4.cloned.1.call-done = bf16[8,32,2304]{2,1,0:T(8,128)(2,1)} async-done(((bf16[1,32,2304]{2,1,0:T(8,128)(2,1)}), bf16[8,32,2304]{2,1,0:T(8,128)(2,1)}) %all-gather.4.cloned.1.call-update) | async-done | bytes 1179664 | tf_op jit(solution)/shard_map/all_gather | solution.py:236
  141.4 2.4 %collective-permute-start.1 = (bf16[256,2304]{1,0:T(8,128)(2,1)}, bf16[256,2304]{1,0:T(8,128)(2,1)S(1)}, u32[]{:S(2)}, u32[]{:S(2)}) collective-permute-start(bf16[256,2304]{1,0:T(8,128)(2,1)} %bitcast.17), channel_id=1, source_target_pairs={{0,128},{128,256},{256,384},{384,0},{1,129},{129,257},{257,385},{3... | collective-permute-start | bytes 3538952 | tf_op jit(solution)/shard_map/ppermute | solution.py:224
  143.8 3.6 %collective-permute-start.2 = (bf16[256,2304]{1,0:T(8,128)(2,1)}, bf16[256,2304]{1,0:T(8,128)(2,1)S(1)}, u32[]{:S(2)}, u32[]{:S(2)}) collective-permute-start(bf16[256,2304]{1,0:T(8,128)(2,1)} %bitcast.18), channel_id=1, source_target_pairs={{0,384},{128,0},{256,128},{384,256},{1,385},{129,1},{257,129},{385... | collective-permute-start | bytes 3538952 | tf_op jit(solution)/shard_map/ppermute | solution.py:224
  147.4 3.7 %collective-permute-start.5 = (bf16[4,32,1920]{2,1,0:T(8,128)(2,1)S(1)}, bf16[4,32,1920]{2,1,0:T(8,128)(2,1)S(1)}, u32[]{:S(2)}, u32[]{:S(2)}) collective-permute-start(bf16[4,32,1920]{2,1,0:T(8,128)(2,1)S(1)} %all_to_all.37.b0), channel_id=1, source_target_pairs={{0,112},{16,0},{32,16},{48,32},{64,48},{80,64},{96,80},{112,96},{1... | collective-permute-start | bytes 1474568 | tf_op jit(solution)/shard_map/ppermute | solution.py:224
  151.1 2.2 %collective-permute-start.4 = (bf16[4,32,1920]{2,1,0:T(8,128)(2,1)S(1)}, bf16[4,32,1920]{2,1,0:T(8,128)(2,1)S(1)}, u32[]{:S(2)}, u32[]{:S(2)}) collective-permute-start(bf16[4,32,1920]{2,1,0:T(8,128)(2,1)S(1)} %collective-permute-done.3.b1), channel_id=1, source_target_pairs={{0,16},{16,32},{32,48},{48,64},{64,80},{80,96},{96,112},{112,0},{1... | collective-permute-start | bytes 1474568 | tf_op jit(solution)/shard_map/ppermute | solution.py:224
  153.3 6.5 %collective-permute-done.5.b7 = bf16[4,32,1920]{2,1,0:T(8,128)(2,1)S(1)} collective-permute-done((bf16[4,32,1920]{2,1,0:T(8,128)(2,1)S(1)}, bf16[4,32,1920]{2,1,0:T(8,128)(2,1)S(1)}, u32[]{:S(2)}, u32[]{:S(2)}) %collective-permute-start.5) | collective-permute-done | bytes 491552 | tf_op jit(solution)/shard_map/ppermute | solution.py:224
  159.8 3.2 %collective-permute-start.6 = (bf16[4,32,1920]{2,1,0:T(8,128)(2,1)S(1)}, bf16[4,32,1920]{2,1,0:T(8,128)(2,1)S(1)}, u32[]{:S(2)}, u32[]{:S(2)}) collective-permute-start(bf16[4,32,1920]{2,1,0:T(8,128)(2,1)S(1)} %collective-permute-done.5.b7), channel_id=1, source_target_pairs={{0,112},{16,0},{32,16},{48,32},{64,48},{80,64},{96,80},{112,96},{1... | collective-permute-start | bytes 1474568 | tf_op jit(solution)/shard_map/ppermute | solution.py:224
  163.0 0.8 collective-permute-done.4.b2
  163.8 1.9 collective-permute-start.9
  165.7 1.9 collective-permute-done.1.a1
  167.6 2.8 %collective-permute-start.7 = (bf16[128,2304]{1,0:T(8,128)(2,1)S(1)}, bf16[128,2304]{1,0:T(8,128)(2,1)S(1)}, u32[]{:S(2)}, u32[]{:S(2)}) collective-permute-start(bf16[128,2304]{1,0:T(8,128)(2,1)S(1)} %slice.8), channel_id=1, source_target_pairs={{0,128},{128,256},{256,384},{384,0},{1,129},{129,257},{257,385},{3... | collective-permute-start | bytes 1769480 | tf_op jit(solution)/shard_map/ppermute | solution.py:224
  170.5 3.1 %collective-permute-start.8 = (bf16[128,2304]{1,0:T(8,128)(2,1)S(1)}, bf16[128,2304]{1,0:T(8,128)(2,1)S(1)}, u32[]{:S(2)}, u32[]{:S(2)}) collective-permute-start(bf16[128,2304]{1,0:T(8,128)(2,1)S(1)} %slice.9), channel_id=1, source_target_pairs={{0,384},{128,0},{256,128},{384,256},{1,385},{129,1},{257,129},{385... | collective-permute-start | bytes 1769480 | tf_op jit(solution)/shard_map/ppermute | solution.py:224
  173.6 3.4 %collective-permute-start.11 = (bf16[4,32,1920]{2,1,0:T(8,128)(2,1)S(1)}, bf16[4,32,1920]{2,1,0:T(8,128)(2,1)S(1)}, u32[]{:S(2)}, u32[]{:S(2)}) collective-permute-start(bf16[4,32,1920]{2,1,0:T(8,128)(2,1)S(1)} %collective-permute-done.6.b6), channel_id=1, source_target_pairs={{0,112},{16,0},{32,16},{48,32},{64,48},{80,64},{96,80},{112,96},{1... | collective-permute-start | bytes 1474568 | tf_op jit(solution)/shard_map/ppermute | solution.py:224
  176.9 2.5 %collective-permute-start.10 = (bf16[4,32,1920]{2,1,0:T(8,128)(2,1)S(1)}, bf16[4,32,1920]{2,1,0:T(8,128)(2,1)S(1)}, u32[]{:S(2)}, u32[]{:S(2)}) collective-permute-start(bf16[4,32,1920]{2,1,0:T(8,128)(2,1)S(1)} %collective-permute-done.9.b3), channel_id=1, source_target_pairs={{0,16},{16,32},{32,48},{48,64},{64,80},{80,96},{96,112},{112,0},{1... | collective-permute-start | bytes 1474568 | tf_op jit(solution)/shard_map/ppermute | solution.py:224
  179.4 0.1 pad_add_fusion.place_ref
  179.5 2.2 %copy-done.1 = bf16[4096,512]{1,0:T(8,128)(2,1)S(1)} copy-done((bf16[4096,512]{1,0:T(8,128)(2,1)S(1)}, bf16[4096,512]{1,0:T(8,128)(2,1)}, u32[]{:S(2)}) %copy-start.1) | copy-done | bytes 4194328
  181.7 4.0 %shard_map.142.p_ref = f32[4,256,512]{2,1,0:T(8,128)S(1)} custom-call(s32[2]{0:T(128)S(1)} %pad_add_fusion.place_ref, bf16[256,2304]{1,0:T(8,128)(2,1)S(1)} %bitcast.19, bf16[256,2304]{1,0:T(8,128)(2,1)S(1)} %collective-permute-done.1.a1, bf16[256,2304]{1,0:T(8,128)(2,1)S(1)} %collective-permute-done.2.a3, bf16[4,32,1920]{2,1,0:T(8,128)(2,1)S(1)} %all_to_all.37.b0, ...), custom_call_target="tpu_custom_call" | custom-call | flops 2863311616 | bytes 8388608 | tf_op jit(solution)/shard_map/pallas_call | solution.py:372
  185.7 3.2 %collective-permute-done.10.b4 = bf16[4,32,1920]{2,1,0:T(8,128)(2,1)S(1)} collective-permute-done((bf16[4,32,1920]{2,1,0:T(8,128)(2,1)S(1)}, bf16[4,32,1920]{2,1,0:T(8,128)(2,1)S(1)}, u32[]{:S(2)}, u32[]{:S(2)}) %collective-permute-start.10) | collective-permute-done | bytes 491552 | tf_op jit(solution)/shard_map/ppermute | solution.py:224
  188.9 3.9 %shard_map.143 = bf16[224,1024]{1,0:T(8,128)(2,1)} custom-call(s32[2]{0:T(128)S(1)} %pad_add_fusion.place_ref, f32[4,256,512]{2,1,0:T(8,128)S(1)} %shard_map.142.p_ref, bf16[256,2304]{1,0:T(8,128)(2,1)S(1)} %bitcast.20, bf16[256,2304]{1,0:T(8,128)(2,1)S(1)} %collective-permute-done.1.a1, bf16[128,2304]{1,0:T(8,128)(2,1)S(1)} %collective-permute-done.7.a20, ...), custom_call_target="tpu_custom_call" | custom-call | flops 1431655808 | bytes 8388608 | tf_op jit(solution)/shard_map/pallas_call | solution.py:383
  (45 shorter events, 0.3 us)
Async XLA Ops:
  6.5 34.1 %copy-start.10 = (bf16[128,512]{1,0:T(8,128)(2,1)S(1)}, bf16[128,512]{1,0:T(8,128)(2,1)}, u32[]{:S(2)}) copy-start(bf16[128,512]{1,0:T(8,128)(2,1)} %x_ref.3) | copy-start | bytes 393220
  6.5 34.1 %copy-start.11 = (bf16[128,512]{1,0:T(8,128)(2,1)S(1)}, bf16[128,512]{1,0:T(8,128)(2,1)}, u32[]{:S(2)}) copy-start(bf16[128,512]{1,0:T(8,128)(2,1)} %d_ref.3) | copy-start | bytes 393220
  6.5 24.5 %copy-start.7 = (f32[512,16]{0,1:T(8,128)S(1)}, f32[512,16]{0,1:T(8,128)}, u32[]{:S(2)}) copy-start(f32[512,16]{0,1:T(8,128)} %param.17) | copy-start | bytes 98308
  6.5 34.1 %copy-start.13 = (f32[128,16]{0,1:T(8,128)S(1)}, f32[128,16]{0,1:T(8,128)}, u32[]{:S(2)}) copy-start(f32[128,16]{0,1:T(8,128)} %param.18) | copy-start | bytes 24580
  6.5 34.1 %copy-start.12 = (bf16[128,512]{1,0:T(8,128)(2,1)S(1)}, bf16[128,512]{1,0:T(8,128)(2,1)}, u32[]{:S(2)}) copy-start(bf16[128,512]{1,0:T(8,128)(2,1)} %z_ref.1) | copy-start | bytes 393220
  6.5 34.1 %copy-start.14 = (f32[128,16]{0,1:T(8,128)S(1)}, f32[128,16]{0,1:T(8,128)}, u32[]{:S(2)}) copy-start(f32[128,16]{0,1:T(8,128)} %param.19) | copy-start | bytes 24580
  6.6 34.1 %copy-start.15 = (f32[512]{0:T(512)S(1)}, f32[512]{0:T(512)}, u32[]{:S(2)}) copy-start(f32[512]{0:T(512)} %param.20) | copy-start | bytes 6148
  6.6 49.1 %all-gather.6.cloned.1.call-start = ((), (), s32[]{:S(2)}) async-start(), calls=%async_computation.8 | async-start | bytes 1179648 | tf_op jit(solution)/shard_map/all_gather | solution.py:276
  10.7 20.4 %all-to-all-start = ((f32[8,16,640]{2,1,0:T(8,128)}), f32[8,16,640]{2,1,0:T(8,128)S(1)}, u32[]{:S(2)}, u32[]{:S(2)}) async-start(f32[8,16,640]{2,1,0:T(8,128)} %shard_map.136), calls=%async_computation | async-start | bytes 655360 | tf_op jit(solution)/shard_map/all_to_all | solution.py:220
  31.8 8.9 %all-to-all-start.1 = ((f32[4,16,640]{2,1,0:T(8,128)}), f32[4,16,640]{2,1,0:T(8,128)S(1)}, u32[]{:S(2)}, u32[]{:S(2)}) async-start(f32[4,16,640]{2,1,0:T(8,128)} %get-tuple-element.17), calls=%async_computation.1 | async-start | bytes 327680 | tf_op jit(solution)/shard_map/all_to_all | solution.py:220
  44.2 11.5 %all-to-all-start.2 = ((bf16[4,128,512]{2,1,0:T(8,128)(2,1)}), bf16[4,128,512]{2,1,0:T(8,128)(2,1)S(1)}, u32[]{:S(2)}, u32[]{:S(2)}) async-start(bf16[4,128,512]{2,1,0:T(8,128)(2,1)} %shard_map.138), calls=%async_computation.2 | async-start | bytes 1048576 | tf_op jit(solution)/shard_map/all_to_all | solution.py:220
  55.7 1.2 copy-start.9
  57.7 19.6 %copy-start.17 = (bf16[8,2]{0,1:T(2,128)(2,1)S(1)}, bf16[8,2]{0,1:T(2,128)(2,1)}, u32[]{:S(2)}) copy-start(bf16[8,2]{0,1:T(2,128)(2,1)} %param.25) | copy-start | bytes 100
  57.7 19.7 %copy-start.16 = (s32[8,2]{0,1:T(2,128)S(1)}, s32[8,2]{0,1:T(2,128)}, u32[]{:S(2)}) copy-start(s32[8,2]{0,1:T(2,128)} %param.24) | copy-start | bytes 196
  57.7 20.7 %copy-start.4 = (bf16[1,224,4096]{2,1,0:T(8,128)(2,1)S(1)}, bf16[1,224,4096]{2,1,0:T(8,128)(2,1)}, u32[]{:S(2)}) copy-start(bf16[1,224,4096]{2,1,0:T(8,128)(2,1)} %param.26) | copy-start | bytes 5505028
  57.7 3.9 %collective-permute-start = (bf16[4,8,8,1024]{3,2,1,0:T(8,128)(2,1)S(1)}, bf16[4,8,8,1024]{3,2,1,0:T(8,128)(2,1)S(1)}, u32[]{:S(2)}, u32[]{:S(2)}) collective-permute-start(bf16[4,8,8,1024]{3,2,1,0:T(8,128)(2,1)S(1)} %get-tuple-element.19), channel_id=1, source_target_pairs={{0,1},{1,0},{2,3},{3,2},{4,5},{5,4},{6,7},{7,6},{8,9},{9,8},{10,11... | collective-permute-start | bytes 1572872 | tf_op jit(solution)/shard_map/ppermute | solution.py:224
  62.6 30.2 %all-to-all-start.3 = ((bf16[32,8,1024]{2,1,0:T(8,128)(2,1)}), bf16[32,8,1024]{2,1,0:T(8,128)(2,1)S(1)}, u32[]{:S(2)}, u32[]{:S(2)}) async-start(bf16[32,8,1024]{2,1,0:T(8,128)(2,1)} %bitcast.8), calls=%async_computation.3 | async-start | bytes 1048576 | tf_op jit(solution)/shard_map/all_to_all | solution.py:336
  77.3 64.2 %all-gather.4.cloned.1.call-start = ((), (), s32[]{:S(2)}) async-start(), calls=%async_computation.7 | async-start | bytes 1327104 | tf_op jit(solution)/shard_map/all_gather | solution.py:236
  78.4 1.5 copy-start.5
  79.9 12.8 %copy-start.6 = (bf16[8,4096]{1,0:T(8,128)(2,1)S(1)}, bf16[8,4096]{1,0:T(8,128)(2,1)}, u32[]{:S(2)}) copy-start(bf16[8,4096]{1,0:T(8,128)(2,1)} %stream_ref.1) | copy-start | bytes 196612
  79.9 12.8 %copy-start.8 = (f32[4096]{0:T(1024)S(1)}, f32[4096]{0:T(1024)}, u32[]{:S(2)}) copy-start(f32[4096]{0:T(1024)} %param.23) | copy-start | bytes 49156
  82.2 2.0 copy-start
  131.9 19.2 %collective-permute-start.3 = (bf16[4,32,1920]{2,1,0:T(8,128)(2,1)S(1)}, bf16[4,32,1920]{2,1,0:T(8,128)(2,1)S(1)}, u32[]{:S(2)}, u32[]{:S(2)}) collective-permute-start(bf16[4,32,1920]{2,1,0:T(8,128)(2,1)S(1)} %all_to_all.37.b0), channel_id=1, source_target_pairs={{0,16},{16,32},{32,48},{48,64},{64,80},{80,96},{96,112},{112,0},{1... | collective-permute-start | bytes 1474568 | tf_op jit(solution)/shard_map/ppermute | solution.py:224
  141.4 38.1 %copy-start.3 = (bf16[8,32,2304]{2,1,0:T(8,128)(2,1)S(1)}, bf16[8,32,2304]{2,1,0:T(8,128)(2,1)}, u32[]{:S(2)}) copy-start(bf16[8,32,2304]{2,1,0:T(8,128)(2,1)} %all-gather.4.cloned.1.call-done) | copy-start | bytes 3538948
  141.4 26.2 %collective-permute-start.1 = (bf16[256,2304]{1,0:T(8,128)(2,1)}, bf16[256,2304]{1,0:T(8,128)(2,1)S(1)}, u32[]{:S(2)}, u32[]{:S(2)}) collective-permute-start(bf16[256,2304]{1,0:T(8,128)(2,1)} %bitcast.17), channel_id=1, source_target_pairs={{0,128},{128,256},{256,384},{384,0},{1,129},{129,257},{257,385},{3... | collective-permute-start | bytes 3538952 | tf_op jit(solution)/shard_map/ppermute | solution.py:224
  143.8 26.6 %collective-permute-start.2 = (bf16[256,2304]{1,0:T(8,128)(2,1)}, bf16[256,2304]{1,0:T(8,128)(2,1)S(1)}, u32[]{:S(2)}, u32[]{:S(2)}) collective-permute-start(bf16[256,2304]{1,0:T(8,128)(2,1)} %bitcast.18), channel_id=1, source_target_pairs={{0,384},{128,0},{256,128},{384,256},{1,385},{129,1},{257,129},{385... | collective-permute-start | bytes 3538952 | tf_op jit(solution)/shard_map/ppermute | solution.py:224
  147.4 12.4 %collective-permute-start.5 = (bf16[4,32,1920]{2,1,0:T(8,128)(2,1)S(1)}, bf16[4,32,1920]{2,1,0:T(8,128)(2,1)S(1)}, u32[]{:S(2)}, u32[]{:S(2)}) collective-permute-start(bf16[4,32,1920]{2,1,0:T(8,128)(2,1)S(1)} %all_to_all.37.b0), channel_id=1, source_target_pairs={{0,112},{16,0},{32,16},{48,32},{64,48},{80,64},{96,80},{112,96},{1... | collective-permute-start | bytes 1474568 | tf_op jit(solution)/shard_map/ppermute | solution.py:224
  151.1 12.7 %collective-permute-start.4 = (bf16[4,32,1920]{2,1,0:T(8,128)(2,1)S(1)}, bf16[4,32,1920]{2,1,0:T(8,128)(2,1)S(1)}, u32[]{:S(2)}, u32[]{:S(2)}) collective-permute-start(bf16[4,32,1920]{2,1,0:T(8,128)(2,1)S(1)} %collective-permute-done.3.b1), channel_id=1, source_target_pairs={{0,16},{16,32},{32,48},{48,64},{64,80},{80,96},{96,112},{112,0},{1... | collective-permute-start | bytes 1474568 | tf_op jit(solution)/shard_map/ppermute | solution.py:224
  159.8 13.8 %collective-permute-start.6 = (bf16[4,32,1920]{2,1,0:T(8,128)(2,1)S(1)}, bf16[4,32,1920]{2,1,0:T(8,128)(2,1)S(1)}, u32[]{:S(2)}, u32[]{:S(2)}) collective-permute-start(bf16[4,32,1920]{2,1,0:T(8,128)(2,1)S(1)} %collective-permute-done.5.b7), channel_id=1, source_target_pairs={{0,112},{16,0},{32,16},{48,32},{64,48},{80,64},{96,80},{112,96},{1... | collective-permute-start | bytes 1474568 | tf_op jit(solution)/shard_map/ppermute | solution.py:224
  163.8 13.1 %collective-permute-start.9 = (bf16[4,32,1920]{2,1,0:T(8,128)(2,1)S(1)}, bf16[4,32,1920]{2,1,0:T(8,128)(2,1)S(1)}, u32[]{:S(2)}, u32[]{:S(2)}) collective-permute-start(bf16[4,32,1920]{2,1,0:T(8,128)(2,1)S(1)} %collective-permute-done.4.b2), channel_id=1, source_target_pairs={{0,16},{16,32},{32,48},{48,64},{64,80},{80,96},{96,112},{112,0},{1... | collective-permute-start | bytes 1474568 | tf_op jit(solution)/shard_map/ppermute | solution.py:224
  167.6 21.2 %collective-permute-start.7 = (bf16[128,2304]{1,0:T(8,128)(2,1)S(1)}, bf16[128,2304]{1,0:T(8,128)(2,1)S(1)}, u32[]{:S(2)}, u32[]{:S(2)}) collective-permute-start(bf16[128,2304]{1,0:T(8,128)(2,1)S(1)} %slice.8), channel_id=1, source_target_pairs={{0,128},{128,256},{256,384},{384,0},{1,129},{129,257},{257,385},{3... | collective-permute-start | bytes 1769480 | tf_op jit(solution)/shard_map/ppermute | solution.py:224
  170.5 18.4 %collective-permute-start.8 = (bf16[128,2304]{1,0:T(8,128)(2,1)S(1)}, bf16[128,2304]{1,0:T(8,128)(2,1)S(1)}, u32[]{:S(2)}, u32[]{:S(2)}) collective-permute-start(bf16[128,2304]{1,0:T(8,128)(2,1)S(1)} %slice.9), channel_id=1, source_target_pairs={{0,384},{128,0},{256,128},{384,256},{1,385},{129,1},{257,129},{385... | collective-permute-start | bytes 1769480 | tf_op jit(solution)/shard_map/ppermute | solution.py:224
  173.6 12.1 %collective-permute-start.11 = (bf16[4,32,1920]{2,1,0:T(8,128)(2,1)S(1)}, bf16[4,32,1920]{2,1,0:T(8,128)(2,1)S(1)}, u32[]{:S(2)}, u32[]{:S(2)}) collective-permute-start(bf16[4,32,1920]{2,1,0:T(8,128)(2,1)S(1)} %collective-permute-done.6.b6), channel_id=1, source_target_pairs={{0,112},{16,0},{32,16},{48,32},{64,48},{80,64},{96,80},{112,96},{1... | collective-permute-start | bytes 1474568 | tf_op jit(solution)/shard_map/ppermute | solution.py:224
  176.9 11.9 %collective-permute-start.10 = (bf16[4,32,1920]{2,1,0:T(8,128)(2,1)S(1)}, bf16[4,32,1920]{2,1,0:T(8,128)(2,1)S(1)}, u32[]{:S(2)}, u32[]{:S(2)}) collective-permute-start(bf16[4,32,1920]{2,1,0:T(8,128)(2,1)S(1)} %collective-permute-done.9.b3), channel_id=1, source_target_pairs={{0,16},{16,32},{32,48},{48,64},{64,80},{80,96},{96,112},{112,0},{1... | collective-permute-start | bytes 1474568 | tf_op jit(solution)/shard_map/ppermute | solution.py:224
  179.5 2.2 %copy-start.1 = (bf16[4096,512]{1,0:T(8,128)(2,1)S(1)}, bf16[4096,512]{1,0:T(8,128)(2,1)}, u32[]{:S(2)}) copy-start(bf16[4096,512]{1,0:T(8,128)(2,1)} %copy-done) | copy-start | bytes 12582916
  181.7 7.2 %copy-start.2 = (bf16[4096,512]{1,0:T(8,128)(2,1)S(1)}, bf16[4096,512]{1,0:T(8,128)(2,1)}, u32[]{:S(2)}) copy-start(bf16[4096,512]{1,0:T(8,128)(2,1)} %copy-done) | copy-start | bytes 12582916
Sparse Core Ops, SparseCore 0:
  9.5 45.4 all-gather.5
  107.5 33.9 all-gather.3

commit v6 on v5

--- a/solution.py
+++ b/solution.py
@@ -352,7 +352,7 @@
     gate = jnp.sum(pairs * gate_weights.astype(jnp.float32)[:, :, None, None], axis=(0, 1)).reshape(slots, 1)
     gate = jnp.pad(gate, ((0, 0), (0, PAD - 1))).astype(jnp.bfloat16)
 
-    wide = features * 17 // 32
+    wide = features * 18 // 32
     a_rows, b_rows = pl.pallas_call(
         slots_kernel,
         out_shape=[

time: 202 us -> 209 us (1.035)
  blocking collectives: 37.4 us -> 24.7 us
  starting transfers between devices: 64.7 us -> 74.5 us
  waiting for transfers between devices: 54.6 us -> 64 us
    all_to_all x1 -> x0, blocking collectives: 12.8 us -> none  [spread(): return lax.all_to_all(copies, axis, split_axis=0, concat_axis=0, tiled=True)]
    all_gather x1, waiting for transfers between devices: 7.63 us -> 15.8 us  [everywhere(): a0 = lax.all_gather(a, 'y').reshape(NY * slots, wide)]
    all_to_all x3 -> x4, starting transfers between devices: 17.4 us -> 22.9 us  [spread(): return lax.all_to_all(copies, axis, split_axis=0, concat_axis=0, tiled=True)]
    ppermute x12, starting transfers between devices: 32.6 us -> 36.8 us  [ring(): return lax.ppermute(a, axis, [(i, (i + hop) % size) for i in range(size)])]
    all_to_all x3 -> x4, waiting for transfers between devices: 23.4 us -> 23.4 us  [spread(): return lax.all_to_all(copies, axis, split_axis=0, concat_axis=0, tiled=True)]
  transfers between devices with their start and end apart: 18 -> 19, of which waited for: 10 -> 10; matrix products, arithmetic and copies ran while one was open for 1% -> 1% of each run, Pallas kernels for 7% -> 7%
where the time goes in v6:
time: 209 us; the launch traced here: 206 us
  starting transfers between devices  74.5 us (36%)
  waiting for transfers between devices  64 us (31%)
  blocking collectives  24.7 us (12%)
  Pallas kernels  18.7 us (9%)
  between operations  13.8 us (7%)
  local copies, waits for them, and re-layouts  9.31 us (4%)
    ppermute x12, starting transfers between devices, ring(): return lax.ppermute(a, axis, [(i, (i + hop) % size) for i in range(size)])  36.8 us
    all_to_all x2, blocking collectives, dispatched(): lax.all_to_all(rows, EXP, split_axis=0, concat_axis=0, tiled=True)  24.7 us
    all_to_all x4, waiting for transfers between devices, spread(): return lax.all_to_all(copies, axis, split_axis=0, concat_axis=0, tiled=True)  23.4 us
    all_to_all x4, starting transfers between devices, spread(): return lax.all_to_all(copies, axis, split_axis=0, concat_axis=0, tiled=True)  22.9 us
    all_gather x1, waiting for transfers between devices, everywhere(): a0 = lax.all_gather(a, 'y').reshape(NY * slots, wide)  15.8 us
    ppermute x12, waiting for transfers between devices, ring(): return lax.ppermute(a, axis, [(i, (i + hop) % size) for i in range(size)])  15.4 us
    all_to_all x1, starting transfers between devices, body(): lax.all_to_all(both, ('x', 'z'), split_axis=0, concat_axis=0, tiled=True)  14.7 us
    all_to_all x1, waiting for transfers between devices, body(): lax.all_to_all(both, ('x', 'z'), split_axis=0, concat_axis=0, tiled=True)  8.62 us
  transfers between devices with their start and end apart: 19, of which 10 were waited for; matrix products, arithmetic and copies ran while one was open for 1% of the time, Pallas kernels for 7%

profile of v6, /device:TPU:6, one launch (start us, length us, event | category | flops | bytes accessed | tf_op | source)
XLA Modules:
  0.0 206.3 jit_solution(16207153646590532091)
XLA Ops:
  6.6 0.0 all-gather.6.cloned.1.call-start
  6.6 0.7 all-gather.6.cloned.1.call-update
  7.3 3.4 %shard_map.136 = f32[8,16,640]{2,1,0:T(8,128)} custom-call(bf16[128,512]{1,0:T(8,128)(2,1)} %x_ref.3, bf16[128,512]{1,0:T(8,128)(2,1)} %d_ref.3, f32[16,512]{1,0:T(8,128)} %bitcast.24, f32[16,128]{1,0:T(8,128)} %bitcast.29), custom_call_target="tpu_custom_call" | custom-call | flops 4194304 | bytes 262144 | tf_op jit(solution)/shard_map/pallas_call | solution.py:282
  10.7 7.1 %all-to-all-start = ((f32[8,16,640]{2,1,0:T(8,128)}), f32[8,16,640]{2,1,0:T(8,128)S(1)}, u32[]{:S(2)}, u32[]{:S(2)}) async-start(f32[8,16,640]{2,1,0:T(8,128)} %shard_map.136), calls=%async_computation | async-start | bytes 655360 | tf_op jit(solution)/shard_map/all_to_all | solution.py:220
  17.8 13.3 %all-to-all-done.parts_ref = f32[8,16,640]{2,1,0:T(8,128)S(1)} async-done(((f32[8,16,640]{2,1,0:T(8,128)}), f32[8,16,640]{2,1,0:T(8,128)S(1)}, u32[]{:S(2)}, u32[]{:S(2)}) %all-to-all-start) | async-done | bytes 327712 | tf_op jit(solution)/shard_map/all_to_all | solution.py:220
  31.1 0.7 shard_map.137
  31.8 4.8 %all-to-all-start.1 = ((f32[4,16,640]{2,1,0:T(8,128)}), f32[4,16,640]{2,1,0:T(8,128)S(1)}, u32[]{:S(2)}, u32[]{:S(2)}) async-start(f32[4,16,640]{2,1,0:T(8,128)} %get-tuple-element.17), calls=%async_computation.1 | async-start | bytes 327680 | tf_op jit(solution)/shard_map/all_to_all | solution.py:220
  36.6 4.1 %all-to-all-done.1.rows_ref = f32[4,16,640]{2,1,0:T(8,128)S(1)} async-done(((f32[4,16,640]{2,1,0:T(8,128)}), f32[4,16,640]{2,1,0:T(8,128)S(1)}, u32[]{:S(2)}, u32[]{:S(2)}) %all-to-all-start.1) | async-done | bytes 163872 | tf_op jit(solution)/shard_map/all_to_all | solution.py:220
  40.7 3.5 %shard_map.138 = bf16[4,128,512]{2,1,0:T(8,128)(2,1)} custom-call(s32[1]{0:T(128)} %bitcast.place_ref, bf16[128,512]{1,0:T(8,128)(2,1)S(1)} %copy-done.10, bf16[128,512]{1,0:T(8,128)(2,1)S(1)} %copy-done.11, bf16[128,512]{1,0:T(8,128)(2,1)S(1)} %copy-done.12, f32[16,512]{1,0:T(8,128)S(1)} %bitcast.26, f32[16,128]{1,0:T(8,128)S(1)} %bitcast.30, ...), custom_call_target="tpu_custom_call" | custom-call | flops 6291456 | bytes 524288 | tf_op jit(solution)/shard_map/pallas_call | solution.py:301
  44.2 5.5 %all-to-all-start.2 = ((bf16[4,128,512]{2,1,0:T(8,128)(2,1)}), bf16[4,128,512]{2,1,0:T(8,128)(2,1)S(1)}, u32[]{:S(2)}, u32[]{:S(2)}) async-start(bf16[4,128,512]{2,1,0:T(8,128)(2,1)} %shard_map.138), calls=%async_computation.2 | async-start | bytes 1048576 | tf_op jit(solution)/shard_map/all_to_all | solution.py:220
  49.7 6.0 %all-to-all-done.2.g_ref = bf16[4,128,512]{2,1,0:T(8,128)(2,1)S(1)} async-done(((bf16[4,128,512]{2,1,0:T(8,128)(2,1)}), bf16[4,128,512]{2,1,0:T(8,128)(2,1)S(1)}, u32[]{:S(2)}, u32[]{:S(2)}) %all-to-all-start.2) | async-done | bytes 524320 | tf_op jit(solution)/shard_map/all_to_all | solution.py:220
  55.7 1.2 copy-done.9
  56.9 0.7 shard_map.139
  57.7 0.0 copy-start.16
  57.7 0.0 copy-start.17
  57.7 0.0 copy-start.4
  57.7 2.1 collective-permute-start
  59.8 1.9 collective-permute-done
  61.6 1.0 add_convert_fusion
  62.6 14.7 %all-to-all-start.3 = ((bf16[32,8,1024]{2,1,0:T(8,128)(2,1)}), bf16[32,8,1024]{2,1,0:T(8,128)(2,1)S(1)}, u32[]{:S(2)}, u32[]{:S(2)}) async-start(bf16[32,8,1024]{2,1,0:T(8,128)(2,1)} %bitcast.8), calls=%async_computation.3 | async-start | bytes 1048576 | tf_op jit(solution)/shard_map/all_to_all | solution.py:336
  77.3 0.0 all-gather.4.cloned.1.call-start
  77.3 0.1 copy.27
  77.4 0.1 eq.48
  77.5 0.1 fusion.1
  77.6 0.2 select_reduce_fusion
  77.8 0.1 eq.52
  77.9 0.1 copy.28
  78.0 0.1 convert_convert_fusion
  78.0 0.1 fusion
  78.1 0.1 copy.30
  78.2 0.1 reshape.45
  78.3 0.1 copy.29
  78.4 1.5 copy-done.5
  79.9 2.2 %shard_map.140.w_ref = bf16[4096,512]{1,0:T(8,128)(2,1)S(1)} custom-call(bf16[224,4096]{1,0:T(8,128)(2,1)S(1)} %bitcast.21, bf16[224,4096]{1,0:T(8,128)(2,1)S(1)} %bitcast.22), custom_call_target="tpu_custom_call" | custom-call | flops 16777216 | bytes 16777216 | tf_op jit(solution)/shard_map/pallas_call | solution.py:328
  82.2 2.0 copy-done
  84.1 8.6 %all-to-all-done.3.got_ref = bf16[32,8,1024]{2,1,0:T(8,128)(2,1)S(1)} async-done(((bf16[32,8,1024]{2,1,0:T(8,128)(2,1)}), bf16[32,8,1024]{2,1,0:T(8,128)(2,1)S(1)}, u32[]{:S(2)}, u32[]{:S(2)}) %all-to-all-start.3) | async-done | bytes 524320 | tf_op jit(solution)/shard_map/all_to_all | solution.py:336
  92.8 0.7 shard_map.141
  93.5 0.1 reshape.41
  93.6 13.2 %all_to_all.35 = bf16[16,2,2432]{2,1,0:T(2,128)(2,1)S(1)} all-to-all(bf16[16,2,2432]{2,1,0:T(2,128)(2,1)S(1)} %reshape.41), channel_id=1, replica_groups=mesh['x'=4,'y'=8,'z'=8,'c'=2] {'z','c'}, dimensions={0} | all-to-all | bytes 311296 | tf_op jit(solution)/shard_map/all_to_all | solution.py:230
  106.8 0.7 all_gather_reshape.3
  107.5 0.0 all-gather.4.cloned.1.call-update
  107.6 11.5 %all_to_all.36 = bf16[16,2,1792]{2,1,0:T(2,128)(2,1)S(1)} all-to-all(bf16[16,2,1792]{2,1,0:T(2,128)(2,1)S(1)} %reshape.43), channel_id=1, replica_groups=mesh['x'=4,'y'=8,'z'=8,'c'=2] {'z','c'}, dimensions={0} | all-to-all | bytes 229376 | tf_op jit(solution)/shard_map/all_to_all | solution.py:230
  119.1 0.8 broadcast_in_dim.25
  119.9 5.6 %all-to-all-start.6 = ((bf16[4,32,1792]{2,1,0:T(8,128)(2,1)}), bf16[4,32,1792]{2,1,0:T(8,128)(2,1)S(1)}, u32[]{:S(2)}, u32[]{:S(2)}) async-start(bf16[4,32,1792]{2,1,0:T(8,128)(2,1)} %broadcast_in_dim.25), calls=%async_computation.6 | async-start | bytes 917504 | tf_op jit(solution)/shard_map/all_to_all | solution.py:220
  125.4 15.8 %all-gather.4.cloned.1.call-done = bf16[8,32,2432]{2,1,0:T(8,128)(2,1)} async-done(((bf16[1,32,2432]{2,1,0:T(8,128)(2,1)}), bf16[8,32,2432]{2,1,0:T(8,128)(2,1)}) %all-gather.4.cloned.1.call-update) | async-done | bytes 1245200 | tf_op jit(solution)/shard_map/all_gather | solution.py:236
  141.3 2.6 %collective-permute-start.1 = (bf16[256,2432]{1,0:T(8,128)(2,1)}, bf16[256,2432]{1,0:T(8,128)(2,1)S(1)}, u32[]{:S(2)}, u32[]{:S(2)}) collective-permute-start(bf16[256,2432]{1,0:T(8,128)(2,1)} %bitcast.17), channel_id=1, source_target_pairs={{0,128},{128,256},{256,384},{384,0},{1,129},{129,257},{257,385},{3... | collective-permute-start | bytes 3735560 | tf_op jit(solution)/shard_map/ppermute | solution.py:224
  143.8 3.3 %collective-permute-start.2 = (bf16[256,2432]{1,0:T(8,128)(2,1)}, bf16[256,2432]{1,0:T(8,128)(2,1)S(1)}, u32[]{:S(2)}, u32[]{:S(2)}) collective-permute-start(bf16[256,2432]{1,0:T(8,128)(2,1)} %bitcast.18), channel_id=1, source_target_pairs={{0,384},{128,0},{256,128},{384,256},{1,385},{129,1},{257,129},{385... | collective-permute-start | bytes 3735560 | tf_op jit(solution)/shard_map/ppermute | solution.py:224
  147.1 3.4 %collective-permute-start.3 = (bf16[4,32,1792]{2,1,0:T(8,128)(2,1)S(1)}, bf16[4,32,1792]{2,1,0:T(8,128)(2,1)S(1)}, u32[]{:S(2)}, u32[]{:S(2)}) collective-permute-start(bf16[4,32,1792]{2,1,0:T(8,128)(2,1)S(1)} %all-to-all-done.6.b0), channel_id=1, source_target_pairs={{0,16},{16,32},{32,48},{48,64},{64,80},{80,96},{96,112},{112,0},{1... | collective-permute-start | bytes 1376264 | tf_op jit(solution)/shard_map/ppermute | solution.py:224
  150.6 3.8 %collective-permute-start.5 = (bf16[4,32,1792]{2,1,0:T(8,128)(2,1)S(1)}, bf16[4,32,1792]{2,1,0:T(8,128)(2,1)S(1)}, u32[]{:S(2)}, u32[]{:S(2)}) collective-permute-start(bf16[4,32,1792]{2,1,0:T(8,128)(2,1)S(1)} %all-to-all-done.6.b0), channel_id=1, source_target_pairs={{0,112},{16,0},{32,16},{48,32},{64,48},{80,64},{96,80},{112,96},{1... | collective-permute-start | bytes 1376264 | tf_op jit(solution)/shard_map/ppermute | solution.py:224
  154.3 4.5 %collective-permute-done.3.b1 = bf16[4,32,1792]{2,1,0:T(8,128)(2,1)S(1)} collective-permute-done((bf16[4,32,1792]{2,1,0:T(8,128)(2,1)S(1)}, bf16[4,32,1792]{2,1,0:T(8,128)(2,1)S(1)}, u32[]{:S(2)}, u32[]{:S(2)}) %collective-permute-start.3) | collective-permute-done | bytes 458784 | tf_op jit(solution)/shard_map/ppermute | solution.py:224
  158.8 3.1 %collective-permute-start.4 = (bf16[4,32,1792]{2,1,0:T(8,128)(2,1)S(1)}, bf16[4,32,1792]{2,1,0:T(8,128)(2,1)S(1)}, u32[]{:S(2)}, u32[]{:S(2)}) collective-permute-start(bf16[4,32,1792]{2,1,0:T(8,128)(2,1)S(1)} %collective-permute-done.3.b1), channel_id=1, source_target_pairs={{0,16},{16,32},{32,48},{48,64},{64,80},{80,96},{96,112},{112,0},{1... | collective-permute-start | bytes 1376264 | tf_op jit(solution)/shard_map/ppermute | solution.py:224
  162.0 0.3 collective-permute-done.5.b7
  162.2 3.8 %collective-permute-start.6 = (bf16[4,32,1792]{2,1,0:T(8,128)(2,1)S(1)}, bf16[4,32,1792]{2,1,0:T(8,128)(2,1)S(1)}, u32[]{:S(2)}, u32[]{:S(2)}) collective-permute-start(bf16[4,32,1792]{2,1,0:T(8,128)(2,1)S(1)} %collective-permute-done.5.b7), channel_id=1, source_target_pairs={{0,112},{16,0},{32,16},{48,32},{64,48},{80,64},{96,80},{112,96},{1... | collective-permute-start | bytes 1376264 | tf_op jit(solution)/shard_map/ppermute | solution.py:224
  166.1 5.1 %collective-permute-done.4.b2 = bf16[4,32,1792]{2,1,0:T(8,128)(2,1)S(1)} collective-permute-done((bf16[4,32,1792]{2,1,0:T(8,128)(2,1)S(1)}, bf16[4,32,1792]{2,1,0:T(8,128)(2,1)S(1)}, u32[]{:S(2)}, u32[]{:S(2)}) %collective-permute-start.4) | collective-permute-done | bytes 458784 | tf_op jit(solution)/shard_map/ppermute | solution.py:224
  171.2 2.8 %collective-permute-start.9 = (bf16[4,32,1792]{2,1,0:T(8,128)(2,1)S(1)}, bf16[4,32,1792]{2,1,0:T(8,128)(2,1)S(1)}, u32[]{:S(2)}, u32[]{:S(2)}) collective-permute-start(bf16[4,32,1792]{2,1,0:T(8,128)(2,1)S(1)} %collective-permute-done.4.b2), channel_id=1, source_target_pairs={{0,16},{16,32},{32,48},{48,64},{64,80},{80,96},{96,112},{112,0},{1... | collective-permute-start | bytes 1376264 | tf_op jit(solution)/shard_map/ppermute | solution.py:224
  174.1 3.5 %collective-permute-start.7 = (bf16[128,2432]{1,0:T(8,128)(2,1)S(1)}, bf16[128,2432]{1,0:T(8,128)(2,1)S(1)}, u32[]{:S(2)}, u32[]{:S(2)}) collective-permute-start(bf16[128,2432]{1,0:T(8,128)(2,1)S(1)} %slice.8), channel_id=1, source_target_pairs={{0,128},{128,256},{256,384},{384,0},{1,129},{129,257},{257,385},{3... | collective-permute-start | bytes 1867784 | tf_op jit(solution)/shard_map/ppermute | solution.py:224
  177.7 2.3 %collective-permute-start.8 = (bf16[128,2432]{1,0:T(8,128)(2,1)S(1)}, bf16[128,2432]{1,0:T(8,128)(2,1)S(1)}, u32[]{:S(2)}, u32[]{:S(2)}) collective-permute-start(bf16[128,2432]{1,0:T(8,128)(2,1)S(1)} %slice.9), channel_id=1, source_target_pairs={{0,384},{128,0},{256,128},{384,256},{1,385},{129,1},{257,129},{385... | collective-permute-start | bytes 1867784 | tf_op jit(solution)/shard_map/ppermute | solution.py:224
  180.0 4.2 %collective-permute-start.11 = (bf16[4,32,1792]{2,1,0:T(8,128)(2,1)S(1)}, bf16[4,32,1792]{2,1,0:T(8,128)(2,1)S(1)}, u32[]{:S(2)}, u32[]{:S(2)}) collective-permute-start(bf16[4,32,1792]{2,1,0:T(8,128)(2,1)S(1)} %collective-permute-done.6.b6), channel_id=1, source_target_pairs={{0,112},{16,0},{32,16},{48,32},{64,48},{80,64},{96,80},{112,96},{1... | collective-permute-start | bytes 1376264 | tf_op jit(solution)/shard_map/ppermute | solution.py:224
  184.3 1.9 collective-permute-start.10
  186.2 0.1 pad_add_fusion.place_ref
  186.3 2.2 %copy-done.1 = bf16[4096,512]{1,0:T(8,128)(2,1)S(1)} copy-done((bf16[4096,512]{1,0:T(8,128)(2,1)S(1)}, bf16[4096,512]{1,0:T(8,128)(2,1)}, u32[]{:S(2)}) %copy-start.1) | copy-done | bytes 4194328
  188.5 3.7 %shard_map.142.p_ref = f32[4,256,512]{2,1,0:T(8,128)S(1)} custom-call(s32[2]{0:T(128)S(1)} %pad_add_fusion.place_ref, bf16[256,2432]{1,0:T(8,128)(2,1)S(1)} %bitcast.19, bf16[256,2432]{1,0:T(8,128)(2,1)S(1)} %collective-permute-done.1.a1, bf16[256,2432]{1,0:T(8,128)(2,1)S(1)} %collective-permute-done.2.a3, bf16[4,32,1792]{2,1,0:T(8,128)(2,1)S(1)} %all-to-all-done.6.b0, ...), custom_call_target="tpu_custom_call" | custom-call | flops 2863311616 | bytes 8388608 | tf_op jit(solution)/shard_map/pallas_call | solution.py:372
  192.2 3.6 %collective-permute-done.10.b4 = bf16[4,32,1792]{2,1,0:T(8,128)(2,1)S(1)} collective-permute-done((bf16[4,32,1792]{2,1,0:T(8,128)(2,1)S(1)}, bf16[4,32,1792]{2,1,0:T(8,128)(2,1)S(1)}, u32[]{:S(2)}, u32[]{:S(2)}) %collective-permute-start.10) | collective-permute-done | bytes 458784 | tf_op jit(solution)/shard_map/ppermute | solution.py:224
  195.9 3.6 %shard_map.143 = bf16[224,1024]{1,0:T(8,128)(2,1)} custom-call(s32[2]{0:T(128)S(1)} %pad_add_fusion.place_ref, f32[4,256,512]{2,1,0:T(8,128)S(1)} %shard_map.142.p_ref, bf16[256,2432]{1,0:T(8,128)(2,1)S(1)} %bitcast.20, bf16[256,2432]{1,0:T(8,128)(2,1)S(1)} %collective-permute-done.1.a1, bf16[128,2432]{1,0:T(8,128)(2,1)S(1)} %collective-permute-done.7.a20, ...), custom_call_target="tpu_custom_call" | custom-call | flops 1431655808 | bytes 8388608 | tf_op jit(solution)/shard_map/pallas_call | solution.py:383
  (46 shorter events, 0.3 us)
Async XLA Ops:
  6.5 24.5 %copy-start.7 = (f32[512,16]{0,1:T(8,128)S(1)}, f32[512,16]{0,1:T(8,128)}, u32[]{:S(2)}) copy-start(f32[512,16]{0,1:T(8,128)} %param.17) | copy-start | bytes 98308
  6.5 34.1 %copy-start.13 = (f32[128,16]{0,1:T(8,128)S(1)}, f32[128,16]{0,1:T(8,128)}, u32[]{:S(2)}) copy-start(f32[128,16]{0,1:T(8,128)} %param.18) | copy-start | bytes 24580
  6.5 34.1 %copy-start.10 = (bf16[128,512]{1,0:T(8,128)(2,1)S(1)}, bf16[128,512]{1,0:T(8,128)(2,1)}, u32[]{:S(2)}) copy-start(bf16[128,512]{1,0:T(8,128)(2,1)} %x_ref.3) | copy-start | bytes 393220
  6.5 34.1 %copy-start.11 = (bf16[128,512]{1,0:T(8,128)(2,1)S(1)}, bf16[128,512]{1,0:T(8,128)(2,1)}, u32[]{:S(2)}) copy-start(bf16[128,512]{1,0:T(8,128)(2,1)} %d_ref.3) | copy-start | bytes 393220
  6.5 34.1 %copy-start.14 = (f32[128,16]{0,1:T(8,128)S(1)}, f32[128,16]{0,1:T(8,128)}, u32[]{:S(2)}) copy-start(f32[128,16]{0,1:T(8,128)} %param.19) | copy-start | bytes 24580
  6.5 34.1 %copy-start.15 = (f32[512]{0:T(512)S(1)}, f32[512]{0:T(512)}, u32[]{:S(2)}) copy-start(f32[512]{0:T(512)} %param.20) | copy-start | bytes 6148
  6.6 34.1 %copy-start.12 = (bf16[128,512]{1,0:T(8,128)(2,1)S(1)}, bf16[128,512]{1,0:T(8,128)(2,1)}, u32[]{:S(2)}) copy-start(bf16[128,512]{1,0:T(8,128)(2,1)} %z_ref.1) | copy-start | bytes 393220
  6.6 49.2 %all-gather.6.cloned.1.call-start = ((), (), s32[]{:S(2)}) async-start(), calls=%async_computation.8 | async-start | bytes 1179648 | tf_op jit(solution)/shard_map/all_gather | solution.py:276
  10.7 20.4 %all-to-all-start = ((f32[8,16,640]{2,1,0:T(8,128)}), f32[8,16,640]{2,1,0:T(8,128)S(1)}, u32[]{:S(2)}, u32[]{:S(2)}) async-start(f32[8,16,640]{2,1,0:T(8,128)} %shard_map.136), calls=%async_computation | async-start | bytes 655360 | tf_op jit(solution)/shard_map/all_to_all | solution.py:220
  31.8 8.9 %all-to-all-start.1 = ((f32[4,16,640]{2,1,0:T(8,128)}), f32[4,16,640]{2,1,0:T(8,128)S(1)}, u32[]{:S(2)}, u32[]{:S(2)}) async-start(f32[4,16,640]{2,1,0:T(8,128)} %get-tuple-element.17), calls=%async_computation.1 | async-start | bytes 327680 | tf_op jit(solution)/shard_map/all_to_all | solution.py:220
  44.2 11.5 %all-to-all-start.2 = ((bf16[4,128,512]{2,1,0:T(8,128)(2,1)}), bf16[4,128,512]{2,1,0:T(8,128)(2,1)S(1)}, u32[]{:S(2)}, u32[]{:S(2)}) async-start(bf16[4,128,512]{2,1,0:T(8,128)(2,1)} %shard_map.138), calls=%async_computation.2 | async-start | bytes 1048576 | tf_op jit(solution)/shard_map/all_to_all | solution.py:220
  55.7 1.2 copy-start.9
  57.7 19.6 %copy-start.16 = (s32[8,2]{0,1:T(2,128)S(1)}, s32[8,2]{0,1:T(2,128)}, u32[]{:S(2)}) copy-start(s32[8,2]{0,1:T(2,128)} %param.24) | copy-start | bytes 196
  57.7 20.3 %copy-start.17 = (bf16[8,2]{0,1:T(2,128)(2,1)S(1)}, bf16[8,2]{0,1:T(2,128)(2,1)}, u32[]{:S(2)}) copy-start(bf16[8,2]{0,1:T(2,128)(2,1)} %param.25) | copy-start | bytes 100
  57.7 20.7 %copy-start.4 = (bf16[1,224,4096]{2,1,0:T(8,128)(2,1)S(1)}, bf16[1,224,4096]{2,1,0:T(8,128)(2,1)}, u32[]{:S(2)}) copy-start(bf16[1,224,4096]{2,1,0:T(8,128)(2,1)} %param.26) | copy-start | bytes 5505028
  57.7 3.9 %collective-permute-start = (bf16[4,8,8,1024]{3,2,1,0:T(8,128)(2,1)S(1)}, bf16[4,8,8,1024]{3,2,1,0:T(8,128)(2,1)S(1)}, u32[]{:S(2)}, u32[]{:S(2)}) collective-permute-start(bf16[4,8,8,1024]{3,2,1,0:T(8,128)(2,1)S(1)} %get-tuple-element.19), channel_id=1, source_target_pairs={{0,1},{1,0},{2,3},{3,2},{4,5},{5,4},{6,7},{7,6},{8,9},{9,8},{10,11... | collective-permute-start | bytes 1572872 | tf_op jit(solution)/shard_map/ppermute | solution.py:224
  62.6 30.2 %all-to-all-start.3 = ((bf16[32,8,1024]{2,1,0:T(8,128)(2,1)}), bf16[32,8,1024]{2,1,0:T(8,128)(2,1)S(1)}, u32[]{:S(2)}, u32[]{:S(2)}) async-start(bf16[32,8,1024]{2,1,0:T(8,128)(2,1)} %bitcast.8), calls=%async_computation.3 | async-start | bytes 1048576 | tf_op jit(solution)/shard_map/all_to_all | solution.py:336
  77.3 64.0 %all-gather.4.cloned.1.call-start = ((), (), s32[]{:S(2)}) async-start(), calls=%async_computation.7 | async-start | bytes 1400832 | tf_op jit(solution)/shard_map/all_gather | solution.py:236
  78.4 1.5 copy-start.5
  79.9 12.8 %copy-start.6 = (bf16[8,4096]{1,0:T(8,128)(2,1)S(1)}, bf16[8,4096]{1,0:T(8,128)(2,1)}, u32[]{:S(2)}) copy-start(bf16[8,4096]{1,0:T(8,128)(2,1)} %stream_ref.1) | copy-start | bytes 196612
  79.9 12.8 %copy-start.8 = (f32[4096]{0:T(1024)S(1)}, f32[4096]{0:T(1024)}, u32[]{:S(2)}) copy-start(f32[4096]{0:T(1024)} %param.23) | copy-start | bytes 49156
  82.2 2.0 copy-start
  119.9 27.2 %all-to-all-start.6 = ((bf16[4,32,1792]{2,1,0:T(8,128)(2,1)}), bf16[4,32,1792]{2,1,0:T(8,128)(2,1)S(1)}, u32[]{:S(2)}, u32[]{:S(2)}) async-start(bf16[4,32,1792]{2,1,0:T(8,128)(2,1)} %broadcast_in_dim.25), calls=%async_computation.6 | async-start | bytes 917504 | tf_op jit(solution)/shard_map/all_to_all | solution.py:220
  141.3 32.8 %collective-permute-start.1 = (bf16[256,2432]{1,0:T(8,128)(2,1)}, bf16[256,2432]{1,0:T(8,128)(2,1)S(1)}, u32[]{:S(2)}, u32[]{:S(2)}) collective-permute-start(bf16[256,2432]{1,0:T(8,128)(2,1)} %bitcast.17), channel_id=1, source_target_pairs={{0,128},{128,256},{256,384},{384,0},{1,129},{129,257},{257,385},{3... | collective-permute-start | bytes 3735560 | tf_op jit(solution)/shard_map/ppermute | solution.py:224
  143.8 33.8 %collective-permute-start.2 = (bf16[256,2432]{1,0:T(8,128)(2,1)}, bf16[256,2432]{1,0:T(8,128)(2,1)S(1)}, u32[]{:S(2)}, u32[]{:S(2)}) collective-permute-start(bf16[256,2432]{1,0:T(8,128)(2,1)} %bitcast.18), channel_id=1, source_target_pairs={{0,384},{128,0},{256,128},{384,256},{1,385},{129,1},{257,129},{385... | collective-permute-start | bytes 3735560 | tf_op jit(solution)/shard_map/ppermute | solution.py:224
  147.1 39.1 %copy-start.3 = (bf16[8,32,2432]{2,1,0:T(8,128)(2,1)S(1)}, bf16[8,32,2432]{2,1,0:T(8,128)(2,1)}, u32[]{:S(2)}) copy-start(bf16[8,32,2432]{2,1,0:T(8,128)(2,1)} %all-gather.4.cloned.1.call-done) | copy-start | bytes 3735556
  147.1 11.7 %collective-permute-start.3 = (bf16[4,32,1792]{2,1,0:T(8,128)(2,1)S(1)}, bf16[4,32,1792]{2,1,0:T(8,128)(2,1)S(1)}, u32[]{:S(2)}, u32[]{:S(2)}) collective-permute-start(bf16[4,32,1792]{2,1,0:T(8,128)(2,1)S(1)} %all-to-all-done.6.b0), channel_id=1, source_target_pairs={{0,16},{16,32},{32,48},{48,64},{64,80},{80,96},{96,112},{112,0},{1... | collective-permute-start | bytes 1376264 | tf_op jit(solution)/shard_map/ppermute | solution.py:224
  150.6 11.7 %collective-permute-start.5 = (bf16[4,32,1792]{2,1,0:T(8,128)(2,1)S(1)}, bf16[4,32,1792]{2,1,0:T(8,128)(2,1)S(1)}, u32[]{:S(2)}, u32[]{:S(2)}) collective-permute-start(bf16[4,32,1792]{2,1,0:T(8,128)(2,1)S(1)} %all-to-all-done.6.b0), channel_id=1, source_target_pairs={{0,112},{16,0},{32,16},{48,32},{64,48},{80,64},{96,80},{112,96},{1... | collective-permute-start | bytes 1376264 | tf_op jit(solution)/shard_map/ppermute | solution.py:224
  158.8 12.4 %collective-permute-start.4 = (bf16[4,32,1792]{2,1,0:T(8,128)(2,1)S(1)}, bf16[4,32,1792]{2,1,0:T(8,128)(2,1)S(1)}, u32[]{:S(2)}, u32[]{:S(2)}) collective-permute-start(bf16[4,32,1792]{2,1,0:T(8,128)(2,1)S(1)} %collective-permute-done.3.b1), channel_id=1, source_target_pairs={{0,16},{16,32},{32,48},{48,64},{64,80},{80,96},{96,112},{112,0},{1... | collective-permute-start | bytes 1376264 | tf_op jit(solution)/shard_map/ppermute | solution.py:224
  162.2 17.8 %collective-permute-start.6 = (bf16[4,32,1792]{2,1,0:T(8,128)(2,1)S(1)}, bf16[4,32,1792]{2,1,0:T(8,128)(2,1)S(1)}, u32[]{:S(2)}, u32[]{:S(2)}) collective-permute-start(bf16[4,32,1792]{2,1,0:T(8,128)(2,1)S(1)} %collective-permute-done.5.b7), channel_id=1, source_target_pairs={{0,112},{16,0},{32,16},{48,32},{64,48},{80,64},{96,80},{112,96},{1... | collective-permute-start | bytes 1376264 | tf_op jit(solution)/shard_map/ppermute | solution.py:224
  171.2 13.1 %collective-permute-start.9 = (bf16[4,32,1792]{2,1,0:T(8,128)(2,1)S(1)}, bf16[4,32,1792]{2,1,0:T(8,128)(2,1)S(1)}, u32[]{:S(2)}, u32[]{:S(2)}) collective-permute-start(bf16[4,32,1792]{2,1,0:T(8,128)(2,1)S(1)} %collective-permute-done.4.b2), channel_id=1, source_target_pairs={{0,16},{16,32},{32,48},{48,64},{64,80},{80,96},{96,112},{112,0},{1... | collective-permute-start | bytes 1376264 | tf_op jit(solution)/shard_map/ppermute | solution.py:224
  174.1 21.8 %collective-permute-start.7 = (bf16[128,2432]{1,0:T(8,128)(2,1)S(1)}, bf16[128,2432]{1,0:T(8,128)(2,1)S(1)}, u32[]{:S(2)}, u32[]{:S(2)}) collective-permute-start(bf16[128,2432]{1,0:T(8,128)(2,1)S(1)} %slice.8), channel_id=1, source_target_pairs={{0,128},{128,256},{256,384},{384,0},{1,129},{129,257},{257,385},{3... | collective-permute-start | bytes 1867784 | tf_op jit(solution)/shard_map/ppermute | solution.py:224
  177.7 18.2 %collective-permute-start.8 = (bf16[128,2432]{1,0:T(8,128)(2,1)S(1)}, bf16[128,2432]{1,0:T(8,128)(2,1)S(1)}, u32[]{:S(2)}, u32[]{:S(2)}) collective-permute-start(bf16[128,2432]{1,0:T(8,128)(2,1)S(1)} %slice.9), channel_id=1, source_target_pairs={{0,384},{128,0},{256,128},{384,256},{1,385},{129,1},{257,129},{385... | collective-permute-start | bytes 1867784 | tf_op jit(solution)/shard_map/ppermute | solution.py:224
  180.0 12.2 %collective-permute-start.11 = (bf16[4,32,1792]{2,1,0:T(8,128)(2,1)S(1)}, bf16[4,32,1792]{2,1,0:T(8,128)(2,1)S(1)}, u32[]{:S(2)}, u32[]{:S(2)}) collective-permute-start(bf16[4,32,1792]{2,1,0:T(8,128)(2,1)S(1)} %collective-permute-done.6.b6), channel_id=1, source_target_pairs={{0,112},{16,0},{32,16},{48,32},{64,48},{80,64},{96,80},{112,96},{1... | collective-permute-start | bytes 1376264 | tf_op jit(solution)/shard_map/ppermute | solution.py:224
  184.3 11.6 %collective-permute-start.10 = (bf16[4,32,1792]{2,1,0:T(8,128)(2,1)S(1)}, bf16[4,32,1792]{2,1,0:T(8,128)(2,1)S(1)}, u32[]{:S(2)}, u32[]{:S(2)}) collective-permute-start(bf16[4,32,1792]{2,1,0:T(8,128)(2,1)S(1)} %collective-permute-done.9.b3), channel_id=1, source_target_pairs={{0,16},{16,32},{32,48},{48,64},{64,80},{80,96},{96,112},{112,0},{1... | collective-permute-start | bytes 1376264 | tf_op jit(solution)/shard_map/ppermute | solution.py:224
  186.3 2.2 %copy-start.1 = (bf16[4096,512]{1,0:T(8,128)(2,1)S(1)}, bf16[4096,512]{1,0:T(8,128)(2,1)}, u32[]{:S(2)}) copy-start(bf16[4096,512]{1,0:T(8,128)(2,1)} %copy-done) | copy-start | bytes 12582916
  188.5 7.4 %copy-start.2 = (bf16[4096,512]{1,0:T(8,128)(2,1)S(1)}, bf16[4096,512]{1,0:T(8,128)(2,1)}, u32[]{:S(2)}) copy-start(bf16[4096,512]{1,0:T(8,128)(2,1)} %copy-done) | copy-start | bytes 12582916
Sparse Core Ops, SparseCore 0:
  9.5 45.4 all-gather.5
  107.6 33.5 all-gather.3
